TPU v7x, 512 devices: a whole 4x4x16 slice. The times are simulated.
512 devices in a mesh: ctx: 16 (over z_lo, core), tp: 32 (over z_hi, x, y).
Axes of the slice: x: 4, y: 4, z: 16 (z_hi: 2, z_lo: 8; z = z_hi * 8 + z_lo), core: 2. Of those that a mesh axis runs over, the one named last changes fastest.
Arguments:
- residual: bfloat16 [4096, 8192], P('ctx', 'tp'), may hold values from -8 to 8
- queries: bfloat16 [4096, 8192], P('ctx', 'tp'), may hold values from -15 to 15
- keys_values: bfloat16 [4096, 2048], P('ctx'), may hold values from -6 to 6
- out_weight: bfloat16 [8192, 8192], P('tp', 'ctx'), may hold values from -0.125 to 0.125
- norm_gain: float32 [8192], replicated, may hold values from 0.1 to 1.9
- cache_weight: bfloat16 [8192, 2048], P(None, 'tp'), may hold values from -0.0625 to 0.0625
- positions: int32 [4096], P('ctx'), may hold values from 0 to 8191, as said below
- keep_rows: int32 [4096], P('ctx'), may hold values from 0 to 255, as said below
- kept_count: int32 [16], P('ctx'), may hold values from 64 to 256, as said below
Outputs:
- kept_hidden: bfloat16 [4096, 8192], P('ctx', 'tp')
- kept_cache: bfloat16 [4096, 2048], P('ctx', 'tp')
Inputs may be any that keep to these rules, and one draw needn't show every extreme that they name: `keep_rows`: within every shard of ctx the 256 entries are a permutation of the shard's local rows: first its kept rows in ascending order, as many as its kept_count, then its dropped rows in ascending order. `kept_count`: for every even shard index e, shards e and e + 1 keep 2 * 160 rows together. `positions`: strictly increasing along the tokens.
All inputs are finite; a program needn't handle non-finite values.
Results may differ from a plain program's by a relative error of at most 0.019.
Values may be sent and summed in bfloat16 or wider, within the bound.
No kernel may reach another device: no remote copies, remote signals or barrier semaphores. Data moves between devices by JAX's collectives and lax.ppermute only.
A program may use at most 64 MiB of HBM per device.

v0:
```python
import math

import jax
import jax.numpy as jnp
from jax import lax
from jax.sharding import PartitionSpec as P

D = 8192
HQ = 64
KVH = 8
HD = 128


THETA = 1000000.0
EPS = 1e-06


def rotate_pairs(cache_rows, position_ids, first_col, head_dim):
    pair_count = cache_rows.shape[1] // 2
    columns = first_col + 2 * jnp.arange(pair_count, dtype=jnp.int32)
    within = columns % (2 * head_dim)
    is_key = within < head_dim
    exponent = jnp.where(is_key, within, 0).astype(jnp.float32) / head_dim
    frequency = jnp.power(jnp.float32(THETA), -exponent)
    angles = position_ids.astype(jnp.float32)[:, None] * frequency[None, :]
    paired = cache_rows.reshape(cache_rows.shape[0], pair_count, 2)
    first_half = paired[..., 0]
    second = paired[..., 1]
    cosine = jnp.cos(angles)
    sine_rows = jnp.sin(angles)
    turned_first = first_half * cosine - second * sine_rows
    turned_second = second * cosine + first_half * sine_rows
    turned = jnp.stack(
        [jnp.where(is_key, turned_first, first_half), jnp.where(is_key, turned_second, second)], -1
    )
    return turned.reshape(cache_rows.shape)


def shards(
    residual,
    queries,
    keys_values,
    out_weight,
    norm_gain,
    cache_weight,
    positions,
    keep_rows,
    kept_count,
):
    row_count = residual.shape[0]
    ctx_index = lax.axis_index("ctx")
    tp_index = lax.axis_index("tp")
    head_count = queries.shape[1] // HD
    kv_head = tp_index * head_count // (HQ // KVH)
    head_block = lax.dynamic_slice_in_dim(keys_values, kv_head * 2 * HD, 2 * HD, 1)
    key_rows = head_block[:, :HD]
    value_rows = head_block[:, HD:]
    query_rows = queries.reshape(row_count, head_count, HD)
    own_index = ctx_index * row_count + jnp.arange(row_count, dtype=jnp.int32)
    score_scale = 1.0 / math.sqrt(HD)
    running_max = jnp.full((row_count, head_count), -1e30, jnp.float32)
    key_block = lax.all_gather(key_rows, "ctx", axis=0, tiled=True)
    value_block = lax.all_gather(value_rows, "ctx", axis=0, tiled=True)
    block_rows = key_block.shape[0]
    scores = (
        jnp.einsum("rgd,kd->rgk", query_rows, key_block, preferred_element_type=jnp.float32)
        * score_scale
    )
    visible = jnp.arange(block_rows, dtype=jnp.int32)[None, :] <= own_index[:, None]
    visible = visible[:, None, :]
    scores = jnp.where(visible, scores, -1e30)
    new_max = jnp.maximum(running_max, jnp.max(scores, axis=-1))
    weights = jnp.where(visible, jnp.exp(scores - new_max[..., None]), 0.0)
    new_sum = jnp.sum(weights, axis=-1)
    update = jnp.einsum(
        "rgk,kd->rgd", weights.astype(jnp.bfloat16), value_block, preferred_element_type=jnp.float32
    )
    attended = (
        (update / new_sum[..., None]).reshape(row_count, head_count * HD).astype(jnp.bfloat16)
    )
    own_count = kept_count[0]
    valid_rows = jnp.arange(row_count, dtype=jnp.int32) < own_count
    partials = jnp.dot(
        attended,
        lax.all_gather(out_weight, "ctx", axis=1, tiled=True),
        preferred_element_type=jnp.float32,
    )
    group_sums = lax.psum_scatter(
        partials.astype(jnp.bfloat16), "tp", scatter_dimension=1, tiled=True
    ).astype(jnp.float32)
    hidden = (residual.astype(jnp.float32) + group_sums).astype(jnp.bfloat16)
    feat_width = hidden.shape[1]
    wide_hidden = hidden.astype(jnp.float32)
    square_total = lax.psum(jnp.sum(wide_hidden * wide_hidden, axis=-1), "tp")
    inverse = lax.rsqrt(square_total / D + EPS)
    gain_part = lax.dynamic_slice_in_dim(norm_gain, tp_index * feat_width, feat_width)
    normed = (wide_hidden * inverse[:, None] * gain_part[None, :]).astype(jnp.bfloat16)
    gathered = lax.all_gather(normed, "tp", axis=1, tiled=True)
    cache_rows = jnp.dot(gathered, cache_weight, preferred_element_type=jnp.float32)
    cache_rot = rotate_pairs(cache_rows, positions, tp_index * cache_rows.shape[1], HD).astype(
        jnp.bfloat16
    )
    kept_flags = jnp.zeros((row_count,), jnp.int32).at[keep_rows].set(valid_rows.astype(jnp.int32))
    kept_mask = kept_flags[:, None] > 0
    kept_hidden = jnp.where(kept_mask, hidden, jnp.zeros_like(hidden))
    kept_cache = jnp.where(kept_mask, cache_rot, jnp.zeros_like(cache_rot))
    return (kept_hidden, kept_cache)


def solution(mesh):
    in_specs = (
        P("ctx", "tp"),
        P("ctx", "tp"),
        P("ctx", None),
        P("tp", "ctx"),
        P(),
        P(None, "tp"),
        P("ctx"),
        P("ctx"),
        P("ctx"),
    )
    out_specs = (P("ctx", "tp"), P("ctx", "tp"))
    return jax.shard_map(shards, mesh=mesh, in_specs=in_specs, out_specs=out_specs, check_vma=False)
```

profile of v0, /device:TPU:1, one launch (start us, length us, event | category | flops | bytes accessed | tf_op | source)
XLA Modules:
  0.0 1150.2 jit_solution(1571548678201377905)
XLA Ops:
  7.2 0.0 copy-start
  7.2 0.0 all-gather.5.cloned.1.call-start
  7.2 1.6 constant_dynamic-slice_fusion.1
  8.9 0.0 all-gather.5.cloned.1.call-update
  8.9 0.0 all-gather.7.cloned.1.call-start
  8.9 0.7 all-gather.7.cloned.1.call-update
  9.6 0.0 all-gather.9.cloned.1.call-start
  9.7 0.7 all-gather.9.cloned.1.call-update
  10.4 0.0 reduce-scatter.2.cloned.1.call-start
  10.4 0.7 iota_compare_fusion
  11.1 102.8 %all-gather.5.cloned.1.call-done = bf16[4096,128]{1,0:T(8,128)(2,1)} async-done(((bf16[256,128]{1,0:T(8,128)(2,1)}), bf16[4096,128]{1,0:T(8,128)(2,1)}) %all-gather.5.cloned.1.call-update) | async-done | bytes 1048592 | tf_op jit(solution)/shard_map/all_gather | solution.py:62
  114.0 2.5 fusion
  116.5 0.0 copy-start.1
  116.5 3.2 copy-done.1
  119.7 2.2 fusion.1
  121.9 93.9 %all-gather.7.cloned.1.call-done = bf16[4096,128]{1,0:T(8,128)(2,1)} async-done(((bf16[256,128]{1,0:T(8,128)(2,1)}), bf16[4096,128]{1,0:T(8,128)(2,1)}) %all-gather.7.cloned.1.call-update) | async-done | bytes 1048592 | tf_op jit(solution)/shard_map/all_gather | solution.py:63
  215.9 5.7 fusion.9
  221.6 0.0 copy-start.2
  221.6 0.0 copy-start.3
  221.6 0.0 copy-start.4
  221.6 102.4 %all-gather.9.cloned.1.call-done = bf16[256,8192]{1,0:T(8,128)(2,1)} async-done(((bf16[256,512]{1,0:T(8,128)(2,1)}), bf16[256,8192]{1,0:T(8,128)(2,1)}) %all-gather.9.cloned.1.call-update) | async-done | bytes 4194320 | tf_op jit(solution)/shard_map/all_gather | solution.py:85
  324.0 5.4 convolution_convert_fusion
  329.4 0.0 reduce-scatter.2.cloned.1.call-update
  329.4 0.0 all-gather.11.cloned.1.call-start
  329.5 0.8 dynamic_slice.7
  330.3 450.2 %reduce-scatter.2.cloned.1.call-done = bf16[256,256]{1,0:T(8,128)(2,1)} async-done(((bf16[256,8192]{1,0:T(8,128)(2,1)}), bf16[256,256]{1,0:T(8,128)(2,1)}) %reduce-scatter.2.cloned.1.call-update) | async-done | bytes 131088 | tf_op jit(solution)/shard_map/reduce_scatter | solution.py:88
  780.4 0.0 copy-done.2
  780.4 1.0 fusion.15
  781.4 132.6 %psum.7 = f32[256]{0:T(256)S(1)} all-reduce(f32[256]{0:T(256)S(1)} %fusion.15), channel_id=1, replica_groups=mesh['ctx'=16,'tp'=32] {'tp'}, use_global_device_ids=true, to_apply=%region_5.6 | all-reduce | flops 256 | bytes 2048 | tf_op jit(solution)/shard_map/psum | solution.py:94
  914.1 1.7 fusion.17
  915.7 0.0 all-gather.11.cloned.1.call-update
  915.8 0.0 copy-done.3
  916.4 0.0 copy-done.4
  916.5 1.4 scatter_custom_fusion
  917.9 1.7 broadcast_select_fusion
  919.6 218.5 %all-gather.11.cloned.1.call-done = bf16[256,8192]{1,0:T(8,128)(2,1)} async-done(((bf16[256,256]{1,0:T(8,128)(2,1)}), bf16[256,8192]{1,0:T(8,128)(2,1)}) %all-gather.11.cloned.1.call-update) | async-done | bytes 4194320 | tf_op jit(solution)/shard_map/all_gather | solution.py:98
  1138.1 0.0 copy-done
  1138.1 3.6 fusion.28
  1141.7 1.2 fusion.20
  1143.0 0.1 pad_maximum_fusion
  1143.1 0.6 broadcast_select_fusion.3
  (11 shorter events, 0.1 us)
Async XLA Ops:
  7.2 1130.9 %copy-start = (bf16[8192,64]{0,1:T(8,128)(2,1)S(1)}, bf16[8192,64]{0,1:T(8,128)(2,1)}, u32[]{:S(2)}) copy-start(bf16[8192,64]{0,1:T(8,128)(2,1)} %param.14) | copy-start | bytes 3145732
  7.2 106.8 %all-gather.5.cloned.1.call-start = ((), (), s32[]{:S(2)}) async-start(), calls=%async_computation.1 | async-start | bytes 1114112 | tf_op jit(solution)/shard_map/all_gather | solution.py:62
  8.9 207.0 %all-gather.7.cloned.1.call-start = ((), (), s32[]{:S(2)}) async-start(), calls=%async_computation.2 | async-start | bytes 1114112 | tf_op jit(solution)/shard_map/all_gather | solution.py:63
  9.6 314.4 %all-gather.9.cloned.1.call-start = ((), (), s32[]{:S(2)}) async-start(), calls=%async_computation.3 | async-start | bytes 4456448 | tf_op jit(solution)/shard_map/all_gather | solution.py:85
  10.4 770.0 %reduce-scatter.2.cloned.1.call-start = ((), (), s32[]{:S(2)}) async-start(), calls=%async_computation.4 | async-start | bytes 4325376 | tf_op jit(solution)/shard_map/reduce_scatter | solution.py:88
  116.5 3.2 copy-start.1
  221.6 558.8 %copy-start.2 = (bf16[256,256]{1,0:T(8,128)(2,1)S(1)}, bf16[256,256]{1,0:T(8,128)(2,1)}, u32[]{:S(2)}) copy-start(bf16[256,256]{1,0:T(8,128)(2,1)} %param.9) | copy-start | bytes 393220
  221.6 694.2 %copy-start.3 = (s32[256]{0:T(256)S(1)}, s32[256]{0:T(256)}, u32[]{:S(2)}) copy-start(s32[256]{0:T(256)} %param.15) | copy-start | bytes 3076
  221.6 694.8 %copy-start.4 = (s32[256]{0:T(256)S(1)}, s32[256]{0:T(256)}, u32[]{:S(2)}) copy-start(s32[256]{0:T(256)} %param.16) | copy-start | bytes 3076
  329.4 808.7 %all-gather.11.cloned.1.call-start = ((), (), s32[]{:S(2)}) async-start(), calls=%async_computation.5 | async-start | bytes 4325376 | tf_op jit(solution)/shard_map/all_gather | solution.py:98
Sparse Core Ops, SparseCore 0:
  10.1 103.8 all-gather.4
  116.6 99.2 all-gather.6
  218.0 105.9 all-gather.8
  329.6 450.8 reduce-scatter.1
  915.9 222.1 all-gather.10
where the time goes:
time: 1150 us
  waiting for transfers between devices  969 us (84%)
  blocking collectives  133 us (12%)
  matrix products  17.2 us (1%)
  between operations  14.6 us (1%)
    reduce_scatter x1, waiting for transfers between devices, shards(): lax.psum_scatter(partials.astype(jnp.bfloat16), 'tp', scatter_dimension=1...  450 us
    all_gather x1, waiting for transfers between devices, shards(): gathered = lax.all_gather(normed, 'tp', axis=1, tiled=True)  219 us
    psum x1, blocking collectives, shards(): square_total = lax.psum(jnp.sum(wide_hidden * wide_hidden, axis=-1), 'tp')  133 us
    all_gather x1, waiting for transfers between devices, shards(): key_block = lax.all_gather(key_rows, 'ctx', axis=0, tiled=True)  103 us
    all_gather x1, waiting for transfers between devices, shards(): lax.all_gather(out_weight, 'ctx', axis=1, tiled=True)  102 us
    all_gather x1, waiting for transfers between devices, shards(): value_block = lax.all_gather(value_rows, 'ctx', axis=0, tiled=True)  93.9 us
  transfers between devices with their start and end apart: 5, of which 5 were waited for; matrix products, arithmetic and copies ran while one was open for 1% of the time, Pallas kernels for 0%

commit v1 on v0

v1 whole, which is shorter than its diff:
```python
import math

import jax
import jax.numpy as jnp
from jax import lax
from jax.sharding import PartitionSpec as P

D = 8192
HQ = 64
KVH = 8
HD = 128
THETA = 1000000.0
EPS = 1e-06

ZL, CORES, ZH, NX, NY = 8, 2, 2, 4, 4
PAIR_KEEP = 320
OWN = PAIR_KEEP // 2
AXES = ("ctx", "tp")
BF = jnp.bfloat16
F32 = jnp.float32


def pairs(move):
    found = []
    for zl in range(ZL):
        for core in range(CORES):
            for zh in range(ZH):
                target = move(zh, zl, core)
                if target is None:
                    continue
                for plane in range(NX * NY):
                    source = (zl * CORES + core) * (ZH * NX * NY) + zh * NX * NY + plane
                    to = (target[1] * CORES + target[2]) * (ZH * NX * NY) + target[0] * NX * NY + plane
                    found.append((source, to))
    return found


CORE = pairs(lambda zh, zl, core: (zh, zl, 1 - core))
FOUR = pairs(lambda zh, zl, core: (zh, zl ^ 4, core))
EIGHT = pairs(lambda zh, zl, core: (1 - zh, zl, core))
TWELVE = pairs(lambda zh, zl, core: (1 - zh, zl ^ 4, core))
QUAD = [None] + [pairs(lambda zh, zl, core, k=k: (zh, zl ^ k, core)) for k in (1, 2, 3)]
BACK = [None] + [
    pairs(lambda zh, zl, core, k=k: (zh if k <= 4 else 1 - zh, zl + k, core) if zl + k < ZL else None)
    for k in range(1, ZL)
]
PLANES = [[half * NX * NY + i for i in range(NX * NY)] for half in range(ZH)]


def send(x, table):
    return lax.ppermute(x, AXES, table)


def plane_exchange(x):
    return lax.all_to_all(x, "tp", 0, 0, tiled=True, axis_index_groups=PLANES)


def turn(cache_rows, position_ids, first_col):
    column = first_col + jnp.arange(cache_rows.shape[1], dtype=jnp.int32)
    within = column % (2 * HD)
    is_key = within < HD
    exponent = jnp.where(is_key, within - within % 2, 0).astype(F32) / HD
    frequency = jnp.power(F32(THETA), -exponent)
    angles = position_ids[:, None] * frequency[None, :]
    even = (column % 2 == 0)[None, :]
    other = jnp.where(even, -jnp.roll(cache_rows, -1, axis=1), jnp.roll(cache_rows, 1, axis=1))
    turned = cache_rows * jnp.cos(angles) + other * jnp.sin(angles)
    return jnp.where(is_key[None, :], turned, cache_rows)


def shards(
    residual, queries, keys_values, out_weight, norm_gain, cache_weight, positions, keep_rows, kept_count
):
    rows = residual.shape[0]
    ctx = lax.axis_index("ctx")
    tp = lax.axis_index("tp")
    zl, core = ctx // CORES, ctx % CORES
    zh, plane = tp // (NX * NY), tp % (NX * NY)
    first = core == 0

    local = jnp.arange(rows, dtype=jnp.int32)
    order = jnp.where(local < kept_count[0], local, -1)
    hits = keep_rows[:, None] == local[None, :]
    rank = jnp.sum(jnp.where(hits, order[:, None], 0), axis=0)
    meta = jnp.stack([rank, positions // 128, positions % 128], axis=1).astype(BF)
    meta = jnp.pad(meta, ((0, 0), (0, 125)))
    mine = jnp.concatenate([queries, residual, meta], axis=1)
    theirs = send(mine, CORE)

    head = zh * (KVH // ZH) + plane // NY
    far_head = (1 - zh) * (KVH // ZH) + plane // NY
    own_kv = lax.dynamic_slice_in_dim(keys_values, head * 2 * HD, 2 * HD, 1)
    far_kv = lax.dynamic_slice_in_dim(keys_values, far_head * 2 * HD, 2 * HD, 1)
    blocks = [own_kv] + [send(own_kv if k <= 4 else far_kv, BACK[k]) for k in range(1, ZL)]

    weight = jnp.stack([out_weight[:, :256], out_weight[:, 256:]])
    quad = jnp.stack([weight] + [send(weight, QUAD[k]) for k in (1, 2, 3)])
    quad_other = send(quad, CORE)

    columns = cache_weight.shape[1]
    gained = (cache_weight.astype(F32) * norm_gain[:, None]).astype(BF)
    gained = gained.T.reshape(columns, ZH, NX * NY, D // (ZH * NX * NY)).transpose(2, 0, 1, 3)
    gained = plane_exchange(gained.reshape(NX * NY, columns, -1))

    pair = jnp.where(first, jnp.concatenate([mine, theirs]), jnp.concatenate([theirs, mine]))
    pair_rank = pair[:, 512].astype(jnp.int32)
    count0 = jnp.sum((pair_rank[:rows] >= 0).astype(jnp.int32))
    pair_row = jnp.arange(2 * rows, dtype=jnp.int32)
    pair_rank = jnp.where(pair_rank >= 0, pair_rank + jnp.where(pair_row >= rows, count0, 0), -1)
    wanted = core * OWN + jnp.arange(OWN, dtype=jnp.int32)
    chosen = wanted[:, None] == pair_rank[None, :]
    picked = jnp.dot(chosen.astype(BF), pair, preferred_element_type=F32)
    token = zl * 2 * rows + jnp.sum(jnp.where(chosen, pair_row[None, :], 0), axis=1)
    position = picked[:, 513] * 128.0 + picked[:, 514]
    query = picked[:, :256].astype(BF).reshape(OWN, 2, HD).transpose(1, 0, 2).reshape(2 * OWN, HD)
    own_residual = picked[:, 256:512].astype(BF)
    far_residual = send(own_residual, EIGHT)

    kv_mine = jnp.concatenate(blocks)
    kv_theirs = send(kv_mine, CORE)
    key_row = jnp.arange(ZL * rows, dtype=jnp.int32)
    key_token = (zl - key_row // rows) * 2 * rows + key_row % rows
    query_token = jnp.concatenate([token, token])

    def scored(kv, offset):
        scores = lax.dot_general(query, kv[:, :HD], (((1,), (1,)), ((), ())), preferred_element_type=F32)
        at = key_token + offset
        visible = (at[None, :] <= query_token[:, None]) & (at >= 0)[None, :]
        return jnp.where(visible, scores * (1.0 / math.sqrt(HD)), -1e30)

    score_a = scored(kv_mine, core * rows)
    score_b = scored(kv_theirs, (1 - core) * rows)
    top = jnp.maximum(jnp.max(score_a, axis=1), jnp.max(score_b, axis=1))[:, None]
    prob_a, prob_b = jnp.exp(score_a - top), jnp.exp(score_b - top)
    total = jnp.sum(prob_a, axis=1) + jnp.sum(prob_b, axis=1)
    mixed = jnp.dot(prob_a.astype(BF), kv_mine[:, HD:], preferred_element_type=F32) + jnp.dot(
        prob_b.astype(BF), kv_theirs[:, HD:], preferred_element_type=F32
    )
    attended = (mixed / total[:, None]).astype(BF)
    attended = jnp.concatenate([attended[:OWN], attended[OWN:]], axis=1)

    both = jnp.concatenate([attended, send(attended, FOUR)])
    low = jnp.where(first, quad, quad_other)
    high = jnp.where(first, quad_other, quad)
    blocks_w = jnp.concatenate([low, high], axis=1)
    arranged = jnp.stack(
        [lax.dynamic_index_in_dim(blocks_w, (zl % 4) ^ k, 0, keepdims=False) for k in range(4)]
    ).reshape(NX * NY, 256, 256)
    terms = jnp.einsum("rk,ekn->ern", both, arranged, preferred_element_type=F32).astype(BF)
    summed = jnp.sum(plane_exchange(terms).reshape(NX * NY, 2 * OWN, 256).astype(F32), axis=0).astype(BF)
    near, far = summed[:OWN], summed[OWN:]
    from4, from8, from12 = send(far, FOUR), send(near, EIGHT), send(far, TWELVE)
    same = near.astype(F32) + from8.astype(F32)
    cross = from4.astype(F32) + from12.astype(F32)
    low_half = zl < 4
    first_half = jnp.where(low_half, same, cross)
    second_half = jnp.where(low_half, cross, same)
    hidden0 = (jnp.where(zh == 0, own_residual, far_residual).astype(F32) + first_half).astype(BF)
    hidden1 = (jnp.where(zh == 0, far_residual, own_residual).astype(F32) + second_half).astype(BF)
    hidden = jnp.concatenate([hidden0, hidden1], axis=1)

    wide = hidden.astype(F32)
    square = jnp.sum(wide * wide, axis=1, keepdims=True)
    square_high = square.astype(BF)
    square_low = (square - square_high.astype(F32)).astype(BF)
    parts = jnp.einsum(
        "rf,ecf->erc", hidden, gained.reshape(NX * NY, columns, -1), preferred_element_type=F32
    ).astype(BF)
    tail = jnp.pad(jnp.concatenate([square_high, square_low], axis=1), ((0, 0), (0, 128 - columns - 2)))
    message = jnp.concatenate([parts, jnp.broadcast_to(tail[None], (NX * NY,) + tail.shape)], axis=2)
    gathered = jnp.sum(plane_exchange(message).astype(F32), axis=0)
    square_total = gathered[:, columns] + gathered[:, columns + 1]
    cache_rows = gathered[:, :columns] * lax.rsqrt(square_total / D + EPS)[:, None]
    cache_rot = turn(cache_rows, position, tp * columns).astype(BF)

    own_hidden = jnp.where(zh == 0, hidden0, hidden1)
    done = jnp.concatenate([own_hidden, jnp.pad(cache_rot, ((0, 0), (0, 128 - columns)))], axis=1)
    done_other = send(done, CORE)
    kept = jnp.where(first, jnp.concatenate([done, done_other]), jnp.concatenate([done_other, done]))
    own_rank = jnp.where(rank >= 0, rank + jnp.where(first, 0, count0), -1)
    place = own_rank[:, None] == jnp.arange(PAIR_KEEP, dtype=jnp.int32)[None, :]
    output = jnp.dot(place.astype(BF), kept, preferred_element_type=F32).astype(BF)
    return output[:, :256], output[:, 256 : 256 + columns]


def solution(mesh):
    in_specs = (
        P("ctx", "tp"),
        P("ctx", "tp"),
        P("ctx", None),
        P("tp", "ctx"),
        P(),
        P(None, "tp"),
        P("ctx"),
        P("ctx"),
        P("ctx"),
    )
    out_specs = (P("ctx", "tp"), P("ctx", "tp"))
    return jax.shard_map(shards, mesh=mesh, in_specs=in_specs, out_specs=out_specs, check_vma=False)
```

time: 1150 us -> 200 us (0.17)
  the two profiles are of different devices: /device:TPU:1 before, /device:TPU:65 now
where the time goes in v1:
time: 200 us; the launch traced here: 199 us
  starting transfers between devices  102 us (51%)
  waiting for transfers between devices  66.6 us (33%)
  local copies, waits for them, and re-layouts  10.2 us (5%)
  other arithmetic  9.36 us (5%)
  matrix products  7.61 us (4%)
  between operations  2.78 us (1%)
    ppermute x19, starting transfers between devices, send(): return lax.ppermute(x, AXES, table)  81.6 us
    all_to_all x3, waiting for transfers between devices, plane_exchange(): return lax.all_to_all(x, 'tp', 0, 0, tiled=True, axis_index_groups=PLANES)  37.4 us
    ppermute x19, waiting for transfers between devices, send(): return lax.ppermute(x, AXES, table)  29.2 us
    all_to_all x3, starting transfers between devices, plane_exchange(): return lax.all_to_all(x, 'tp', 0, 0, tiled=True, axis_index_groups=PLANES)  20.5 us
  transfers between devices with their start and end apart: 22, of which 9 were waited for; matrix products, arithmetic and copies ran while one was open for 9% of the time, Pallas kernels for 0%

profile of v1, /device:TPU:65, one launch (start us, length us, event | category | flops | bytes accessed | tf_op | source)
XLA Modules:
  0.0 198.7 jit_solution(14507870224632477639)
XLA Ops:
  0.7 1.0 constant_dynamic-update-slice_fusion.7
  1.8 3.5 %collective-permute-start.6 = (bf16[256,256]{1,0:T(8,128)(2,1)S(1)}, bf16[256,256]{1,0:T(8,128)(2,1)S(1)}, u32[]{:S(2)}, u32[]{:S(2)}) collective-permute-start(bf16[256,256]{1,0:T(8,128)(2,1)S(1)} %get-tuple-element.16), channel_id=1, source_target_pairs={{0,64},{1,65},{2,66},{3,67},{4,68},{5,69},{6,70},{7,71},{8,72},{9,... | collective-permute-start | bytes 393224 | tf_op jit(solution)/shard_map/ppermute | solution.py:51
  5.3 6.1 %collective-permute-start.7 = (bf16[256,256]{1,0:T(8,128)(2,1)S(1)}, bf16[256,256]{1,0:T(8,128)(2,1)S(1)}, u32[]{:S(2)}, u32[]{:S(2)}) collective-permute-start(bf16[256,256]{1,0:T(8,128)(2,1)S(1)} %get-tuple-element.16), channel_id=1, source_target_pairs={{0,128},{1,129},{2,130},{3,131},{4,132},{5,133},{6,134},{7,135},{8... | collective-permute-start | bytes 393224 | tf_op jit(solution)/shard_map/ppermute | solution.py:51
  11.4 4.0 %collective-permute-start.8 = (bf16[256,256]{1,0:T(8,128)(2,1)S(1)}, bf16[256,256]{1,0:T(8,128)(2,1)S(1)}, u32[]{:S(2)}, u32[]{:S(2)}) collective-permute-start(bf16[256,256]{1,0:T(8,128)(2,1)S(1)} %get-tuple-element.16), channel_id=1, source_target_pairs={{0,192},{1,193},{2,194},{3,195},{4,196},{5,197},{6,198},{7,199},{8... | collective-permute-start | bytes 393224 | tf_op jit(solution)/shard_map/ppermute | solution.py:51
  15.4 1.3 collective-permute-start.9
  16.7 1.3 collective-permute-start.10
  18.8 0.8 select_reduce_fusion
  19.6 0.7 fusion.73
  20.5 1.0 slice_bitcast_fusion.1
  21.7 0.7 collective-permute-start.11
  22.4 0.7 collective-permute-start.12
  23.1 7.1 %collective-permute-done.8 = bf16[256,256]{1,0:T(8,128)(2,1)S(1)} collective-permute-done((bf16[256,256]{1,0:T(8,128)(2,1)S(1)}, bf16[256,256]{1,0:T(8,128)(2,1)S(1)}, u32[]{:S(2)}, u32[]{:S(2)}) %collective-permute-start.8) | collective-permute-done | bytes 131104 | tf_op jit(solution)/shard_map/ppermute | solution.py:51
  30.3 1.9 collective-permute-start.2
  32.2 0.9 collective-permute-done.9
  33.1 1.9 collective-permute-start.3
  35.0 7.7 %collective-permute-start.4 = (bf16[2,256,256]{2,1,0:T(8,128)(2,1)S(1)}, bf16[2,256,256]{2,1,0:T(8,128)(2,1)S(1)}, u32[]{:S(2)}, u32[]{:S(2)}) collective-permute-start(bf16[2,256,256]{2,1,0:T(8,128)(2,1)S(1)} %get-tuple-element.25), channel_id=1, source_target_pairs={{0,192},{1,193},{2,194},{3,195},{4,196},{5,197},{6,198},{7,199},{8... | collective-permute-start | bytes 786440 | tf_op jit(solution)/shard_map/ppermute | solution.py:51
  42.8 3.6 %collective-permute-start = (bf16[256,640]{1,0:T(8,128)(2,1)S(1)}, bf16[256,640]{1,0:T(8,128)(2,1)S(1)}, u32[]{:S(2)}, u32[]{:S(2)}) collective-permute-start(bf16[256,640]{1,0:T(8,128)(2,1)S(1)} %pad_maximum_fusion.3), channel_id=1, source_target_pairs={{0,32},{1,33},{2,34},{3,35},{4,36},{5,37},{6,38},{7,39},{8,40},{9,... | collective-permute-start | bytes 983048 | tf_op jit(solution)/shard_map/ppermute | solution.py:51
  46.4 1.9 collective-permute-start.13
  48.3 11.7 %collective-permute-done.4 = bf16[2,256,256]{2,1,0:T(8,128)(2,1)S(1)} collective-permute-done((bf16[2,256,256]{2,1,0:T(8,128)(2,1)S(1)}, bf16[2,256,256]{2,1,0:T(8,128)(2,1)S(1)}, u32[]{:S(2)}, u32[]{:S(2)}) %collective-permute-start.4) | collective-permute-done | bytes 262176 | tf_op jit(solution)/shard_map/ppermute | solution.py:51
  60.2 3.9 %collective-permute-start.5 = (bf16[4,2,256,256]{3,2,1,0:T(8,128)(2,1)S(1)}, bf16[4,2,256,256]{3,2,1,0:T(8,128)(2,1)S(1)}, u32[]{:S(2)}, u32[]{:S(2)}) collective-permute-start(bf16[4,2,256,256]{3,2,1,0:T(8,128)(2,1)S(1)} %pad_maximum_fusion.1), channel_id=1, source_target_pairs={{0,32},{1,33},{2,34},{3,35},{4,36},{5,37},{6,38},{7,39},{8,40},{9,... | collective-permute-start | bytes 3145736 | tf_op jit(solution)/shard_map/ppermute | solution.py:51
  64.1 0.3 maximum_select_fusion
  64.4 0.1 fusion.60
  64.6 0.7 convert_reduce_fusion.1
  65.3 0.6 add_select_fusion.1
  65.9 0.3 fusion.88
  66.3 0.2 fusion.32
  66.6 0.9 fusion.89
  67.5 0.9 fusion.90
  68.3 0.9 fusion.4
  69.2 0.6 fusion.6
  69.8 0.6 fusion.19
  70.4 10.7 %collective-permute-start.14 = (bf16[160,256]{1,0:T(8,128)(2,1)S(1)}, bf16[160,256]{1,0:T(8,128)(2,1)S(1)}, u32[]{:S(2)}, u32[]{:S(2)}) collective-permute-start(bf16[160,256]{1,0:T(8,128)(2,1)S(1)} %pad_maximum_fusion.8), channel_id=1, source_target_pairs={{0,256},{1,257},{2,258},{3,259},{4,260},{5,261},{6,262},{7,263},{8... | collective-permute-start | bytes 245768 | tf_op jit(solution)/shard_map/ppermute | solution.py:51
  81.1 0.2 broadcast_select_fusion
  81.3 0.2 fusion.23
  81.5 0.3 pad_maximum_fusion
  81.8 2.2 %collective-permute-done.14 = bf16[160,256]{1,0:T(8,128)(2,1)S(1)} collective-permute-done((bf16[160,256]{1,0:T(8,128)(2,1)S(1)}, bf16[160,256]{1,0:T(8,128)(2,1)S(1)}, u32[]{:S(2)}, u32[]{:S(2)}) %collective-permute-start.14) | collective-permute-done | bytes 81952 | tf_op jit(solution)/shard_map/ppermute | solution.py:51
  84.0 2.4 %convert_bitcast_fusion = bf16[16,320,256]{2,1,0:T(8,128)(2,1)} fusion(bf16[16,256,256]{2,1,0:T(8,128)(2,1)S(1)} %bitcast.44, bf16[160,256]{1,0:T(8,128)(2,1)S(1)} %collective-permute-done.14, bf16[160,128]{1,0:T(8,128)(2,1)S(1)} %get-tuple-element.39, bf16[160,128]{1,0:T(8,128)(2,1)S(1)} %get-tuple-element.38), kind=kOutput, calls=%fused_computation.12 | convolution fusion | flops 672890880 | bytes 4882432 | tf_op jit(solution)/shard_map/rk,ekn->ern/dot_general | solution.py:149
  86.4 7.1 %all-to-all-start = ((bf16[16,320,256]{2,1,0:T(8,128)(2,1)}), bf16[16,320,256]{2,1,0:T(8,128)(2,1)S(1)}, u32[]{:S(2)}, u32[]{:S(2)}) async-start(bf16[16,320,256]{2,1,0:T(8,128)(2,1)} %convert_bitcast_fusion), calls=%async_computation | async-start | bytes 5242880 | tf_op jit(solution)/shard_map/all_to_all | solution.py:55
  93.5 1.4 multiply_convert_fusion
  95.0 0.3 copy.38
  95.2 1.9 copy.41
  97.2 2.5 %reshape.177 = bf16[16,64,512]{2,1,0:T(8,128)(2,1)} reshape(bf16[16,64,2,256]{3,2,1,0:T(2,128)(2,1)} %bitcast.46) | data formatting | bytes 2097152 | tf_op jit(solution)/shard_map/reshape | solution.py:103
  99.7 28.5 %all-to-all-done = bf16[16,320,256]{2,1,0:T(8,128)(2,1)S(1)} async-done(((bf16[16,320,256]{2,1,0:T(8,128)(2,1)}), bf16[16,320,256]{2,1,0:T(8,128)(2,1)S(1)}, u32[]{:S(2)}, u32[]{:S(2)}) %all-to-all-start) | async-done | bytes 2621472 | tf_op jit(solution)/shard_map/all_to_all | solution.py:55
  128.2 6.8 %all-to-all-start.1 = ((bf16[16,64,512]{2,1,0:T(8,128)(2,1)}), bf16[16,64,512]{2,1,0:T(8,128)(2,1)}, u32[]{:S(2)}, u32[]{:S(2)}) async-start(bf16[16,64,512]{2,1,0:T(8,128)(2,1)} %reshape.177), calls=%async_computation.1 | async-start | bytes 2097152 | tf_op jit(solution)/shard_map/all_to_all | solution.py:55
  135.0 8.9 %collective-permute-start.1 = (bf16[160,256]{1,0:T(8,128)(2,1)S(1)}, bf16[160,256]{1,0:T(8,128)(2,1)}, u32[]{:S(2)}, u32[]{:S(2)}) collective-permute-start(bf16[160,256]{1,0:T(8,128)(2,1)S(1)} %get-tuple-element.28), channel_id=1, source_target_pairs={{0,16},{1,17},{2,18},{3,19},{4,20},{5,21},{6,22},{7,23},{8,24},{9,... | collective-permute-start | bytes 245768 | tf_op jit(solution)/shard_map/ppermute | solution.py:51
  143.9 0.4 reduce_sum.85
  144.3 5.1 %collective-permute-start.15 = (bf16[160,256]{1,0:T(8,128)(2,1)S(1)}, bf16[160,256]{1,0:T(8,128)(2,1)S(1)}, u32[]{:S(2)}, u32[]{:S(2)}) collective-permute-start(bf16[160,256]{1,0:T(8,128)(2,1)S(1)} %get-tuple-element.30), channel_id=1, source_target_pairs={{0,16},{1,17},{2,18},{3,19},{4,20},{5,21},{6,22},{7,23},{8,24},{9,... | collective-permute-start | bytes 245768 | tf_op jit(solution)/shard_map/ppermute | solution.py:51
  149.4 8.2 %collective-permute-start.16 = (bf16[160,256]{1,0:T(8,128)(2,1)S(1)}, bf16[160,256]{1,0:T(8,128)(2,1)S(1)}, u32[]{:S(2)}, u32[]{:S(2)}) collective-permute-start(bf16[160,256]{1,0:T(8,128)(2,1)S(1)} %get-tuple-element.31), channel_id=1, source_target_pairs={{0,256},{1,257},{2,258},{3,259},{4,260},{5,261},{6,262},{7,263},{8... | collective-permute-start | bytes 245768 | tf_op jit(solution)/shard_map/ppermute | solution.py:51
  157.6 3.8 %collective-permute-start.17 = (bf16[160,256]{1,0:T(8,128)(2,1)S(1)}, bf16[160,256]{1,0:T(8,128)(2,1)S(1)}, u32[]{:S(2)}, u32[]{:S(2)}) collective-permute-start(bf16[160,256]{1,0:T(8,128)(2,1)S(1)} %get-tuple-element.31), channel_id=1, source_target_pairs={{0,272},{1,273},{2,274},{3,275},{4,276},{5,277},{6,278},{7,279},{8... | collective-permute-start | bytes 245768 | tf_op jit(solution)/shard_map/ppermute | solution.py:51
  161.4 4.4 %collective-permute-done.16 = bf16[160,256]{1,0:T(8,128)(2,1)S(1)} collective-permute-done((bf16[160,256]{1,0:T(8,128)(2,1)S(1)}, bf16[160,256]{1,0:T(8,128)(2,1)S(1)}, u32[]{:S(2)}, u32[]{:S(2)}) %collective-permute-start.16) | collective-permute-done | bytes 81952 | tf_op jit(solution)/shard_map/ppermute | solution.py:51
  165.8 1.9 collective-permute-done.17
  167.7 1.0 broadcast_select_fusion.2
  168.9 1.7 fusion.12
  170.6 0.2 pad_maximum_fusion.2
  170.8 1.2 copy.27
  172.0 6.6 %all-to-all-start.2 = ((bf16[16,160,128]{2,1,0:T(8,128)(2,1)}), bf16[16,160,128]{2,1,0:T(8,128)(2,1)S(1)}, u32[]{:S(2)}, u32[]{:S(2)}) async-start(bf16[16,160,128]{2,1,0:T(8,128)(2,1)} %copy.27), calls=%async_computation.2 | async-start | bytes 1310720 | tf_op jit(solution)/shard_map/all_to_all | solution.py:55
  179.3 0.2 fusion.56
  179.5 8.9 %all-to-all-done.2 = bf16[16,160,128]{2,1,0:T(8,128)(2,1)S(1)} async-done(((bf16[16,160,128]{2,1,0:T(8,128)(2,1)}), bf16[16,160,128]{2,1,0:T(8,128)(2,1)S(1)}, u32[]{:S(2)}, u32[]{:S(2)}) %all-to-all-start.2) | async-done | bytes 655392 | tf_op jit(solution)/shard_map/all_to_all | solution.py:55
  189.0 0.4 fusion.54
  189.5 6.5 %collective-permute-start.18 = (bf16[160,384]{1,0:T(8,128)(2,1)S(1)}, bf16[160,384]{1,0:T(8,128)(2,1)S(1)}, u32[]{:S(2)}, u32[]{:S(2)}) collective-permute-start(bf16[160,384]{1,0:T(8,128)(2,1)S(1)} %pad_maximum_fusion.6), channel_id=1, source_target_pairs={{0,32},{1,33},{2,34},{3,35},{4,36},{5,37},{6,38},{7,39},{8,40},{9,... | collective-permute-start | bytes 368648 | tf_op jit(solution)/shard_map/ppermute | solution.py:51
  196.0 0.9 collective-permute-done.18
  197.0 0.3 convolution_convert_fusion.1
  197.3 0.7 slice.128
  198.0 0.7 copy.30
  (71 shorter events, 1.7 us)
Async XLA Ops:
  0.6 20.9 %copy-start.1 = (bf16[256,256]{1,0:T(8,128)(2,1)S(1)}, bf16[256,256]{1,0:T(8,128)(2,1)}, u32[]{:S(2)}) copy-start(bf16[256,256]{1,0:T(8,128)(2,1)} %param.10) | copy-start | bytes 393220
  0.6 20.9 %copy-start = (bf16[256,256]{1,0:T(8,128)(2,1)S(1)}, bf16[256,256]{1,0:T(8,128)(2,1)}, u32[]{:S(2)}) copy-start(bf16[256,256]{1,0:T(8,128)(2,1)} %param.9) | copy-start | bytes 393220
  1.8 19.9 %collective-permute-start.6 = (bf16[256,256]{1,0:T(8,128)(2,1)S(1)}, bf16[256,256]{1,0:T(8,128)(2,1)S(1)}, u32[]{:S(2)}, u32[]{:S(2)}) collective-permute-start(bf16[256,256]{1,0:T(8,128)(2,1)S(1)} %get-tuple-element.16), channel_id=1, source_target_pairs={{0,64},{1,65},{2,66},{3,67},{4,68},{5,69},{6,70},{7,71},{8,72},{9,... | collective-permute-start | bytes 393224 | tf_op jit(solution)/shard_map/ppermute | solution.py:51
  5.3 17.1 %collective-permute-start.7 = (bf16[256,256]{1,0:T(8,128)(2,1)S(1)}, bf16[256,256]{1,0:T(8,128)(2,1)S(1)}, u32[]{:S(2)}, u32[]{:S(2)}) collective-permute-start(bf16[256,256]{1,0:T(8,128)(2,1)S(1)} %get-tuple-element.16), channel_id=1, source_target_pairs={{0,128},{1,129},{2,130},{3,131},{4,132},{5,133},{6,134},{7,135},{8... | collective-permute-start | bytes 393224 | tf_op jit(solution)/shard_map/ppermute | solution.py:51
  11.4 18.8 %collective-permute-start.8 = (bf16[256,256]{1,0:T(8,128)(2,1)S(1)}, bf16[256,256]{1,0:T(8,128)(2,1)S(1)}, u32[]{:S(2)}, u32[]{:S(2)}) collective-permute-start(bf16[256,256]{1,0:T(8,128)(2,1)S(1)} %get-tuple-element.16), channel_id=1, source_target_pairs={{0,192},{1,193},{2,194},{3,195},{4,196},{5,197},{6,198},{7,199},{8... | collective-permute-start | bytes 393224 | tf_op jit(solution)/shard_map/ppermute | solution.py:51
  15.4 17.6 %collective-permute-start.9 = (bf16[256,256]{1,0:T(8,128)(2,1)S(1)}, bf16[256,256]{1,0:T(8,128)(2,1)S(1)}, u32[]{:S(2)}, u32[]{:S(2)}) collective-permute-start(bf16[256,256]{1,0:T(8,128)(2,1)S(1)} %get-tuple-element.16), channel_id=1, source_target_pairs={{0,256},{1,257},{2,258},{3,259},{4,260},{5,261},{6,262},{7,263},{8... | collective-permute-start | bytes 393224 | tf_op jit(solution)/shard_map/ppermute | solution.py:51
  16.7 18.3 %collective-permute-start.10 = (bf16[256,256]{1,0:T(8,128)(2,1)S(1)}, bf16[256,256]{1,0:T(8,128)(2,1)S(1)}, u32[]{:S(2)}, u32[]{:S(2)}) collective-permute-start(bf16[256,256]{1,0:T(8,128)(2,1)S(1)} %get-tuple-element.23), channel_id=1, source_target_pairs={{0,336},{1,337},{2,338},{3,339},{4,340},{5,341},{6,342},{7,343},{8... | collective-permute-start | bytes 393224 | tf_op jit(solution)/shard_map/ppermute | solution.py:51
  21.7 21.1 %collective-permute-start.11 = (bf16[256,256]{1,0:T(8,128)(2,1)S(1)}, bf16[256,256]{1,0:T(8,128)(2,1)S(1)}, u32[]{:S(2)}, u32[]{:S(2)}) collective-permute-start(bf16[256,256]{1,0:T(8,128)(2,1)S(1)} %get-tuple-element.23), channel_id=1, source_target_pairs={{0,400},{1,401},{2,402},{3,403},{4,404},{5,405},{6,406},{7,407},{8... | collective-permute-start | bytes 393224 | tf_op jit(solution)/shard_map/ppermute | solution.py:51
  22.4 24.0 %collective-permute-start.12 = (bf16[256,256]{1,0:T(8,128)(2,1)S(1)}, bf16[256,256]{1,0:T(8,128)(2,1)S(1)}, u32[]{:S(2)}, u32[]{:S(2)}) collective-permute-start(bf16[256,256]{1,0:T(8,128)(2,1)S(1)} %get-tuple-element.23), channel_id=1, source_target_pairs={{0,464},{1,465},{2,466},{3,467},{4,468},{5,469},{6,470},{7,471},{8... | collective-permute-start | bytes 393224 | tf_op jit(solution)/shard_map/ppermute | solution.py:51
  30.3 18.1 %collective-permute-start.2 = (bf16[2,256,256]{2,1,0:T(8,128)(2,1)S(1)}, bf16[2,256,256]{2,1,0:T(8,128)(2,1)S(1)}, u32[]{:S(2)}, u32[]{:S(2)}) collective-permute-start(bf16[2,256,256]{2,1,0:T(8,128)(2,1)S(1)} %get-tuple-element.25), channel_id=1, source_target_pairs={{0,64},{1,65},{2,66},{3,67},{4,68},{5,69},{6,70},{7,71},{8,72},{9,... | collective-permute-start | bytes 786440 | tf_op jit(solution)/shard_map/ppermute | solution.py:51
  33.1 15.3 %collective-permute-start.3 = (bf16[2,256,256]{2,1,0:T(8,128)(2,1)S(1)}, bf16[2,256,256]{2,1,0:T(8,128)(2,1)S(1)}, u32[]{:S(2)}, u32[]{:S(2)}) collective-permute-start(bf16[2,256,256]{2,1,0:T(8,128)(2,1)S(1)} %get-tuple-element.25), channel_id=1, source_target_pairs={{0,128},{1,129},{2,130},{3,131},{4,132},{5,133},{6,134},{7,135},{8... | collective-permute-start | bytes 786440 | tf_op jit(solution)/shard_map/ppermute | solution.py:51
  35.0 25.1 %collective-permute-start.4 = (bf16[2,256,256]{2,1,0:T(8,128)(2,1)S(1)}, bf16[2,256,256]{2,1,0:T(8,128)(2,1)S(1)}, u32[]{:S(2)}, u32[]{:S(2)}) collective-permute-start(bf16[2,256,256]{2,1,0:T(8,128)(2,1)S(1)} %get-tuple-element.25), channel_id=1, source_target_pairs={{0,192},{1,193},{2,194},{3,195},{4,196},{5,197},{6,198},{7,199},{8... | collective-permute-start | bytes 786440 | tf_op jit(solution)/shard_map/ppermute | solution.py:51
  42.8 21.4 %collective-permute-start = (bf16[256,640]{1,0:T(8,128)(2,1)S(1)}, bf16[256,640]{1,0:T(8,128)(2,1)S(1)}, u32[]{:S(2)}, u32[]{:S(2)}) collective-permute-start(bf16[256,640]{1,0:T(8,128)(2,1)S(1)} %pad_maximum_fusion.3), channel_id=1, source_target_pairs={{0,32},{1,33},{2,34},{3,35},{4,36},{5,37},{6,38},{7,39},{8,40},{9,... | collective-permute-start | bytes 983048 | tf_op jit(solution)/shard_map/ppermute | solution.py:51
  46.4 21.0 %collective-permute-start.13 = (bf16[2048,256]{1,0:T(8,128)(2,1)S(1)}, bf16[2048,256]{1,0:T(8,128)(2,1)S(1)}, u32[]{:S(2)}, u32[]{:S(2)}) collective-permute-start(bf16[2048,256]{1,0:T(8,128)(2,1)S(1)} %constant_dynamic-update-slice_fusion), channel_id=1, source_target_pairs={{0,32},{1,33},{2,34},{3,35},{4,36},{5,37},{6,38},{7,39},{8,40},{9,... | collective-permute-start | bytes 3145736 | tf_op jit(solution)/shard_map/ppermute | solution.py:51
  60.2 20.9 %collective-permute-start.5 = (bf16[4,2,256,256]{3,2,1,0:T(8,128)(2,1)S(1)}, bf16[4,2,256,256]{3,2,1,0:T(8,128)(2,1)S(1)}, u32[]{:S(2)}, u32[]{:S(2)}) collective-permute-start(bf16[4,2,256,256]{3,2,1,0:T(8,128)(2,1)S(1)} %pad_maximum_fusion.1), channel_id=1, source_target_pairs={{0,32},{1,33},{2,34},{3,35},{4,36},{5,37},{6,38},{7,39},{8,40},{9,... | collective-permute-start | bytes 3145736 | tf_op jit(solution)/shard_map/ppermute | solution.py:51
  70.4 13.6 %collective-permute-start.14 = (bf16[160,256]{1,0:T(8,128)(2,1)S(1)}, bf16[160,256]{1,0:T(8,128)(2,1)S(1)}, u32[]{:S(2)}, u32[]{:S(2)}) collective-permute-start(bf16[160,256]{1,0:T(8,128)(2,1)S(1)} %pad_maximum_fusion.8), channel_id=1, source_target_pairs={{0,256},{1,257},{2,258},{3,259},{4,260},{5,261},{6,262},{7,263},{8... | collective-permute-start | bytes 245768 | tf_op jit(solution)/shard_map/ppermute | solution.py:51
  86.4 7.1 %copy-start.2 = (f32[8192]{0:T(1024)S(1)}, f32[8192]{0:T(1024)}, u32[]{:S(2)}) copy-start(f32[8192]{0:T(1024)} %param.13) | copy-start | bytes 98308
  86.4 41.8 %all-to-all-start = ((bf16[16,320,256]{2,1,0:T(8,128)(2,1)}), bf16[16,320,256]{2,1,0:T(8,128)(2,1)S(1)}, u32[]{:S(2)}, u32[]{:S(2)}) async-start(bf16[16,320,256]{2,1,0:T(8,128)(2,1)} %convert_bitcast_fusion), calls=%async_computation | async-start | bytes 5242880 | tf_op jit(solution)/shard_map/all_to_all | solution.py:55
  128.2 40.6 %all-to-all-start.1 = ((bf16[16,64,512]{2,1,0:T(8,128)(2,1)}), bf16[16,64,512]{2,1,0:T(8,128)(2,1)}, u32[]{:S(2)}, u32[]{:S(2)}) async-start(bf16[16,64,512]{2,1,0:T(8,128)(2,1)} %reshape.177), calls=%async_computation.1 | async-start | bytes 2097152 | tf_op jit(solution)/shard_map/all_to_all | solution.py:55
  135.0 26.4 %collective-permute-start.1 = (bf16[160,256]{1,0:T(8,128)(2,1)S(1)}, bf16[160,256]{1,0:T(8,128)(2,1)}, u32[]{:S(2)}, u32[]{:S(2)}) collective-permute-start(bf16[160,256]{1,0:T(8,128)(2,1)S(1)} %get-tuple-element.28), channel_id=1, source_target_pairs={{0,16},{1,17},{2,18},{3,19},{4,20},{5,21},{6,22},{7,23},{8,24},{9,... | collective-permute-start | bytes 245768 | tf_op jit(solution)/shard_map/ppermute | solution.py:51
  144.3 17.1 %collective-permute-start.15 = (bf16[160,256]{1,0:T(8,128)(2,1)S(1)}, bf16[160,256]{1,0:T(8,128)(2,1)S(1)}, u32[]{:S(2)}, u32[]{:S(2)}) collective-permute-start(bf16[160,256]{1,0:T(8,128)(2,1)S(1)} %get-tuple-element.30), channel_id=1, source_target_pairs={{0,16},{1,17},{2,18},{3,19},{4,20},{5,21},{6,22},{7,23},{8,24},{9,... | collective-permute-start | bytes 245768 | tf_op jit(solution)/shard_map/ppermute | solution.py:51
  149.4 16.4 %collective-permute-start.16 = (bf16[160,256]{1,0:T(8,128)(2,1)S(1)}, bf16[160,256]{1,0:T(8,128)(2,1)S(1)}, u32[]{:S(2)}, u32[]{:S(2)}) collective-permute-start(bf16[160,256]{1,0:T(8,128)(2,1)S(1)} %get-tuple-element.31), channel_id=1, source_target_pairs={{0,256},{1,257},{2,258},{3,259},{4,260},{5,261},{6,262},{7,263},{8... | collective-permute-start | bytes 245768 | tf_op jit(solution)/shard_map/ppermute | solution.py:51
  157.6 10.1 %collective-permute-start.17 = (bf16[160,256]{1,0:T(8,128)(2,1)S(1)}, bf16[160,256]{1,0:T(8,128)(2,1)S(1)}, u32[]{:S(2)}, u32[]{:S(2)}) collective-permute-start(bf16[160,256]{1,0:T(8,128)(2,1)S(1)} %get-tuple-element.31), channel_id=1, source_target_pairs={{0,272},{1,273},{2,274},{3,275},{4,276},{5,277},{6,278},{7,279},{8... | collective-permute-start | bytes 245768 | tf_op jit(solution)/shard_map/ppermute | solution.py:51
  172.0 16.4 %all-to-all-start.2 = ((bf16[16,160,128]{2,1,0:T(8,128)(2,1)}), bf16[16,160,128]{2,1,0:T(8,128)(2,1)S(1)}, u32[]{:S(2)}, u32[]{:S(2)}) async-start(bf16[16,160,128]{2,1,0:T(8,128)(2,1)} %copy.27), calls=%async_computation.2 | async-start | bytes 1310720 | tf_op jit(solution)/shard_map/all_to_all | solution.py:55
  189.5 7.4 %collective-permute-start.18 = (bf16[160,384]{1,0:T(8,128)(2,1)S(1)}, bf16[160,384]{1,0:T(8,128)(2,1)S(1)}, u32[]{:S(2)}, u32[]{:S(2)}) collective-permute-start(bf16[160,384]{1,0:T(8,128)(2,1)S(1)} %pad_maximum_fusion.6), channel_id=1, source_target_pairs={{0,32},{1,33},{2,34},{3,35},{4,36},{5,37},{6,38},{7,39},{8,40},{9,... | collective-permute-start | bytes 368648 | tf_op jit(solution)/shard_map/ppermute | solution.py:51

commit v2 on v1

--- a/solution.py
+++ b/solution.py
@@ -40,19 +40,27 @@
 EIGHT = pairs(lambda zh, zl, core: (1 - zh, zl, core))
 TWELVE = pairs(lambda zh, zl, core: (1 - zh, zl ^ 4, core))
 QUAD = [None] + [pairs(lambda zh, zl, core, k=k: (zh, zl ^ k, core)) for k in (1, 2, 3)]
+
+
+def near(zl, k):
+    return k < 4 or (k == 4 and zl >= 2)
+
+
 BACK = [None] + [
-    pairs(lambda zh, zl, core, k=k: (zh if k <= 4 else 1 - zh, zl + k, core) if zl + k < ZL else None)
+    pairs(lambda zh, zl, core, k=k: (zh if near(zl, k) else 1 - zh, zl + k, core) if zl + k < ZL else None)
     for k in range(1, ZL)
 ]
 PLANES = [[half * NX * NY + i for i in range(NX * NY)] for half in range(ZH)]
+ALONG_Y = [[start * NY + y for y in range(NY)] for start in range(ZH * NX)]
+ALONG_X = [[half * NX * NY + x * NY + y for x in range(NX)] for half in range(ZH) for y in range(NY)]
 
 
 def send(x, table):
     return lax.ppermute(x, AXES, table)
 
 
-def plane_exchange(x):
-    return lax.all_to_all(x, "tp", 0, 0, tiled=True, axis_index_groups=PLANES)
+def exchange(x, groups):
+    return lax.all_to_all(x, "tp", 0, 0, tiled=True, axis_index_groups=groups)
 
 
 def turn(cache_rows, position_ids, first_col):
@@ -91,16 +99,21 @@
     far_head = (1 - zh) * (KVH // ZH) + plane // NY
     own_kv = lax.dynamic_slice_in_dim(keys_values, head * 2 * HD, 2 * HD, 1)
     far_kv = lax.dynamic_slice_in_dim(keys_values, far_head * 2 * HD, 2 * HD, 1)
-    blocks = [own_kv] + [send(own_kv if k <= 4 else far_kv, BACK[k]) for k in range(1, ZL)]
-
-    weight = jnp.stack([out_weight[:, :256], out_weight[:, 256:]])
-    quad = jnp.stack([weight] + [send(weight, QUAD[k]) for k in (1, 2, 3)])
-    quad_other = send(quad, CORE)
+    sent = {4: jnp.where(zl >= 2, own_kv, far_kv)}
+    blocks = [own_kv] + [send(sent.get(k, own_kv if k < 4 else far_kv), BACK[k]) for k in range(1, ZL)]
 
     columns = cache_weight.shape[1]
     gained = (cache_weight.astype(F32) * norm_gain[:, None]).astype(BF)
     gained = gained.T.reshape(columns, ZH, NX * NY, D // (ZH * NX * NY)).transpose(2, 0, 1, 3)
-    gained = plane_exchange(gained.reshape(NX * NY, columns, -1))
+    gained = exchange(gained.reshape(NX * NY, columns, -1), PLANES)
+
+    kept_rows = lax.dynamic_slice_in_dim(out_weight, core * HD, HD, 0)
+    given_rows = lax.dynamic_slice_in_dim(out_weight, (1 - core) * HD, HD, 0)
+    taken_rows = send(given_rows, CORE)
+    weight = jnp.concatenate(
+        [jnp.where(first, kept_rows, taken_rows), jnp.where(first, taken_rows, kept_rows)], axis=1
+    )
+    weight = exchange(weight.reshape(HD, NY, 256).transpose(1, 0, 2), ALONG_Y).reshape(NY * HD, 256)
 
     pair = jnp.where(first, jnp.concatenate([mine, theirs]), jnp.concatenate([theirs, mine]))
     pair_rank = pair[:, 512].astype(jnp.int32)
@@ -117,7 +130,11 @@
     far_residual = send(own_residual, EIGHT)
 
     kv_mine = jnp.concatenate(blocks)
+    kv_mine, weight, query, gained, far_residual = lax.optimization_barrier(
+        (kv_mine, weight, query, gained, far_residual)
+    )
     kv_theirs = send(kv_mine, CORE)
+    quad = [weight] + [send(weight, QUAD[k]) for k in (1, 2, 3)]
     key_row = jnp.arange(ZL * rows, dtype=jnp.int32)
     key_token = (zl - key_row // rows) * 2 * rows + key_row % rows
     query_token = jnp.concatenate([token, token])
@@ -137,20 +154,23 @@
         prob_b.astype(BF), kv_theirs[:, HD:], preferred_element_type=F32
     )
     attended = (mixed / total[:, None]).astype(BF)
-    attended = jnp.concatenate([attended[:OWN], attended[OWN:]], axis=1)
-
-    both = jnp.concatenate([attended, send(attended, FOUR)])
-    low = jnp.where(first, quad, quad_other)
-    high = jnp.where(first, quad_other, quad)
-    blocks_w = jnp.concatenate([low, high], axis=1)
-    arranged = jnp.stack(
-        [lax.dynamic_index_in_dim(blocks_w, (zl % 4) ^ k, 0, keepdims=False) for k in range(4)]
-    ).reshape(NX * NY, 256, 256)
-    terms = jnp.einsum("rk,ekn->ern", both, arranged, preferred_element_type=F32).astype(BF)
-    summed = jnp.sum(plane_exchange(terms).reshape(NX * NY, 2 * OWN, 256).astype(F32), axis=0).astype(BF)
-    near, far = summed[:OWN], summed[OWN:]
-    from4, from8, from12 = send(far, FOUR), send(near, EIGHT), send(far, TWELVE)
-    same = near.astype(F32) + from8.astype(F32)
+    attended = attended.reshape(2, OWN, HD)
+
+    both = jnp.stack([attended, send(attended, FOUR)])
+    both, quad = lax.optimization_barrier((both, quad))
+    heads = exchange(jnp.broadcast_to(both[None], (NY,) + both.shape).reshape(NY * 2, 2, OWN, HD), ALONG_Y)
+    heads = heads.reshape(NY, 2, 2, OWN, HD).transpose(1, 3, 2, 0, 4).reshape(2 * OWN, 2 * NY * HD)
+    quad = jnp.stack(quad)
+    quad = jnp.stack([lax.dynamic_index_in_dim(quad, (zl % 4) ^ k, 0, keepdims=False) for k in range(NX)])
+    quad_other = send(quad, CORE)
+    full = jnp.concatenate(
+        [jnp.where(first, quad, quad_other), jnp.where(first, quad_other, quad)], axis=1
+    )
+    terms = jnp.einsum("rk,ekn->ern", heads, full, preferred_element_type=F32).astype(BF)
+    summed = jnp.sum(exchange(terms, ALONG_X).reshape(NX, 2 * OWN, 256).astype(F32), axis=0).astype(BF)
+    here, away = summed[:OWN], summed[OWN:]
+    from4, from8, from12 = send(away, FOUR), send(here, EIGHT), send(away, TWELVE)
+    same = here.astype(F32) + from8.astype(F32)
     cross = from4.astype(F32) + from12.astype(F32)
     low_half = zl < 4
     first_half = jnp.where(low_half, same, cross)
@@ -168,7 +188,7 @@
     ).astype(BF)
     tail = jnp.pad(jnp.concatenate([square_high, square_low], axis=1), ((0, 0), (0, 128 - columns - 2)))
     message = jnp.concatenate([parts, jnp.broadcast_to(tail[None], (NX * NY,) + tail.shape)], axis=2)
-    gathered = jnp.sum(plane_exchange(message).astype(F32), axis=0)
+    gathered = jnp.sum(exchange(message, PLANES).astype(F32), axis=0)
     square_total = gathered[:, columns] + gathered[:, columns + 1]
     cache_rows = gathered[:, :columns] * lax.rsqrt(square_total / D + EPS)[:, None]
     cache_rot = turn(cache_rows, position, tp * columns).astype(BF)

time: 200 us -> 202 us (1.010)
  blocking collectives: 0 us -> 27.8 us
  waiting for transfers between devices: 66.6 us -> 40.2 us
  local copies, waits for them, and re-layouts: 10.2 us -> 13 us
  starting transfers between devices: 102 us -> 99.8 us
  other arithmetic: 9.36 us -> 11.5 us
    all_to_all x3, waiting for transfers between devices: 37.4 us -> 8.83 us  [exchange(): return lax.all_to_all(x, 'tp', 0, 0, tiled=True, axis_index_groups=groups)]
    all_to_all x0 -> x2, blocking collectives: none -> 27.8 us  [exchange(): return lax.all_to_all(x, 'tp', 0, 0, tiled=True, axis_index_groups=groups)]
    all_to_all x3, starting transfers between devices: 20.5 us -> 14.6 us  [exchange(): return lax.all_to_all(x, 'tp', 0, 0, tiled=True, axis_index_groups=groups)]
    ppermute x19 -> x20, starting transfers between devices: 81.6 us -> 85.2 us  [send(): return lax.ppermute(x, AXES, table)]
    select_n x1 -> x3, other arithmetic: 0.19 us -> 2.86 us  [the longest x1 1.71 us: shards(): sent = {4: jnp.where(zl >= 2, own_kv, far_kv)}]
    ppermute x19 -> x20, waiting for transfers between devices: 29.2 us -> 31.4 us  [send(): return lax.ppermute(x, AXES, table)]
    reshape x2 -> x3, local copies, waits for them, and re-layouts: 4.47 us -> 3.53 us  [the longest x1 1.5 us: shards(): gained = exchange(gained.reshape(NX * NY, columns, -1), PLANES)]
  transfers between devices with their start and end apart: 22 -> 23, of which waited for: 9 -> 6; matrix products, arithmetic and copies ran while one was open for 9% -> 9% of each run, Pallas kernels for 0% -> 0%
where the time goes in v2:
time: 202 us; the launch traced here: 201 us
  starting transfers between devices  99.8 us (49%)
  waiting for transfers between devices  40.2 us (20%)
  blocking collectives  27.8 us (14%)
  local copies, waits for them, and re-layouts  13 us (6%)
  other arithmetic  11.5 us (6%)
  matrix products  5.9 us (3%)
  between operations  2.84 us (1%)
    ppermute x20, starting transfers between devices, send(): return lax.ppermute(x, AXES, table)  85.2 us
    ppermute x20, waiting for transfers between devices, send(): return lax.ppermute(x, AXES, table)  31.4 us
    all_to_all x2, blocking collectives, exchange(): return lax.all_to_all(x, 'tp', 0, 0, tiled=True, axis_index_groups=groups)  27.8 us
    all_to_all x3, starting transfers between devices, exchange(): return lax.all_to_all(x, 'tp', 0, 0, tiled=True, axis_index_groups=groups)  14.6 us
    all_to_all x3, waiting for transfers between devices, exchange(): return lax.all_to_all(x, 'tp', 0, 0, tiled=True, axis_index_groups=groups)  8.83 us
  transfers between devices with their start and end apart: 23, of which 6 were waited for; matrix products, arithmetic and copies ran while one was open for 9% of the time, Pallas kernels for 0%

profile of v2, /device:TPU:65, one launch (start us, length us, event | category | flops | bytes accessed | tf_op | source)
XLA Modules:
  0.0 201.1 jit_solution(277701177967381868)
XLA Ops:
  0.7 1.7 broadcast_select_fusion.4
  2.4 3.5 %collective-permute-start.1 = (bf16[256,256]{1,0:T(8,128)(2,1)S(1)}, bf16[256,256]{1,0:T(8,128)(2,1)S(1)}, u32[]{:S(2)}, u32[]{:S(2)}) collective-permute-start(bf16[256,256]{1,0:T(8,128)(2,1)S(1)} %get-tuple-element.37), channel_id=1, source_target_pairs={{0,64},{1,65},{2,66},{3,67},{4,68},{5,69},{6,70},{7,71},{8,72},{9,... | collective-permute-start | bytes 393224 | tf_op jit(solution)/shard_map/ppermute | solution.py:59
  6.0 6.1 %collective-permute-start.2 = (bf16[256,256]{1,0:T(8,128)(2,1)S(1)}, bf16[256,256]{1,0:T(8,128)(2,1)S(1)}, u32[]{:S(2)}, u32[]{:S(2)}) collective-permute-start(bf16[256,256]{1,0:T(8,128)(2,1)S(1)} %get-tuple-element.37), channel_id=1, source_target_pairs={{0,128},{1,129},{2,130},{3,131},{4,132},{5,133},{6,134},{7,135},{8... | collective-permute-start | bytes 393224 | tf_op jit(solution)/shard_map/ppermute | solution.py:59
  12.1 4.0 %collective-permute-start.3 = (bf16[256,256]{1,0:T(8,128)(2,1)S(1)}, bf16[256,256]{1,0:T(8,128)(2,1)S(1)}, u32[]{:S(2)}, u32[]{:S(2)}) collective-permute-start(bf16[256,256]{1,0:T(8,128)(2,1)S(1)} %get-tuple-element.37), channel_id=1, source_target_pairs={{0,192},{1,193},{2,194},{3,195},{4,196},{5,197},{6,198},{7,199},{8... | collective-permute-start | bytes 393224 | tf_op jit(solution)/shard_map/ppermute | solution.py:59
  16.1 1.3 collective-permute-start.5
  17.4 0.9 constant_dynamic-slice_fusion.4
  18.3 3.1 %collective-permute-start.8 = (bf16[128,512]{1,0:T(8,128)(2,1)S(1)}, bf16[128,512]{1,0:T(8,128)(2,1)}, u32[]{:S(2)}, u32[]{:S(2)}) collective-permute-start(bf16[128,512]{1,0:T(8,128)(2,1)S(1)} %constant_dynamic-slice_fusion.4), channel_id=1, source_target_pairs={{0,32},{1,33},{2,34},{3,35},{4,36},{5,37},{6,38},{7,39},{8,40},{9,... | collective-permute-start | bytes 393224 | tf_op jit(solution)/shard_map/ppermute | solution.py:59
  21.5 0.7 fusion.75
  22.9 0.8 select_reduce_fusion
  23.7 1.4 multiply_convert_fusion
  25.3 0.2 copy.46
  25.6 1.0 copy.32
  26.6 1.5 reshape.194
  28.2 0.7 collective-permute-start.6
  28.9 1.0 broadcast_select_fusion.3
  29.9 0.7 copy.49
  30.6 4.2 %all-to-all-start = ((bf16[4,128,256]{2,1,0:T(8,128)(2,1)}), bf16[4,128,256]{2,1,0:T(8,128)(2,1)S(1)}, u32[]{:S(2)}, u32[]{:S(2)}) async-start(bf16[4,128,256]{2,1,0:T(8,128)(2,1)} %bitcast.46), calls=%async_computation | async-start | bytes 524288 | tf_op jit(solution)/shard_map/all_to_all | solution.py:63
  34.8 0.7 collective-permute-start.7
  35.5 1.6 collective-permute-start.4
  37.2 2.5 %collective-permute-start = (bf16[256,640]{1,0:T(8,128)(2,1)S(1)}, bf16[256,640]{1,0:T(8,128)(2,1)S(1)}, u32[]{:S(2)}, u32[]{:S(2)}) collective-permute-start(bf16[256,640]{1,0:T(8,128)(2,1)S(1)} %pad_maximum_fusion.3), channel_id=1, source_target_pairs={{0,32},{1,33},{2,34},{3,35},{4,36},{5,37},{6,38},{7,39},{8,40},{9,... | collective-permute-start | bytes 983048 | tf_op jit(solution)/shard_map/ppermute | solution.py:59
  39.7 0.4 collective-permute-done.4
  40.2 1.0 copy-done.5
  41.2 0.3 maximum_select_fusion
  41.5 6.8 %all-to-all-start.1 = ((bf16[16,64,512]{2,1,0:T(8,128)(2,1)}), bf16[16,64,512]{2,1,0:T(8,128)(2,1)S(1)}, u32[]{:S(2)}, u32[]{:S(2)}) async-start(bf16[16,64,512]{2,1,0:T(8,128)(2,1)} %reshape.194), calls=%async_computation.1 | async-start | bytes 2097152 | tf_op jit(solution)/shard_map/all_to_all | solution.py:63
  48.3 0.7 convert_reduce_fusion.1
  49.1 0.7 add_select_fusion.1
  49.8 0.3 fusion.88
  50.2 7.9 %collective-permute-start.9 = (bf16[160,256]{1,0:T(8,128)(2,1)S(1)}, bf16[160,256]{1,0:T(8,128)(2,1)S(1)}, u32[]{:S(2)}, u32[]{:S(2)}) collective-permute-start(bf16[160,256]{1,0:T(8,128)(2,1)S(1)} %get-tuple-element.46), channel_id=1, source_target_pairs={{0,16},{1,17},{2,18},{3,19},{4,20},{5,21},{6,22},{7,23},{8,24},{9,... | collective-permute-start | bytes 245768 | tf_op jit(solution)/shard_map/ppermute | solution.py:59
  58.1 0.7 constant_dynamic-update-slice_fusion
  58.8 5.3 %collective-permute-done.9 = bf16[160,256]{1,0:T(8,128)(2,1)S(1)} collective-permute-done((bf16[160,256]{1,0:T(8,128)(2,1)S(1)}, bf16[160,256]{1,0:T(8,128)(2,1)S(1)}, u32[]{:S(2)}, u32[]{:S(2)}) %collective-permute-start.9) | collective-permute-done | bytes 81952 | tf_op jit(solution)/shard_map/ppermute | solution.py:59
  64.1 4.6 %collective-permute-start.10 = (bf16[2048,256]{1,0:T(8,128)(2,1)}, bf16[2048,256]{1,0:T(8,128)(2,1)S(1)}, u32[]{:S(2)}, u32[]{:S(2)}) collective-permute-start(bf16[2048,256]{1,0:T(8,128)(2,1)} %constant_dynamic-update-slice_fusion), channel_id=1, source_target_pairs={{0,32},{1,33},{2,34},{3,35},{4,36},{5,37},{6,38},{7,39},{8,40},{9,... | collective-permute-start | bytes 3145736 | tf_op jit(solution)/shard_map/ppermute | solution.py:59
  69.0 4.5 %collective-permute-start.12 = (bf16[512,256]{1,0:T(8,128)(2,1)S(1)}, bf16[512,256]{1,0:T(8,128)(2,1)S(1)}, u32[]{:S(2)}, u32[]{:S(2)}) collective-permute-start(bf16[512,256]{1,0:T(8,128)(2,1)S(1)} %bitcast.54), channel_id=1, source_target_pairs={{0,64},{1,65},{2,66},{3,67},{4,68},{5,69},{6,70},{7,71},{8,72},{9,... | collective-permute-start | bytes 786440 | tf_op jit(solution)/shard_map/ppermute | solution.py:59
  73.5 7.8 %collective-permute-start.13 = (bf16[512,256]{1,0:T(8,128)(2,1)S(1)}, bf16[512,256]{1,0:T(8,128)(2,1)S(1)}, u32[]{:S(2)}, u32[]{:S(2)}) collective-permute-start(bf16[512,256]{1,0:T(8,128)(2,1)S(1)} %bitcast.55), channel_id=1, source_target_pairs={{0,128},{1,129},{2,130},{3,131},{4,132},{5,133},{6,134},{7,135},{8... | collective-permute-start | bytes 786440 | tf_op jit(solution)/shard_map/ppermute | solution.py:59
  81.4 2.2 %collective-permute-start.14 = (bf16[512,256]{1,0:T(8,128)(2,1)S(1)}, bf16[512,256]{1,0:T(8,128)(2,1)S(1)}, u32[]{:S(2)}, u32[]{:S(2)}) collective-permute-start(bf16[512,256]{1,0:T(8,128)(2,1)S(1)} %bitcast.56), channel_id=1, source_target_pairs={{0,192},{1,193},{2,194},{3,195},{4,196},{5,197},{6,198},{7,199},{8... | collective-permute-start | bytes 786440 | tf_op jit(solution)/shard_map/ppermute | solution.py:59
  83.6 1.9 fusion.89
  85.5 0.9 fusion.90
  86.4 0.9 fusion.4
  87.3 0.6 fusion.13
  87.8 0.7 copy-done.6
  88.5 0.6 fusion.29
  89.1 8.8 %collective-permute-start.11 = (bf16[2,160,128]{2,1,0:T(8,128)(2,1)S(1)}, bf16[2,160,128]{2,1,0:T(8,128)(2,1)S(1)}, u32[]{:S(2)}, u32[]{:S(2)}) collective-permute-start(bf16[2,160,128]{2,1,0:T(8,128)(2,1)S(1)} %bitcast.58), channel_id=1, source_target_pairs={{0,256},{1,257},{2,258},{3,259},{4,260},{5,261},{6,262},{7,263},{8... | collective-permute-start | bytes 245768 | tf_op jit(solution)/shard_map/ppermute | solution.py:59
  97.9 17.3 %collective-permute-done.11 = bf16[2,160,128]{2,1,0:T(8,128)(2,1)S(1)} collective-permute-done((bf16[2,160,128]{2,1,0:T(8,128)(2,1)S(1)}, bf16[2,160,128]{2,1,0:T(8,128)(2,1)S(1)}, u32[]{:S(2)}, u32[]{:S(2)}) %collective-permute-start.11) | collective-permute-done | bytes 81952 | tf_op jit(solution)/shard_map/ppermute | solution.py:59
  115.4 1.1 pad_maximum_fusion.1
  116.6 2.7 %collective-permute-start.15 = (bf16[4,512,256]{2,1,0:T(8,128)(2,1)}, bf16[4,512,256]{2,1,0:T(8,128)(2,1)S(1)}, u32[]{:S(2)}, u32[]{:S(2)}) collective-permute-start(bf16[4,512,256]{2,1,0:T(8,128)(2,1)} %pad_maximum_fusion.1), channel_id=1, source_target_pairs={{0,32},{1,33},{2,34},{3,35},{4,36},{5,37},{6,38},{7,39},{8,40},{9,... | collective-permute-start | bytes 3145736 | tf_op jit(solution)/shard_map/ppermute | solution.py:59
  119.4 14.7 %all_to_all.25 = bf16[8,2,160,128]{3,2,1,0:T(8,128)(2,1)S(1)} all-to-all(bf16[8,2,160,128]{3,2,1,0:T(8,128)(2,1)S(1)} %bitcast.51), channel_id=1, replica_groups={{0,1,2,3},{4,5,6,7},{8,9,10,11},{12,13,14,15},{16,17,18,19},{20,21,22,2..., dimensions={0} | all-to-all | bytes 1310720 | tf_op jit(solution)/shard_map/all_to_all | solution.py:63
  134.0 0.5 copy.33
  134.5 1.3 reshape.199
  136.0 0.9 copy-done.2
  136.9 0.8 fusion.19
  137.8 13.1 %all_to_all.26 = bf16[4,320,256]{2,1,0:T(8,128)(2,1)S(1)} all-to-all(bf16[4,320,256]{2,1,0:T(8,128)(2,1)S(1)} %fusion.19), channel_id=1, replica_groups={{0,4,8,12},{1,5,9,13},{2,6,10,14},{3,7,11,15},{16,20,24,28},{17,21,25,2..., dimensions={0} | all-to-all | bytes 1310720 | tf_op jit(solution)/shard_map/all_to_all | solution.py:63
  151.1 1.9 collective-permute-start.18
  153.0 6.7 %collective-permute-start.17 = (bf16[160,256]{1,0:T(8,128)(2,1)S(1)}, bf16[160,256]{1,0:T(8,128)(2,1)S(1)}, u32[]{:S(2)}, u32[]{:S(2)}) collective-permute-start(bf16[160,256]{1,0:T(8,128)(2,1)S(1)} %get-tuple-element.49), channel_id=1, source_target_pairs={{0,256},{1,257},{2,258},{3,259},{4,260},{5,261},{6,262},{7,263},{8... | collective-permute-start | bytes 245768 | tf_op jit(solution)/shard_map/ppermute | solution.py:59
  159.7 7.8 %collective-permute-start.16 = (bf16[160,256]{1,0:T(8,128)(2,1)S(1)}, bf16[160,256]{1,0:T(8,128)(2,1)S(1)}, u32[]{:S(2)}, u32[]{:S(2)}) collective-permute-start(bf16[160,256]{1,0:T(8,128)(2,1)S(1)} %get-tuple-element.48), channel_id=1, source_target_pairs={{0,16},{1,17},{2,18},{3,19},{4,20},{5,21},{6,22},{7,23},{8,24},{9,... | collective-permute-start | bytes 245768 | tf_op jit(solution)/shard_map/ppermute | solution.py:59
  167.5 7.5 %collective-permute-done.16 = bf16[160,256]{1,0:T(8,128)(2,1)S(1)} collective-permute-done((bf16[160,256]{1,0:T(8,128)(2,1)S(1)}, bf16[160,256]{1,0:T(8,128)(2,1)S(1)}, u32[]{:S(2)}, u32[]{:S(2)}) %collective-permute-start.16) | collective-permute-done | bytes 81952 | tf_op jit(solution)/shard_map/ppermute | solution.py:59
  175.2 0.4 fusion.22
  175.9 1.2 copy.34
  177.2 3.6 %all-to-all-start.4 = ((bf16[16,160,128]{2,1,0:T(8,128)(2,1)}), bf16[16,160,128]{2,1,0:T(8,128)(2,1)S(1)}, u32[]{:S(2)}, u32[]{:S(2)}) async-start(bf16[16,160,128]{2,1,0:T(8,128)(2,1)} %copy.34), calls=%async_computation.4 | async-start | bytes 1310720 | tf_op jit(solution)/shard_map/all_to_all | solution.py:63
  181.6 8.8 %all-to-all-done.4 = bf16[16,160,128]{2,1,0:T(8,128)(2,1)S(1)} async-done(((bf16[16,160,128]{2,1,0:T(8,128)(2,1)}), bf16[16,160,128]{2,1,0:T(8,128)(2,1)S(1)}, u32[]{:S(2)}, u32[]{:S(2)}) %all-to-all-start.4) | async-done | bytes 655392 | tf_op jit(solution)/shard_map/all_to_all | solution.py:63
  191.1 0.4 fusion.56
  191.6 6.8 %collective-permute-start.19 = (bf16[160,384]{1,0:T(8,128)(2,1)S(1)}, bf16[160,384]{1,0:T(8,128)(2,1)S(1)}, u32[]{:S(2)}, u32[]{:S(2)}) collective-permute-start(bf16[160,384]{1,0:T(8,128)(2,1)S(1)} %pad_maximum_fusion.7), channel_id=1, source_target_pairs={{0,32},{1,33},{2,34},{3,35},{4,36},{5,37},{6,38},{7,39},{8,40},{9,... | collective-permute-start | bytes 368648 | tf_op jit(solution)/shard_map/ppermute | solution.py:59
  198.4 0.9 collective-permute-done.19
  199.3 0.4 convolution_convert_fusion.1
  199.7 0.7 slice.108
  200.4 0.7 copy.37
  (90 shorter events, 3.0 us)
Async XLA Ops:
  2.4 32.4 %collective-permute-start.1 = (bf16[256,256]{1,0:T(8,128)(2,1)S(1)}, bf16[256,256]{1,0:T(8,128)(2,1)S(1)}, u32[]{:S(2)}, u32[]{:S(2)}) collective-permute-start(bf16[256,256]{1,0:T(8,128)(2,1)S(1)} %get-tuple-element.37), channel_id=1, source_target_pairs={{0,64},{1,65},{2,66},{3,67},{4,68},{5,69},{6,70},{7,71},{8,72},{9,... | collective-permute-start | bytes 393224 | tf_op jit(solution)/shard_map/ppermute | solution.py:59
  6.0 29.6 %collective-permute-start.2 = (bf16[256,256]{1,0:T(8,128)(2,1)S(1)}, bf16[256,256]{1,0:T(8,128)(2,1)S(1)}, u32[]{:S(2)}, u32[]{:S(2)}) collective-permute-start(bf16[256,256]{1,0:T(8,128)(2,1)S(1)} %get-tuple-element.37), channel_id=1, source_target_pairs={{0,128},{1,129},{2,130},{3,131},{4,132},{5,133},{6,134},{7,135},{8... | collective-permute-start | bytes 393224 | tf_op jit(solution)/shard_map/ppermute | solution.py:59
  12.1 25.1 %collective-permute-start.3 = (bf16[256,256]{1,0:T(8,128)(2,1)S(1)}, bf16[256,256]{1,0:T(8,128)(2,1)S(1)}, u32[]{:S(2)}, u32[]{:S(2)}) collective-permute-start(bf16[256,256]{1,0:T(8,128)(2,1)S(1)} %get-tuple-element.37), channel_id=1, source_target_pairs={{0,192},{1,193},{2,194},{3,195},{4,196},{5,197},{6,198},{7,199},{8... | collective-permute-start | bytes 393224 | tf_op jit(solution)/shard_map/ppermute | solution.py:59
  16.1 24.0 %collective-permute-start.5 = (bf16[256,256]{1,0:T(8,128)(2,1)}, bf16[256,256]{1,0:T(8,128)(2,1)S(1)}, u32[]{:S(2)}, u32[]{:S(2)}) collective-permute-start(bf16[256,256]{1,0:T(8,128)(2,1)} %get-tuple-element.36), channel_id=1, source_target_pairs={{0,336},{1,337},{2,338},{3,339},{4,340},{5,341},{6,342},{7,343},{8... | collective-permute-start | bytes 393224 | tf_op jit(solution)/shard_map/ppermute | solution.py:59
  18.3 9.9 %collective-permute-start.8 = (bf16[128,512]{1,0:T(8,128)(2,1)S(1)}, bf16[128,512]{1,0:T(8,128)(2,1)}, u32[]{:S(2)}, u32[]{:S(2)}) collective-permute-start(bf16[128,512]{1,0:T(8,128)(2,1)S(1)} %constant_dynamic-slice_fusion.4), channel_id=1, source_target_pairs={{0,32},{1,33},{2,34},{3,35},{4,36},{5,37},{6,38},{7,39},{8,40},{9,... | collective-permute-start | bytes 393224 | tf_op jit(solution)/shard_map/ppermute | solution.py:59
  25.6 2.6 %copy-start.3 = (bf16[256,256]{1,0:T(8,128)(2,1)S(1)}, bf16[256,256]{1,0:T(8,128)(2,1)}, u32[]{:S(2)}) copy-start(bf16[256,256]{1,0:T(8,128)(2,1)} %param.9) | copy-start | bytes 393220
  25.6 2.6 %copy-start.4 = (bf16[256,256]{1,0:T(8,128)(2,1)S(1)}, bf16[256,256]{1,0:T(8,128)(2,1)}, u32[]{:S(2)}) copy-start(bf16[256,256]{1,0:T(8,128)(2,1)} %param.10) | copy-start | bytes 393220
  25.6 3.3 %copy-start.7 = (bf16[256,512]{1,0:T(8,128)(2,1)S(1)}, bf16[256,512]{1,0:T(8,128)(2,1)}, u32[]{:S(2)}) copy-start(bf16[256,512]{1,0:T(8,128)(2,1)} %param.12) | copy-start | bytes 786436
  28.2 11.9 %collective-permute-start.6 = (bf16[256,256]{1,0:T(8,128)(2,1)}, bf16[256,256]{1,0:T(8,128)(2,1)S(1)}, u32[]{:S(2)}, u32[]{:S(2)}) collective-permute-start(bf16[256,256]{1,0:T(8,128)(2,1)} %get-tuple-element.36), channel_id=1, source_target_pairs={{0,400},{1,401},{2,402},{3,403},{4,404},{5,405},{6,406},{7,407},{8... | collective-permute-start | bytes 393224 | tf_op jit(solution)/shard_map/ppermute | solution.py:59
  30.6 10.8 %all-to-all-start = ((bf16[4,128,256]{2,1,0:T(8,128)(2,1)}), bf16[4,128,256]{2,1,0:T(8,128)(2,1)S(1)}, u32[]{:S(2)}, u32[]{:S(2)}) async-start(bf16[4,128,256]{2,1,0:T(8,128)(2,1)} %bitcast.46), calls=%async_computation | async-start | bytes 524288 | tf_op jit(solution)/shard_map/all_to_all | solution.py:63
  34.8 23.3 %collective-permute-start.7 = (bf16[256,256]{1,0:T(8,128)(2,1)}, bf16[256,256]{1,0:T(8,128)(2,1)S(1)}, u32[]{:S(2)}, u32[]{:S(2)}) collective-permute-start(bf16[256,256]{1,0:T(8,128)(2,1)} %get-tuple-element.36), channel_id=1, source_target_pairs={{0,464},{1,465},{2,466},{3,467},{4,468},{5,469},{6,470},{7,471},{8... | collective-permute-start | bytes 393224 | tf_op jit(solution)/shard_map/ppermute | solution.py:59
  35.5 4.6 %collective-permute-start.4 = (bf16[256,256]{1,0:T(8,128)(2,1)}, bf16[256,256]{1,0:T(8,128)(2,1)S(1)}, u32[]{:S(2)}, u32[]{:S(2)}) collective-permute-start(bf16[256,256]{1,0:T(8,128)(2,1)} %get-tuple-element.35), channel_id=1, source_target_pairs={{0,272},{1,273},{2,274},{3,275},{4,276},{5,277},{6,278},{7,279},{8... | collective-permute-start | bytes 393224 | tf_op jit(solution)/shard_map/ppermute | solution.py:59
  37.2 4.0 %collective-permute-start = (bf16[256,640]{1,0:T(8,128)(2,1)S(1)}, bf16[256,640]{1,0:T(8,128)(2,1)S(1)}, u32[]{:S(2)}, u32[]{:S(2)}) collective-permute-start(bf16[256,640]{1,0:T(8,128)(2,1)S(1)} %pad_maximum_fusion.3), channel_id=1, source_target_pairs={{0,32},{1,33},{2,34},{3,35},{4,36},{5,37},{6,38},{7,39},{8,40},{9,... | collective-permute-start | bytes 983048 | tf_op jit(solution)/shard_map/ppermute | solution.py:59
  40.2 1.0 copy-start.5
  41.5 22.6 %all-to-all-start.1 = ((bf16[16,64,512]{2,1,0:T(8,128)(2,1)}), bf16[16,64,512]{2,1,0:T(8,128)(2,1)S(1)}, u32[]{:S(2)}, u32[]{:S(2)}) async-start(bf16[16,64,512]{2,1,0:T(8,128)(2,1)} %reshape.194), calls=%async_computation.1 | async-start | bytes 2097152 | tf_op jit(solution)/shard_map/all_to_all | solution.py:63
  50.2 13.9 %collective-permute-start.9 = (bf16[160,256]{1,0:T(8,128)(2,1)S(1)}, bf16[160,256]{1,0:T(8,128)(2,1)S(1)}, u32[]{:S(2)}, u32[]{:S(2)}) collective-permute-start(bf16[160,256]{1,0:T(8,128)(2,1)S(1)} %get-tuple-element.46), channel_id=1, source_target_pairs={{0,16},{1,17},{2,18},{3,19},{4,20},{5,21},{6,22},{7,23},{8,24},{9,... | collective-permute-start | bytes 245768 | tf_op jit(solution)/shard_map/ppermute | solution.py:59
  64.1 22.3 %copy-start = (bf16[16,64,512]{2,1,0:T(8,128)(2,1)}, bf16[16,64,512]{2,1,0:T(8,128)(2,1)S(1)}, u32[]{:S(2)}) copy-start(bf16[16,64,512]{2,1,0:T(8,128)(2,1)S(1)} %all-to-all-done.1) | copy-start | bytes 3145732
  64.1 21.4 %collective-permute-start.10 = (bf16[2048,256]{1,0:T(8,128)(2,1)}, bf16[2048,256]{1,0:T(8,128)(2,1)S(1)}, u32[]{:S(2)}, u32[]{:S(2)}) collective-permute-start(bf16[2048,256]{1,0:T(8,128)(2,1)} %constant_dynamic-update-slice_fusion), channel_id=1, source_target_pairs={{0,32},{1,33},{2,34},{3,35},{4,36},{5,37},{6,38},{7,39},{8,40},{9,... | collective-permute-start | bytes 3145736 | tf_op jit(solution)/shard_map/ppermute | solution.py:59
  69.0 46.2 %collective-permute-start.12 = (bf16[512,256]{1,0:T(8,128)(2,1)S(1)}, bf16[512,256]{1,0:T(8,128)(2,1)S(1)}, u32[]{:S(2)}, u32[]{:S(2)}) collective-permute-start(bf16[512,256]{1,0:T(8,128)(2,1)S(1)} %bitcast.54), channel_id=1, source_target_pairs={{0,64},{1,65},{2,66},{3,67},{4,68},{5,69},{6,70},{7,71},{8,72},{9,... | collective-permute-start | bytes 786440 | tf_op jit(solution)/shard_map/ppermute | solution.py:59
  73.5 41.7 %collective-permute-start.13 = (bf16[512,256]{1,0:T(8,128)(2,1)S(1)}, bf16[512,256]{1,0:T(8,128)(2,1)S(1)}, u32[]{:S(2)}, u32[]{:S(2)}) collective-permute-start(bf16[512,256]{1,0:T(8,128)(2,1)S(1)} %bitcast.55), channel_id=1, source_target_pairs={{0,128},{1,129},{2,130},{3,131},{4,132},{5,133},{6,134},{7,135},{8... | collective-permute-start | bytes 786440 | tf_op jit(solution)/shard_map/ppermute | solution.py:59
  81.4 33.8 %collective-permute-start.14 = (bf16[512,256]{1,0:T(8,128)(2,1)S(1)}, bf16[512,256]{1,0:T(8,128)(2,1)S(1)}, u32[]{:S(2)}, u32[]{:S(2)}) collective-permute-start(bf16[512,256]{1,0:T(8,128)(2,1)S(1)} %bitcast.56), channel_id=1, source_target_pairs={{0,192},{1,193},{2,194},{3,195},{4,196},{5,197},{6,198},{7,199},{8... | collective-permute-start | bytes 786440 | tf_op jit(solution)/shard_map/ppermute | solution.py:59
  87.3 1.2 copy-start.6
  89.1 26.1 %collective-permute-start.11 = (bf16[2,160,128]{2,1,0:T(8,128)(2,1)S(1)}, bf16[2,160,128]{2,1,0:T(8,128)(2,1)S(1)}, u32[]{:S(2)}, u32[]{:S(2)}) collective-permute-start(bf16[2,160,128]{2,1,0:T(8,128)(2,1)S(1)} %bitcast.58), channel_id=1, source_target_pairs={{0,256},{1,257},{2,258},{3,259},{4,260},{5,261},{6,262},{7,263},{8... | collective-permute-start | bytes 245768 | tf_op jit(solution)/shard_map/ppermute | solution.py:59
  116.6 19.3 %collective-permute-start.15 = (bf16[4,512,256]{2,1,0:T(8,128)(2,1)}, bf16[4,512,256]{2,1,0:T(8,128)(2,1)S(1)}, u32[]{:S(2)}, u32[]{:S(2)}) collective-permute-start(bf16[4,512,256]{2,1,0:T(8,128)(2,1)} %pad_maximum_fusion.1), channel_id=1, source_target_pairs={{0,32},{1,33},{2,34},{3,35},{4,36},{5,37},{6,38},{7,39},{8,40},{9,... | collective-permute-start | bytes 3145736 | tf_op jit(solution)/shard_map/ppermute | solution.py:59
  135.8 1.1 copy-start.2
  137.8 37.4 %copy-start.1 = (bf16[16,64,512]{2,1,0:T(8,128)(2,1)S(1)}, bf16[16,64,512]{2,1,0:T(8,128)(2,1)}, u32[]{:S(2)}) copy-start(bf16[16,64,512]{2,1,0:T(8,128)(2,1)} %copy-done) | copy-start | bytes 3145732
  151.1 16.4 %collective-permute-start.18 = (bf16[160,256]{1,0:T(8,128)(2,1)S(1)}, bf16[160,256]{1,0:T(8,128)(2,1)S(1)}, u32[]{:S(2)}, u32[]{:S(2)}) collective-permute-start(bf16[160,256]{1,0:T(8,128)(2,1)S(1)} %get-tuple-element.49), channel_id=1, source_target_pairs={{0,272},{1,273},{2,274},{3,275},{4,276},{5,277},{6,278},{7,279},{8... | collective-permute-start | bytes 245768 | tf_op jit(solution)/shard_map/ppermute | solution.py:59
  153.0 14.5 %collective-permute-start.17 = (bf16[160,256]{1,0:T(8,128)(2,1)S(1)}, bf16[160,256]{1,0:T(8,128)(2,1)S(1)}, u32[]{:S(2)}, u32[]{:S(2)}) collective-permute-start(bf16[160,256]{1,0:T(8,128)(2,1)S(1)} %get-tuple-element.49), channel_id=1, source_target_pairs={{0,256},{1,257},{2,258},{3,259},{4,260},{5,261},{6,262},{7,263},{8... | collective-permute-start | bytes 245768 | tf_op jit(solution)/shard_map/ppermute | solution.py:59
  159.7 15.3 %collective-permute-start.16 = (bf16[160,256]{1,0:T(8,128)(2,1)S(1)}, bf16[160,256]{1,0:T(8,128)(2,1)S(1)}, u32[]{:S(2)}, u32[]{:S(2)}) collective-permute-start(bf16[160,256]{1,0:T(8,128)(2,1)S(1)} %get-tuple-element.48), channel_id=1, source_target_pairs={{0,16},{1,17},{2,18},{3,19},{4,20},{5,21},{6,22},{7,23},{8,24},{9,... | collective-permute-start | bytes 245768 | tf_op jit(solution)/shard_map/ppermute | solution.py:59
  177.2 13.3 %all-to-all-start.4 = ((bf16[16,160,128]{2,1,0:T(8,128)(2,1)}), bf16[16,160,128]{2,1,0:T(8,128)(2,1)S(1)}, u32[]{:S(2)}, u32[]{:S(2)}) async-start(bf16[16,160,128]{2,1,0:T(8,128)(2,1)} %copy.34), calls=%async_computation.4 | async-start | bytes 1310720 | tf_op jit(solution)/shard_map/all_to_all | solution.py:63
  191.6 7.7 %collective-permute-start.19 = (bf16[160,384]{1,0:T(8,128)(2,1)S(1)}, bf16[160,384]{1,0:T(8,128)(2,1)S(1)}, u32[]{:S(2)}, u32[]{:S(2)}) collective-permute-start(bf16[160,384]{1,0:T(8,128)(2,1)S(1)} %pad_maximum_fusion.7), channel_id=1, source_target_pairs={{0,32},{1,33},{2,34},{3,35},{4,36},{5,37},{6,38},{7,39},{8,40},{9,... | collective-permute-start | bytes 368648 | tf_op jit(solution)/shard_map/ppermute | solution.py:59

commit v3 on v2

v3 whole, which is shorter than its diff:
```python
import itertools
import math

import jax
import jax.numpy as jnp
from jax import lax
from jax.sharding import PartitionSpec as P

D = 8192
HQ = 64
KVH = 8
HD = 128
THETA = 1000000.0
EPS = 1e-06

ZL, CORES, ZH, NX, NY = 8, 2, 2, 4, 4
PAIR_KEEP = 320
OWN = PAIR_KEEP // 2
AXES = ("ctx", "tp")
BF = jnp.bfloat16
F32 = jnp.float32


def pairs(**moves):
    names = ("zh", "zl", "core", "x", "y")
    found = []
    for source in itertools.product(range(ZH), range(ZL), range(CORES), range(NX), range(NY)):
        at = dict(zip(names, source))
        target = {**at, **{name: move(at) for name, move in moves.items()}}
        if target["zl"] < ZL:
            found.append((place(*source), place(**target)))
    return found


def place(zh, zl, core, x, y):
    return (zl * CORES + core) * (ZH * NX * NY) + (zh * NX + x) * NY + y


CORE = pairs(core=lambda at: 1 - at["core"])
FOUR = pairs(zl=lambda at: at["zl"] ^ 4)
NEXT_X = [None] + [pairs(x=lambda at, k=k: (at["x"] + k) % NX) for k in (1, 2, 3)]
NEXT_Y = [None] + [pairs(y=lambda at, k=k: (at["y"] + k) % NY) for k in (1, 2, 3)]
PLANES = [[half * NX * NY + i for i in range(NX * NY)] for half in range(ZH)]
ALONG_Y = [[start * NY + y for y in range(NY)] for start in range(ZH * NX)]
ALONG_X = [[half * NX * NY + x * NY + y for x in range(NX)] for half in range(ZH) for y in range(NY)]
QUADS = [
    [place(zh, quad * 4 + low, core, x, y) for low in range(4) for y in range(NY)]
    for zh in range(ZH)
    for quad in range(2)
    for core in range(CORES)
    for x in range(NX)
]
SETS = [
    [place(zh, zl, core, x, y) for zh in range(ZH) for zl in (low, low + 4)]
    for low in range(4)
    for core in range(CORES)
    for x in range(NX)
    for y in range(NY)
]


def near(zl, k):
    return k < 4 or (k == 4 and zl >= 2)


BACK = [None] + [
    pairs(
        zh=lambda at, k=k: at["zh"] if near(at["zl"], k) else 1 - at["zh"],
        zl=lambda at, k=k: at["zl"] + k,
    )
    for k in range(1, ZL)
]


def send(x, table):
    return lax.ppermute(x, AXES, table)


def exchange(x, groups, axes="tp"):
    return lax.all_to_all(x, axes, 0, 0, tiled=True, axis_index_groups=groups)


def swap(x, me, tables):
    count = len(tables)
    out = [lax.dynamic_index_in_dim(x, (me + k) % count, 0, keepdims=False) for k in range(count)]
    got = jnp.stack([out[0]] + [send(out[k], tables[k]) for k in range(1, count)])
    return jnp.stack(
        [lax.dynamic_index_in_dim(got, (me - k) % count, 0, keepdims=False) for k in range(count)]
    )


def turn(cache_rows, position_ids, first_col):
    column = first_col + jnp.arange(cache_rows.shape[1], dtype=jnp.int32)
    within = column % (2 * HD)
    is_key = within < HD
    exponent = jnp.where(is_key, within - within % 2, 0).astype(F32) / HD
    frequency = jnp.power(F32(THETA), -exponent)
    angles = position_ids[:, None] * frequency[None, :]
    even = (column % 2 == 0)[None, :]
    other = jnp.where(even, -jnp.roll(cache_rows, -1, axis=1), jnp.roll(cache_rows, 1, axis=1))
    turned = cache_rows * jnp.cos(angles) + other * jnp.sin(angles)
    return jnp.where(is_key[None, :], turned, cache_rows)


def shards(
    residual, queries, keys_values, out_weight, norm_gain, cache_weight, positions, keep_rows, kept_count
):
    rows = residual.shape[0]
    ctx = lax.axis_index("ctx")
    tp = lax.axis_index("tp")
    zl, core = ctx // CORES, ctx % CORES
    zh, plane = tp // (NX * NY), tp % (NX * NY)
    x, y = plane // NY, plane % NY
    first = core == 0

    local = jnp.arange(rows, dtype=jnp.int32)
    order = jnp.where(local < kept_count[0], local, -1)
    hits = keep_rows[:, None] == local[None, :]
    rank = jnp.sum(jnp.where(hits, order[:, None], 0), axis=0)
    meta = jnp.stack([rank, positions // 128, positions % 128], axis=1).astype(BF)
    meta = jnp.pad(meta, ((0, 0), (0, 125)))
    mine = jnp.concatenate([queries, residual, meta], axis=1)

    head = zh * (KVH // ZH) + plane // NY
    far_head = (1 - zh) * (KVH // ZH) + plane // NY
    own_kv = lax.dynamic_slice_in_dim(keys_values, head * 2 * HD, 2 * HD, 1)
    far_kv = lax.dynamic_slice_in_dim(keys_values, far_head * 2 * HD, 2 * HD, 1)
    sent = {4: jnp.where(zl >= 2, own_kv, far_kv)}
    blocks = [own_kv] + [send(sent.get(k, own_kv if k < 4 else far_kv), BACK[k]) for k in range(1, ZL)]

    kept_rows = lax.dynamic_slice_in_dim(out_weight, core * HD, HD, 0)
    given_rows = lax.dynamic_slice_in_dim(out_weight, (1 - core) * HD, HD, 0)
    taken_rows = send(given_rows, CORE)
    weight = jnp.concatenate(
        [jnp.where(first, kept_rows, taken_rows), jnp.where(first, taken_rows, kept_rows)], axis=1
    )
    weight = weight.reshape(HD, NY, 256).transpose(1, 0, 2)
    weight = jnp.broadcast_to(weight[None], (4,) + weight.shape).reshape(4 * NY, HD, 256)
    weight, mine = lax.optimization_barrier((weight, mine))
    quad = exchange(weight, QUADS, AXES).reshape(NX, NY * HD, 256)
    theirs = send(mine, CORE)

    pair = jnp.where(first, jnp.concatenate([mine, theirs]), jnp.concatenate([theirs, mine]))
    pair_rank = pair[:, 512].astype(jnp.int32)
    count0 = jnp.sum((pair_rank[:rows] >= 0).astype(jnp.int32))
    pair_row = jnp.arange(2 * rows, dtype=jnp.int32)
    pair_rank = jnp.where(pair_rank >= 0, pair_rank + jnp.where(pair_row >= rows, count0, 0), -1)
    wanted = core * OWN + jnp.arange(OWN, dtype=jnp.int32)
    chosen = wanted[:, None] == pair_rank[None, :]
    picked = jnp.dot(chosen.astype(BF), pair, preferred_element_type=F32)
    token = zl * 2 * rows + jnp.sum(jnp.where(chosen, pair_row[None, :], 0), axis=1)
    position = picked[:, 513] * 128.0 + picked[:, 514]
    query = picked[:, :256].astype(BF).reshape(OWN, 2, HD).transpose(1, 0, 2).reshape(2 * OWN, HD)
    own_residual = picked[:, 256:512].astype(BF)

    kv_mine = jnp.concatenate(lax.optimization_barrier(blocks))
    kv_theirs = send(kv_mine, CORE)
    key_row = jnp.arange(ZL * rows, dtype=jnp.int32)
    key_token = (zl - key_row // rows) * 2 * rows + key_row % rows
    query_token = jnp.concatenate([token, token])

    def scored(kv, offset):
        scores = lax.dot_general(query, kv[:, :HD], (((1,), (1,)), ((), ())), preferred_element_type=F32)
        at = key_token + offset
        visible = (at[None, :] <= query_token[:, None]) & (at >= 0)[None, :]
        return jnp.where(visible, scores * (1.0 / math.sqrt(HD)), -1e30)

    score_a = scored(kv_mine, core * rows)
    score_b = scored(kv_theirs, (1 - core) * rows)
    top = jnp.maximum(jnp.max(score_a, axis=1), jnp.max(score_b, axis=1))[:, None]
    prob_a, prob_b = jnp.exp(score_a - top), jnp.exp(score_b - top)
    total = jnp.sum(prob_a, axis=1) + jnp.sum(prob_b, axis=1)
    mixed = jnp.dot(prob_a.astype(BF), kv_mine[:, HD:], preferred_element_type=F32) + jnp.dot(
        prob_b.astype(BF), kv_theirs[:, HD:], preferred_element_type=F32
    )
    attended = (mixed / total[:, None]).astype(BF)

    attended = attended.reshape(2, OWN, HD)
    attended = jnp.where(first, attended, attended[::-1])
    paired_residual = own_residual.reshape(OWN, 2, HD).transpose(1, 0, 2)
    partner = send(jnp.concatenate([attended, paired_residual]), FOUR)
    partner_residual = jnp.concatenate([partner[2], partner[3]], axis=1)
    partner = partner[:2]
    low = zl < 4
    both = jnp.concatenate([jnp.where(low, attended, partner), jnp.where(low, partner, attended)], axis=1)
    both, cache_weight, quad = lax.optimization_barrier((both, cache_weight, quad))
    quad_other = send(quad, CORE)
    cache_weight, quad_other = lax.optimization_barrier((cache_weight, quad_other))

    columns = cache_weight.shape[1]
    part = D // ZH
    gained = lax.dynamic_slice_in_dim(cache_weight, core * part, part, 0).astype(F32)
    gained = (gained * lax.dynamic_slice_in_dim(norm_gain, core * part, part, 0)[:, None]).astype(BF)
    gained = gained.T.reshape(columns, NX, NY, 256).transpose(1, 2, 0, 3)
    gained = swap(gained, x, NEXT_X).transpose(1, 0, 2, 3)

    heads = exchange(jnp.broadcast_to(both[None], (NY,) + both.shape), ALONG_Y)
    gained = swap(gained, y, NEXT_Y).transpose(1, 0, 2, 3).reshape(NX * NY, columns, 256)
    gained_other = send(gained, CORE)
    terms = 0.0
    for k, block in enumerate((quad, quad_other)):
        side = jnp.concatenate([heads[j, k] for j in range(NY)], axis=1)
        terms = terms + jnp.einsum("rk,ekn->ern", side, block, preferred_element_type=F32)
    terms = terms.astype(BF)
    summed = jnp.sum(exchange(terms, ALONG_X).reshape(NX, 2 * OWN, 256).astype(F32), axis=0)
    rest = jnp.concatenate(
        [jnp.where(low, own_residual, partner_residual), jnp.where(low, partner_residual, own_residual)]
    )
    holds = (zh == 0) == low
    summed = jnp.where(holds, summed + rest.astype(F32), summed).astype(BF).reshape(2, OWN, 256)
    halves = exchange(jnp.concatenate([summed, summed]), SETS, AXES).astype(F32)
    hidden0 = (halves[0] + halves[2]).astype(BF)
    hidden1 = (halves[1] + halves[3]).astype(BF)

    wide0, wide1 = hidden0.astype(F32), hidden1.astype(F32)
    square = jnp.sum(wide0 * wide0 + wide1 * wide1, axis=1, keepdims=True)
    square_high = square.astype(BF)
    square_low = (square - square_high.astype(F32)).astype(BF)
    parts = jnp.einsum(
        "rf,ecf->erc", jnp.where(first, hidden0, hidden1), gained, preferred_element_type=F32
    ) + jnp.einsum(
        "rf,ecf->erc", jnp.where(first, hidden1, hidden0), gained_other, preferred_element_type=F32
    )
    parts = parts.astype(BF)
    tail = jnp.pad(jnp.concatenate([square_high, square_low], axis=1), ((0, 0), (0, 128 - columns - 2)))
    message = jnp.concatenate([parts, jnp.broadcast_to(tail[None], (NX * NY,) + tail.shape)], axis=2)
    gathered = jnp.sum(exchange(message, PLANES).astype(F32), axis=0)
    square_total = gathered[:, columns] + gathered[:, columns + 1]
    cache_rows = gathered[:, :columns] * lax.rsqrt(square_total / D + EPS)[:, None]
    cache_rot = turn(cache_rows, position, tp * columns).astype(BF)

    own_hidden = jnp.where(zh == 0, hidden0, hidden1)
    done = jnp.concatenate([own_hidden, jnp.pad(cache_rot, ((0, 0), (0, 128 - columns)))], axis=1)
    done_other = send(done, CORE)
    kept = jnp.where(first, jnp.concatenate([done, done_other]), jnp.concatenate([done_other, done]))
    own_rank = jnp.where(rank >= 0, rank + jnp.where(first, 0, count0), -1)
    put = own_rank[:, None] == jnp.arange(PAIR_KEEP, dtype=jnp.int32)[None, :]
    output = jnp.dot(put.astype(BF), kept, preferred_element_type=F32).astype(BF)
    return output[:, :256], output[:, 256 : 256 + columns]


def solution(mesh):
    in_specs = (
        P("ctx", "tp"),
        P("ctx", "tp"),
        P("ctx", None),
        P("tp", "ctx"),
        P(),
        P(None, "tp"),
        P("ctx"),
        P("ctx"),
        P("ctx"),
    )
    out_specs = (P("ctx", "tp"), P("ctx", "tp"))
    return jax.shard_map(shards, mesh=mesh, in_specs=in_specs, out_specs=out_specs, check_vma=False)
```

time: 202 us -> 176 us (0.87)
  blocking collectives: 27.8 us -> 0 us
  starting transfers between devices: 99.8 us -> 108 us
  local copies, waits for them, and re-layouts: 13 us -> 8.36 us
    all_to_all x2 -> x0, blocking collectives: 27.8 us -> none  [exchange(): return lax.all_to_all(x, 'tp', 0, 0, tiled=True, axis_index_groups=groups)]
    all_to_all x3 -> x5, starting transfers between devices: 14.6 us -> 29.7 us  [exchange(): return lax.all_to_all(x, axes, 0, 0, tiled=True, axis_index_groups=groups)]
    ppermute x20, waiting for transfers between devices: 31.4 us -> 22.6 us  [send(): return lax.ppermute(x, AXES, table)]
    all_to_all x3 -> x5, waiting for transfers between devices: 8.83 us -> 15.5 us  [exchange(): return lax.all_to_all(x, axes, 0, 0, tiled=True, axis_index_groups=groups)]
    ppermute x20, starting transfers between devices: 85.2 us -> 78.8 us  [send(): return lax.ppermute(x, AXES, table)]
    reshape x3, local copies, waits for them, and re-layouts: 3.53 us -> 0.57 us  [the longest x1 0.38 us: shards(): gained = gained.T.reshape(columns, NX, NY, 256).transpose(1, 2, 0, 3)]
    unnamed x28 -> x16, local copies, waits for them, and re-layouts: 3.92 us -> 1.03 us
  transfers between devices with their start and end apart: 23 -> 25, of which waited for: 6 -> 8; matrix products, arithmetic and copies ran while one was open for 9% -> 9% of each run, Pallas kernels for 0% -> 0%
where the time goes in v3:
time: 176 us; the launch traced here: 175 us
  starting transfers between devices  108 us (61%)
  waiting for transfers between devices  38.2 us (22%)
  other arithmetic  11.2 us (6%)
  local copies, waits for them, and re-layouts  8.36 us (5%)
  matrix products  6.03 us (3%)
  between operations  3.2 us (2%)
    ppermute x20, starting transfers between devices, send(): return lax.ppermute(x, AXES, table)  78.8 us
    all_to_all x5, starting transfers between devices, exchange(): return lax.all_to_all(x, axes, 0, 0, tiled=True, axis_index_groups=groups)  29.7 us
    ppermute x20, waiting for transfers between devices, send(): return lax.ppermute(x, AXES, table)  22.6 us
    all_to_all x5, waiting for transfers between devices, exchange(): return lax.all_to_all(x, axes, 0, 0, tiled=True, axis_index_groups=groups)  15.5 us
  transfers between devices with their start and end apart: 25, of which 8 were waited for; matrix products, arithmetic and copies ran while one was open for 9% of the time, Pallas kernels for 0%

profile of v3, /device:TPU:65, one launch (start us, length us, event | category | flops | bytes accessed | tf_op | source)
XLA Modules:
  0.0 175.4 jit_solution(11483696541640526210)
XLA Ops:
  0.7 1.0 broadcast_select_fusion
  1.7 0.7 collective-permute-start.7
  2.4 10.8 %collective-permute-start.6 = (bf16[256,256]{1,0:T(8,128)(2,1)S(1)}, bf16[256,256]{1,0:T(8,128)(2,1)S(1)}, u32[]{:S(2)}, u32[]{:S(2)}) collective-permute-start(bf16[256,256]{1,0:T(8,128)(2,1)S(1)} %get-tuple-element.50), channel_id=1, source_target_pairs={{0,336},{1,337},{2,338},{3,339},{4,340},{5,341},{6,342},{7,343},{8... | collective-permute-start | bytes 393224 | tf_op jit(solution)/shard_map/ppermute | solution.py:76
  13.2 0.7 collective-permute-start.8
  13.9 0.9 constant_dynamic-slice_fusion.14
  14.9 2.9 %collective-permute-start = (bf16[128,512]{1,0:T(8,128)(2,1)S(1)}, bf16[128,512]{1,0:T(8,128)(2,1)S(1)}, u32[]{:S(2)}, u32[]{:S(2)}) collective-permute-start(bf16[128,512]{1,0:T(8,128)(2,1)S(1)} %constant_dynamic-slice_fusion.14), channel_id=1, source_target_pairs={{0,32},{1,33},{2,34},{3,35},{4,36},{5,37},{6,38},{7,39},{8,40},{9,... | collective-permute-start | bytes 393224 | tf_op jit(solution)/shard_map/ppermute | solution.py:76
  17.7 1.3 collective-permute-start.5
  19.8 0.8 select_reduce_fusion
  20.6 0.7 fusion.97
  21.5 1.0 fusion.35
  22.5 1.3 collective-permute-start.4
  23.8 14.7 %collective-permute-start.3 = (bf16[256,256]{1,0:T(8,128)(2,1)S(1)}, bf16[256,256]{1,0:T(8,128)(2,1)S(1)}, u32[]{:S(2)}, u32[]{:S(2)}) collective-permute-start(bf16[256,256]{1,0:T(8,128)(2,1)S(1)} %get-tuple-element.18), channel_id=1, source_target_pairs={{0,128},{1,129},{2,130},{3,131},{4,132},{5,133},{6,134},{7,135},{8... | collective-permute-start | bytes 393224 | tf_op jit(solution)/shard_map/ppermute | solution.py:76
  38.6 1.9 %collective-permute-start.2 = (bf16[256,256]{1,0:T(8,128)(2,1)S(1)}, bf16[256,256]{1,0:T(8,128)(2,1)S(1)}, u32[]{:S(2)}, u32[]{:S(2)}) collective-permute-start(bf16[256,256]{1,0:T(8,128)(2,1)S(1)} %get-tuple-element.18), channel_id=1, source_target_pairs={{0,64},{1,65},{2,66},{3,67},{4,68},{5,69},{6,70},{7,71},{8,72},{9,... | collective-permute-start | bytes 393224 | tf_op jit(solution)/shard_map/ppermute | solution.py:76
  40.5 1.0 broadcast_select_fusion.2
  41.8 2.5 %collective-permute-done.2 = bf16[256,256]{1,0:T(8,128)(2,1)S(1)} collective-permute-done((bf16[256,256]{1,0:T(8,128)(2,1)S(1)}, bf16[256,256]{1,0:T(8,128)(2,1)S(1)}, u32[]{:S(2)}, u32[]{:S(2)}) %collective-permute-start.2) | collective-permute-done | bytes 131104 | tf_op jit(solution)/shard_map/ppermute | solution.py:76
  44.3 1.1 broadcast_in_dim.68
  45.4 7.4 %all-to-all-start = ((bf16[16,128,256]{2,1,0:T(8,128)(2,1)}), bf16[16,128,256]{2,1,0:T(8,128)(2,1)S(1)}, u32[]{:S(2)}, u32[]{:S(2)}) async-start(bf16[16,128,256]{2,1,0:T(8,128)(2,1)} %bitcast.2), calls=%async_computation | async-start | bytes 2097152 | tf_op jit(solution)/shard_map/all_to_all | solution.py:80
  52.8 4.6 %collective-permute-start.1 = (bf16[256,640]{1,0:T(8,128)(2,1)S(1)}, bf16[256,640]{1,0:T(8,128)(2,1)S(1)}, u32[]{:S(2)}, u32[]{:S(2)}) collective-permute-start(bf16[256,640]{1,0:T(8,128)(2,1)S(1)} %fusion.35), channel_id=1, source_target_pairs={{0,32},{1,33},{2,34},{3,35},{4,36},{5,37},{6,38},{7,39},{8,40},{9,... | collective-permute-start | bytes 983048 | tf_op jit(solution)/shard_map/ppermute | solution.py:76
  57.5 1.9 %collective-permute-start.9 = (bf16[2048,256]{1,0:T(8,128)(2,1)S(1)}, bf16[2048,256]{1,0:T(8,128)(2,1)S(1)}, u32[]{:S(2)}, u32[]{:S(2)}) collective-permute-start(bf16[2048,256]{1,0:T(8,128)(2,1)S(1)} %constant_dynamic-update-slice_fusion), channel_id=1, source_target_pairs={{0,32},{1,33},{2,34},{3,35},{4,36},{5,37},{6,38},{7,39},{8,40},{9,... | collective-permute-start | bytes 3145736 | tf_op jit(solution)/shard_map/ppermute | solution.py:76
  59.5 0.3 maximum_select_fusion
  59.8 0.7 convert_reduce_fusion.2
  60.6 0.7 add_select_fusion.2
  61.2 0.3 fusion.109
  61.9 0.9 fusion.110
  62.8 0.9 fusion.111
  63.7 0.9 fusion.4
  64.6 0.6 fusion.9
  65.1 0.6 fusion.22
  65.8 3.8 %collective-permute-start.10 = (bf16[4,160,128]{2,1,0:T(8,128)(2,1)S(1)}, bf16[4,160,128]{2,1,0:T(8,128)(2,1)S(1)}, u32[]{:S(2)}, u32[]{:S(2)}) collective-permute-start(bf16[4,160,128]{2,1,0:T(8,128)(2,1)S(1)} %pad_maximum_fusion.6), channel_id=1, source_target_pairs={{0,256},{1,257},{2,258},{3,259},{4,260},{5,261},{6,262},{7,263},{8... | collective-permute-start | bytes 491528 | tf_op jit(solution)/shard_map/ppermute | solution.py:76
  69.8 15.0 %collective-permute-done.10 = bf16[4,160,128]{2,1,0:T(8,128)(2,1)S(1)} collective-permute-done((bf16[4,160,128]{2,1,0:T(8,128)(2,1)S(1)}, bf16[4,160,128]{2,1,0:T(8,128)(2,1)S(1)}, u32[]{:S(2)}, u32[]{:S(2)}) %collective-permute-start.10) | collective-permute-done | bytes 163872 | tf_op jit(solution)/shard_map/ppermute | solution.py:76
  84.9 0.9 broadcast_in_dim.109
  85.8 4.0 %all-to-all-start.1 = ((bf16[4,2,320,128]{3,2,1,0:T(8,128)(2,1)}), bf16[4,2,320,128]{3,2,1,0:T(8,128)(2,1)S(1)}, u32[]{:S(2)}, u32[]{:S(2)}) async-start(bf16[4,2,320,128]{3,2,1,0:T(8,128)(2,1)} %broadcast_in_dim.109), calls=%async_computation.1 | async-start | bytes 1310720 | tf_op jit(solution)/shard_map/all_to_all | solution.py:80
  89.8 3.7 %collective-permute-start.11 = (bf16[4,512,256]{2,1,0:T(8,128)(2,1)S(1)}, bf16[4,512,256]{2,1,0:T(8,128)(2,1)S(1)}, u32[]{:S(2)}, u32[]{:S(2)}) collective-permute-start(bf16[4,512,256]{2,1,0:T(8,128)(2,1)S(1)} %bitcast.116), channel_id=1, source_target_pairs={{0,32},{1,33},{2,34},{3,35},{4,36},{5,37},{6,38},{7,39},{8,40},{9,... | collective-permute-start | bytes 3145736 | tf_op jit(solution)/shard_map/ppermute | solution.py:76
  93.6 4.9 %all-to-all-done.1 = bf16[4,2,320,128]{3,2,1,0:T(8,128)(2,1)S(1)} async-done(((bf16[4,2,320,128]{3,2,1,0:T(8,128)(2,1)}), bf16[4,2,320,128]{3,2,1,0:T(8,128)(2,1)S(1)}, u32[]{:S(2)}, u32[]{:S(2)}) %all-to-all-start.1) | async-done | bytes 655392 | tf_op jit(solution)/shard_map/all_to_all | solution.py:80
  98.6 0.5 fusion.36
  99.2 1.4 fusion.14
  100.5 4.0 %all-to-all-start.2 = ((bf16[4,320,256]{2,1,0:T(8,128)(2,1)}), bf16[4,320,256]{2,1,0:T(8,128)(2,1)S(1)}, u32[]{:S(2)}, u32[]{:S(2)}) async-start(bf16[4,320,256]{2,1,0:T(8,128)(2,1)} %fusion.14), calls=%async_computation.2 | async-start | bytes 1310720 | tf_op jit(solution)/shard_map/all_to_all | solution.py:80
  104.6 0.4 reshape.219
  105.2 3.4 %collective-permute-start.12 = (bf16[4,64,256]{2,0,1:T(4,128)(2,1)S(1)}, bf16[4,64,256]{2,0,1:T(4,128)(2,1)S(1)}, u32[]{:S(2)}, u32[]{:S(2)}) collective-permute-start(bf16[4,64,256]{2,0,1:T(4,128)(2,1)S(1)} %get-tuple-element.73), channel_id=1, source_target_pairs={{0,4},{1,5},{2,6},{3,7},{4,8},{5,9},{6,10},{7,11},{8,12},{9,13},{1... | collective-permute-start | bytes 393224 | tf_op jit(solution)/shard_map/ppermute | solution.py:76
  108.6 3.1 %collective-permute-start.14 = (bf16[4,64,256]{2,0,1:T(4,128)(2,1)S(1)}, bf16[4,64,256]{2,0,1:T(4,128)(2,1)S(1)}, u32[]{:S(2)}, u32[]{:S(2)}) collective-permute-start(bf16[4,64,256]{2,0,1:T(4,128)(2,1)S(1)} %get-tuple-element.74), channel_id=1, source_target_pairs={{0,12},{1,13},{2,14},{3,15},{4,0},{5,1},{6,2},{7,3},{8,4},{9,5},{1... | collective-permute-start | bytes 393224 | tf_op jit(solution)/shard_map/ppermute | solution.py:76
  111.7 3.7 %collective-permute-start.13 = (bf16[4,64,256]{2,0,1:T(4,128)(2,1)S(1)}, bf16[4,64,256]{2,0,1:T(4,128)(2,1)S(1)}, u32[]{:S(2)}, u32[]{:S(2)}) collective-permute-start(bf16[4,64,256]{2,0,1:T(4,128)(2,1)S(1)} %get-tuple-element.75), channel_id=1, source_target_pairs={{0,8},{1,9},{2,10},{3,11},{4,12},{5,13},{6,14},{7,15},{8,0},{9,1},... | collective-permute-start | bytes 393224 | tf_op jit(solution)/shard_map/ppermute | solution.py:76
  115.6 0.7 pad_maximum_fusion.4
  116.3 10.6 %all-to-all-start.3 = ((bf16[4,160,256]{2,1,0:T(8,128)(2,1)}), bf16[4,160,256]{2,1,0:T(8,128)(2,1)S(1)}, u32[]{:S(2)}, u32[]{:S(2)}) async-start(bf16[4,160,256]{2,1,0:T(8,128)(2,1)} %pad_maximum_fusion.4), calls=%async_computation.3 | async-start | bytes 655360 | tf_op jit(solution)/shard_map/all_to_all | solution.py:80
  126.9 0.5 pad_maximum_fusion.1
  127.6 0.5 pad_maximum_fusion.2
  128.1 1.1 constant_dynamic-slice_fusion.7
  129.3 2.2 %collective-permute-start.15 = (bf16[4,64,256]{2,1,0:T(8,128)(2,1)S(1)}, bf16[4,64,256]{2,1,0:T(8,128)(2,1)S(1)}, u32[]{:S(2)}, u32[]{:S(2)}) collective-permute-start(bf16[4,64,256]{2,1,0:T(8,128)(2,1)S(1)} %bitcast.129), channel_id=1, source_target_pairs={{0,1},{1,2},{2,3},{3,0},{4,5},{5,6},{6,7},{7,4},{8,9},{9,10},{10,1... | collective-permute-start | bytes 393224 | tf_op jit(solution)/shard_map/ppermute | solution.py:76
  131.5 3.7 %collective-permute-start.16 = (bf16[4,64,256]{2,1,0:T(8,128)(2,1)S(1)}, bf16[4,64,256]{2,1,0:T(8,128)(2,1)S(1)}, u32[]{:S(2)}, u32[]{:S(2)}) collective-permute-start(bf16[4,64,256]{2,1,0:T(8,128)(2,1)S(1)} %bitcast.128), channel_id=1, source_target_pairs={{0,2},{1,3},{2,0},{3,1},{4,6},{5,7},{6,4},{7,5},{8,10},{9,11},{10,... | collective-permute-start | bytes 393224 | tf_op jit(solution)/shard_map/ppermute | solution.py:76
  135.2 2.7 %collective-permute-start.17 = (bf16[4,64,256]{2,1,0:T(8,128)(2,1)S(1)}, bf16[4,64,256]{2,1,0:T(8,128)(2,1)S(1)}, u32[]{:S(2)}, u32[]{:S(2)}) collective-permute-start(bf16[4,64,256]{2,1,0:T(8,128)(2,1)S(1)} %bitcast.127), channel_id=1, source_target_pairs={{0,3},{1,0},{2,1},{3,2},{4,7},{5,4},{6,5},{7,6},{8,11},{9,8},{10,9... | collective-permute-start | bytes 393224 | tf_op jit(solution)/shard_map/ppermute | solution.py:76
  138.0 1.0 collective-permute-done.16
  139.0 2.2 %collective-permute-done.17 = bf16[4,64,256]{2,1,0:T(8,128)(2,1)S(1)} collective-permute-done((bf16[4,64,256]{2,1,0:T(8,128)(2,1)S(1)}, bf16[4,64,256]{2,1,0:T(8,128)(2,1)S(1)}, u32[]{:S(2)}, u32[]{:S(2)}) %collective-permute-start.17) | collective-permute-done | bytes 131104 | tf_op jit(solution)/shard_map/ppermute | solution.py:76
  141.4 7.4 %collective-permute-start.18 = (bf16[16,64,256]{2,1,0:T(8,128)(2,1)S(1)}, bf16[16,64,256]{2,1,0:T(8,128)(2,1)S(1)}, u32[]{:S(2)}, u32[]{:S(2)}) collective-permute-start(bf16[16,64,256]{2,1,0:T(8,128)(2,1)S(1)} %bitcast.118), channel_id=1, source_target_pairs={{0,32},{1,33},{2,34},{3,35},{4,36},{5,37},{6,38},{7,39},{8,40},{9,... | collective-permute-start | bytes 1572872 | tf_op jit(solution)/shard_map/ppermute | solution.py:76
  149.1 0.3 fusion.76
  149.4 0.9 collective-permute-done.18
  150.3 0.3 fusion.15
  150.9 1.2 copy.65
  152.1 3.8 %all-to-all-start.4 = ((bf16[16,160,128]{2,1,0:T(8,128)(2,1)}), bf16[16,160,128]{2,1,0:T(8,128)(2,1)S(1)}, u32[]{:S(2)}, u32[]{:S(2)}) async-start(bf16[16,160,128]{2,1,0:T(8,128)(2,1)} %copy.65), calls=%async_computation.4 | async-start | bytes 1310720 | tf_op jit(solution)/shard_map/all_to_all | solution.py:80
  156.8 10.6 %all-to-all-done.4 = bf16[16,160,128]{2,1,0:T(8,128)(2,1)S(1)} async-done(((bf16[16,160,128]{2,1,0:T(8,128)(2,1)}), bf16[16,160,128]{2,1,0:T(8,128)(2,1)S(1)}, u32[]{:S(2)}, u32[]{:S(2)}) %all-to-all-start.4) | async-done | bytes 655392 | tf_op jit(solution)/shard_map/all_to_all | solution.py:80
  167.9 0.4 fusion.67
  168.4 4.3 %collective-permute-start.19 = (bf16[160,384]{1,0:T(8,128)(2,1)S(1)}, bf16[160,384]{1,0:T(8,128)(2,1)S(1)}, u32[]{:S(2)}, u32[]{:S(2)}) collective-permute-start(bf16[160,384]{1,0:T(8,128)(2,1)S(1)} %pad_maximum_fusion.9), channel_id=1, source_target_pairs={{0,32},{1,33},{2,34},{3,35},{4,36},{5,37},{6,38},{7,39},{8,40},{9,... | collective-permute-start | bytes 368648 | tf_op jit(solution)/shard_map/ppermute | solution.py:76
  172.7 0.9 collective-permute-done.19
  173.7 0.3 convolution_convert_fusion
  174.0 0.7 slice.175
  174.7 0.7 copy.66
  (95 shorter events, 3.5 us)
Async XLA Ops:
  1.7 36.9 %collective-permute-start.7 = (bf16[256,256]{1,0:T(8,128)(2,1)S(1)}, bf16[256,256]{1,0:T(8,128)(2,1)S(1)}, u32[]{:S(2)}, u32[]{:S(2)}) collective-permute-start(bf16[256,256]{1,0:T(8,128)(2,1)S(1)} %get-tuple-element.50), channel_id=1, source_target_pairs={{0,400},{1,401},{2,402},{3,403},{4,404},{5,405},{6,406},{7,407},{8... | collective-permute-start | bytes 393224 | tf_op jit(solution)/shard_map/ppermute | solution.py:76
  2.4 39.3 %collective-permute-start.6 = (bf16[256,256]{1,0:T(8,128)(2,1)S(1)}, bf16[256,256]{1,0:T(8,128)(2,1)S(1)}, u32[]{:S(2)}, u32[]{:S(2)}) collective-permute-start(bf16[256,256]{1,0:T(8,128)(2,1)S(1)} %get-tuple-element.50), channel_id=1, source_target_pairs={{0,336},{1,337},{2,338},{3,339},{4,340},{5,341},{6,342},{7,343},{8... | collective-permute-start | bytes 393224 | tf_op jit(solution)/shard_map/ppermute | solution.py:76
  13.2 28.5 %collective-permute-start.8 = (bf16[256,256]{1,0:T(8,128)(2,1)S(1)}, bf16[256,256]{1,0:T(8,128)(2,1)S(1)}, u32[]{:S(2)}, u32[]{:S(2)}) collective-permute-start(bf16[256,256]{1,0:T(8,128)(2,1)S(1)} %get-tuple-element.50), channel_id=1, source_target_pairs={{0,464},{1,465},{2,466},{3,467},{4,468},{5,469},{6,470},{7,471},{8... | collective-permute-start | bytes 393224 | tf_op jit(solution)/shard_map/ppermute | solution.py:76
  14.9 7.7 %collective-permute-start = (bf16[128,512]{1,0:T(8,128)(2,1)S(1)}, bf16[128,512]{1,0:T(8,128)(2,1)S(1)}, u32[]{:S(2)}, u32[]{:S(2)}) collective-permute-start(bf16[128,512]{1,0:T(8,128)(2,1)S(1)} %constant_dynamic-slice_fusion.14), channel_id=1, source_target_pairs={{0,32},{1,33},{2,34},{3,35},{4,36},{5,37},{6,38},{7,39},{8,40},{9,... | collective-permute-start | bytes 393224 | tf_op jit(solution)/shard_map/ppermute | solution.py:76
  17.7 6.1 %collective-permute-start.5 = (bf16[256,256]{1,0:T(8,128)(2,1)S(1)}, bf16[256,256]{1,0:T(8,128)(2,1)S(1)}, u32[]{:S(2)}, u32[]{:S(2)}) collective-permute-start(bf16[256,256]{1,0:T(8,128)(2,1)S(1)} %get-tuple-element.49), channel_id=1, source_target_pairs={{0,272},{1,273},{2,274},{3,275},{4,276},{5,277},{6,278},{7,279},{8... | collective-permute-start | bytes 393224 | tf_op jit(solution)/shard_map/ppermute | solution.py:76
  22.5 19.2 %collective-permute-start.4 = (bf16[256,256]{1,0:T(8,128)(2,1)S(1)}, bf16[256,256]{1,0:T(8,128)(2,1)S(1)}, u32[]{:S(2)}, u32[]{:S(2)}) collective-permute-start(bf16[256,256]{1,0:T(8,128)(2,1)S(1)} %get-tuple-element.18), channel_id=1, source_target_pairs={{0,192},{1,193},{2,194},{3,195},{4,196},{5,197},{6,198},{7,199},{8... | collective-permute-start | bytes 393224 | tf_op jit(solution)/shard_map/ppermute | solution.py:76
  23.8 17.9 %collective-permute-start.3 = (bf16[256,256]{1,0:T(8,128)(2,1)S(1)}, bf16[256,256]{1,0:T(8,128)(2,1)S(1)}, u32[]{:S(2)}, u32[]{:S(2)}) collective-permute-start(bf16[256,256]{1,0:T(8,128)(2,1)S(1)} %get-tuple-element.18), channel_id=1, source_target_pairs={{0,128},{1,129},{2,130},{3,131},{4,132},{5,133},{6,134},{7,135},{8... | collective-permute-start | bytes 393224 | tf_op jit(solution)/shard_map/ppermute | solution.py:76
  38.6 5.7 %collective-permute-start.2 = (bf16[256,256]{1,0:T(8,128)(2,1)S(1)}, bf16[256,256]{1,0:T(8,128)(2,1)S(1)}, u32[]{:S(2)}, u32[]{:S(2)}) collective-permute-start(bf16[256,256]{1,0:T(8,128)(2,1)S(1)} %get-tuple-element.18), channel_id=1, source_target_pairs={{0,64},{1,65},{2,66},{3,67},{4,68},{5,69},{6,70},{7,71},{8,72},{9,... | collective-permute-start | bytes 393224 | tf_op jit(solution)/shard_map/ppermute | solution.py:76
  45.4 39.5 %all-to-all-start = ((bf16[16,128,256]{2,1,0:T(8,128)(2,1)}), bf16[16,128,256]{2,1,0:T(8,128)(2,1)S(1)}, u32[]{:S(2)}, u32[]{:S(2)}) async-start(bf16[16,128,256]{2,1,0:T(8,128)(2,1)} %bitcast.2), calls=%async_computation | async-start | bytes 2097152 | tf_op jit(solution)/shard_map/all_to_all | solution.py:80
  52.8 6.7 %collective-permute-start.1 = (bf16[256,640]{1,0:T(8,128)(2,1)S(1)}, bf16[256,640]{1,0:T(8,128)(2,1)S(1)}, u32[]{:S(2)}, u32[]{:S(2)}) collective-permute-start(bf16[256,640]{1,0:T(8,128)(2,1)S(1)} %fusion.35), channel_id=1, source_target_pairs={{0,32},{1,33},{2,34},{3,35},{4,36},{5,37},{6,38},{7,39},{8,40},{9,... | collective-permute-start | bytes 983048 | tf_op jit(solution)/shard_map/ppermute | solution.py:76
  57.5 5.3 %collective-permute-start.9 = (bf16[2048,256]{1,0:T(8,128)(2,1)S(1)}, bf16[2048,256]{1,0:T(8,128)(2,1)S(1)}, u32[]{:S(2)}, u32[]{:S(2)}) collective-permute-start(bf16[2048,256]{1,0:T(8,128)(2,1)S(1)} %constant_dynamic-update-slice_fusion), channel_id=1, source_target_pairs={{0,32},{1,33},{2,34},{3,35},{4,36},{5,37},{6,38},{7,39},{8,40},{9,... | collective-permute-start | bytes 3145736 | tf_op jit(solution)/shard_map/ppermute | solution.py:76
  65.8 19.1 %collective-permute-start.10 = (bf16[4,160,128]{2,1,0:T(8,128)(2,1)S(1)}, bf16[4,160,128]{2,1,0:T(8,128)(2,1)S(1)}, u32[]{:S(2)}, u32[]{:S(2)}) collective-permute-start(bf16[4,160,128]{2,1,0:T(8,128)(2,1)S(1)} %pad_maximum_fusion.6), channel_id=1, source_target_pairs={{0,256},{1,257},{2,258},{3,259},{4,260},{5,261},{6,262},{7,263},{8... | collective-permute-start | bytes 491528 | tf_op jit(solution)/shard_map/ppermute | solution.py:76
  85.8 12.7 %all-to-all-start.1 = ((bf16[4,2,320,128]{3,2,1,0:T(8,128)(2,1)}), bf16[4,2,320,128]{3,2,1,0:T(8,128)(2,1)S(1)}, u32[]{:S(2)}, u32[]{:S(2)}) async-start(bf16[4,2,320,128]{3,2,1,0:T(8,128)(2,1)} %broadcast_in_dim.109), calls=%async_computation.1 | async-start | bytes 1310720 | tf_op jit(solution)/shard_map/all_to_all | solution.py:80
  89.8 9.3 %collective-permute-start.11 = (bf16[4,512,256]{2,1,0:T(8,128)(2,1)S(1)}, bf16[4,512,256]{2,1,0:T(8,128)(2,1)S(1)}, u32[]{:S(2)}, u32[]{:S(2)}) collective-permute-start(bf16[4,512,256]{2,1,0:T(8,128)(2,1)S(1)} %bitcast.116), channel_id=1, source_target_pairs={{0,32},{1,33},{2,34},{3,35},{4,36},{5,37},{6,38},{7,39},{8,40},{9,... | collective-permute-start | bytes 3145736 | tf_op jit(solution)/shard_map/ppermute | solution.py:76
  99.1 5.4 %dynamic-slice-start = ((f32[8192]{0:T(1024)}, s32[]{:T(128)}), f32[4096]{0:T(1024)S(1)}, s32[]{:S(2)}) async-start(f32[8192]{0:T(1024)} %param.13, s32[]{:T(128)} %select_n.434), calls=%async_computation.5 | async-start | bytes 33280 | tf_op jit(solution)/shard_map/dynamic_slice | solution.py:193
  99.2 5.4 %copy-start = (bf16[8192,64]{0,1:T(8,128)(2,1)S(1)}, bf16[8192,64]{0,1:T(8,128)(2,1)}, u32[]{:S(2)}) copy-start(bf16[8192,64]{0,1:T(8,128)(2,1)} %param.14) | copy-start | bytes 3145732
  100.5 14.9 %all-to-all-start.2 = ((bf16[4,320,256]{2,1,0:T(8,128)(2,1)}), bf16[4,320,256]{2,1,0:T(8,128)(2,1)S(1)}, u32[]{:S(2)}, u32[]{:S(2)}) async-start(bf16[4,320,256]{2,1,0:T(8,128)(2,1)} %fusion.14), calls=%async_computation.2 | async-start | bytes 1310720 | tf_op jit(solution)/shard_map/all_to_all | solution.py:80
  105.2 21.7 %collective-permute-start.12 = (bf16[4,64,256]{2,0,1:T(4,128)(2,1)S(1)}, bf16[4,64,256]{2,0,1:T(4,128)(2,1)S(1)}, u32[]{:S(2)}, u32[]{:S(2)}) collective-permute-start(bf16[4,64,256]{2,0,1:T(4,128)(2,1)S(1)} %get-tuple-element.73), channel_id=1, source_target_pairs={{0,4},{1,5},{2,6},{3,7},{4,8},{5,9},{6,10},{7,11},{8,12},{9,13},{1... | collective-permute-start | bytes 393224 | tf_op jit(solution)/shard_map/ppermute | solution.py:76
  108.6 18.3 %collective-permute-start.14 = (bf16[4,64,256]{2,0,1:T(4,128)(2,1)S(1)}, bf16[4,64,256]{2,0,1:T(4,128)(2,1)S(1)}, u32[]{:S(2)}, u32[]{:S(2)}) collective-permute-start(bf16[4,64,256]{2,0,1:T(4,128)(2,1)S(1)} %get-tuple-element.74), channel_id=1, source_target_pairs={{0,12},{1,13},{2,14},{3,15},{4,0},{5,1},{6,2},{7,3},{8,4},{9,5},{1... | collective-permute-start | bytes 393224 | tf_op jit(solution)/shard_map/ppermute | solution.py:76
  111.7 15.2 %collective-permute-start.13 = (bf16[4,64,256]{2,0,1:T(4,128)(2,1)S(1)}, bf16[4,64,256]{2,0,1:T(4,128)(2,1)S(1)}, u32[]{:S(2)}, u32[]{:S(2)}) collective-permute-start(bf16[4,64,256]{2,0,1:T(4,128)(2,1)S(1)} %get-tuple-element.75), channel_id=1, source_target_pairs={{0,8},{1,9},{2,10},{3,11},{4,12},{5,13},{6,14},{7,15},{8,0},{9,1},... | collective-permute-start | bytes 393224 | tf_op jit(solution)/shard_map/ppermute | solution.py:76
  116.3 32.5 %all-to-all-start.3 = ((bf16[4,160,256]{2,1,0:T(8,128)(2,1)}), bf16[4,160,256]{2,1,0:T(8,128)(2,1)S(1)}, u32[]{:S(2)}, u32[]{:S(2)}) async-start(bf16[4,160,256]{2,1,0:T(8,128)(2,1)} %pad_maximum_fusion.4), calls=%async_computation.3 | async-start | bytes 655360 | tf_op jit(solution)/shard_map/all_to_all | solution.py:80
  129.3 8.7 %collective-permute-start.15 = (bf16[4,64,256]{2,1,0:T(8,128)(2,1)S(1)}, bf16[4,64,256]{2,1,0:T(8,128)(2,1)S(1)}, u32[]{:S(2)}, u32[]{:S(2)}) collective-permute-start(bf16[4,64,256]{2,1,0:T(8,128)(2,1)S(1)} %bitcast.129), channel_id=1, source_target_pairs={{0,1},{1,2},{2,3},{3,0},{4,5},{5,6},{6,7},{7,4},{8,9},{9,10},{10,1... | collective-permute-start | bytes 393224 | tf_op jit(solution)/shard_map/ppermute | solution.py:76
  131.5 7.5 %collective-permute-start.16 = (bf16[4,64,256]{2,1,0:T(8,128)(2,1)S(1)}, bf16[4,64,256]{2,1,0:T(8,128)(2,1)S(1)}, u32[]{:S(2)}, u32[]{:S(2)}) collective-permute-start(bf16[4,64,256]{2,1,0:T(8,128)(2,1)S(1)} %bitcast.128), channel_id=1, source_target_pairs={{0,2},{1,3},{2,0},{3,1},{4,6},{5,7},{6,4},{7,5},{8,10},{9,11},{10,... | collective-permute-start | bytes 393224 | tf_op jit(solution)/shard_map/ppermute | solution.py:76
  135.2 6.0 %collective-permute-start.17 = (bf16[4,64,256]{2,1,0:T(8,128)(2,1)S(1)}, bf16[4,64,256]{2,1,0:T(8,128)(2,1)S(1)}, u32[]{:S(2)}, u32[]{:S(2)}) collective-permute-start(bf16[4,64,256]{2,1,0:T(8,128)(2,1)S(1)} %bitcast.127), channel_id=1, source_target_pairs={{0,3},{1,0},{2,1},{3,2},{4,7},{5,4},{6,5},{7,6},{8,11},{9,8},{10,9... | collective-permute-start | bytes 393224 | tf_op jit(solution)/shard_map/ppermute | solution.py:76
  141.4 8.9 %collective-permute-start.18 = (bf16[16,64,256]{2,1,0:T(8,128)(2,1)S(1)}, bf16[16,64,256]{2,1,0:T(8,128)(2,1)S(1)}, u32[]{:S(2)}, u32[]{:S(2)}) collective-permute-start(bf16[16,64,256]{2,1,0:T(8,128)(2,1)S(1)} %bitcast.118), channel_id=1, source_target_pairs={{0,32},{1,33},{2,34},{3,35},{4,36},{5,37},{6,38},{7,39},{8,40},{9,... | collective-permute-start | bytes 1572872 | tf_op jit(solution)/shard_map/ppermute | solution.py:76
  152.1 15.2 %all-to-all-start.4 = ((bf16[16,160,128]{2,1,0:T(8,128)(2,1)}), bf16[16,160,128]{2,1,0:T(8,128)(2,1)S(1)}, u32[]{:S(2)}, u32[]{:S(2)}) async-start(bf16[16,160,128]{2,1,0:T(8,128)(2,1)} %copy.65), calls=%async_computation.4 | async-start | bytes 1310720 | tf_op jit(solution)/shard_map/all_to_all | solution.py:80
  168.4 5.3 %collective-permute-start.19 = (bf16[160,384]{1,0:T(8,128)(2,1)S(1)}, bf16[160,384]{1,0:T(8,128)(2,1)S(1)}, u32[]{:S(2)}, u32[]{:S(2)}) collective-permute-start(bf16[160,384]{1,0:T(8,128)(2,1)S(1)} %pad_maximum_fusion.9), channel_id=1, source_target_pairs={{0,32},{1,33},{2,34},{3,35},{4,36},{5,37},{6,38},{7,39},{8,40},{9,... | collective-permute-start | bytes 368648 | tf_op jit(solution)/shard_map/ppermute | solution.py:76

commit v4 on v3

--- a/solution.py
+++ b/solution.py
@@ -1,9 +1,12 @@
+import functools
 import itertools
 import math
 
 import jax
 import jax.numpy as jnp
 from jax import lax
+from jax.experimental import pallas as pl
+from jax.experimental.pallas import tpu as pltpu
 from jax.sharding import PartitionSpec as P
 
 D = 8192
@@ -89,6 +92,81 @@
     )
 
 
+def attend_kernel(place_ref, query_ref, token_ref, *refs):
+    own_ref, quarters = refs[0], refs[1 : 1 + NY]
+    out_ref, scores_ref, top_ref, total_ref, sum_ref = refs[1 + NY :]
+    zl, core = place_ref[0], place_ref[1]
+    scale = 1.0 / math.sqrt(HD)
+    groups = [pl.ds(group * OWN, OWN) for group in range(4)]
+    top_ref[...] = jnp.full(top_ref.shape, -1e29, F32)
+    total_ref[...] = jnp.zeros(total_ref.shape, F32)
+    sum_ref[...] = jnp.zeros(sum_ref.shape, F32)
+
+    def block(k, columns):
+        if k == 0:
+            return own_ref[:, columns]
+        return jnp.concatenate([quarter[k - 1, :, columns] for quarter in quarters])
+
+    def score(k):
+        key = block(k, pl.ds(0, HD))
+        for here in groups:
+            scores = lax.dot_general(
+                query_ref[here, :], key, (((1,), (1,)), ((), ())), preferred_element_type=F32
+            )
+            if k == 0:
+                at = core * scores.shape[1] + lax.broadcasted_iota(jnp.int32, scores.shape, 1)
+                scores = jnp.where(at <= token_ref[here, :], scores, -1e30)
+            scores_ref[k, here, :] = scores
+            top = jnp.maximum(scores[:, :HD], scores[:, HD:])
+            top_ref[here, :] = jnp.maximum(top_ref[here, :], top)
+
+    def add(k):
+        value = block(k, pl.ds(HD, HD))
+        for here in groups:
+            top = top_ref[here, :]
+            scores = scores_ref[k, here, :]
+            low, high = jnp.exp((scores[:, :HD] - top) * scale), jnp.exp((scores[:, HD:] - top) * scale)
+            total_ref[here, :] = total_ref[here, :] + (low + high)
+            probs = jnp.concatenate([low.astype(BF), high.astype(BF)], axis=1)
+            sum_ref[here, :] = sum_ref[here, :] + jnp.dot(probs, value, preferred_element_type=F32)
+
+    score(0)
+    for k in range(1, ZL):
+        pl.when(zl >= k)(functools.partial(score, k))
+    for here in groups:
+        top = jnp.max(top_ref[here, :], axis=1, keepdims=True)
+        top_ref[here, :] = jnp.broadcast_to(top, (OWN, HD))
+    add(0)
+    for k in range(1, ZL):
+        pl.when(zl >= k)(functools.partial(add, k))
+
+    lane = lax.broadcasted_iota(jnp.int32, (OWN, HD), 1)
+    for side in range(2):
+        for head in range(2):
+            here = groups[side * 2 + head]
+            total = jnp.sum(total_ref[here, :], axis=1, keepdims=True)
+            out_ref[side, head] = sum_ref[here, :]
+            out_ref[side, 2 + head] = jnp.where(lane == 0, top_ref[here, :] * scale, total)
+
+
+def attend(where, query, token, own, quarters):
+    whole = pl.BlockSpec(memory_space=pltpu.VMEM)
+    rows = query.shape[0]
+    return pl.pallas_call(
+        attend_kernel,
+        out_shape=jax.ShapeDtypeStruct((2, 4, OWN, HD), F32),
+        in_specs=[pl.BlockSpec(memory_space=pltpu.SMEM)] + [whole] * (3 + len(quarters)),
+        out_specs=whole,
+        scratch_shapes=[
+            pltpu.VMEM((ZL, rows, own.shape[0]), F32),
+            pltpu.VMEM((rows, HD), F32),
+            pltpu.VMEM((rows, HD), F32),
+            pltpu.VMEM((rows, HD), F32),
+        ],
+        compiler_params=pltpu.CompilerParams(vmem_limit_bytes=32 * 1024 * 1024),
+    )(where, query, token, own, *quarters)
+
+
 def turn(cache_rows, position_ids, first_col):
     column = first_col + jnp.arange(cache_rows.shape[1], dtype=jnp.int32)
     within = column % (2 * HD)
@@ -125,8 +203,13 @@
     far_head = (1 - zh) * (KVH // ZH) + plane // NY
     own_kv = lax.dynamic_slice_in_dim(keys_values, head * 2 * HD, 2 * HD, 1)
     far_kv = lax.dynamic_slice_in_dim(keys_values, far_head * 2 * HD, 2 * HD, 1)
-    sent = {4: jnp.where(zl >= 2, own_kv, far_kv)}
-    blocks = [own_kv] + [send(sent.get(k, own_kv if k < 4 else far_kv), BACK[k]) for k in range(1, ZL)]
+    quarter = rows // NY
+    near_kv = lax.dynamic_slice_in_dim(own_kv, y * quarter, quarter, 0)
+    far_kv = lax.dynamic_slice_in_dim(far_kv, y * quarter, quarter, 0)
+    sent = {4: jnp.where(zl >= 2, near_kv, far_kv)}
+    blocks = [send(sent.get(k, near_kv if k < 4 else far_kv), BACK[k]) for k in range(1, ZL)]
+    quarters = jnp.stack(blocks)
+    quarters = [quarters] + [send(quarters, NEXT_Y[k]) for k in (1, 2, 3)]
 
     kept_rows = lax.dynamic_slice_in_dim(out_weight, core * HD, HD, 0)
     given_rows = lax.dynamic_slice_in_dim(out_weight, (1 - core) * HD, HD, 0)
@@ -136,46 +219,33 @@
     )
     weight = weight.reshape(HD, NY, 256).transpose(1, 0, 2)
     weight = jnp.broadcast_to(weight[None], (4,) + weight.shape).reshape(4 * NY, HD, 256)
-    weight, mine = lax.optimization_barrier((weight, mine))
+    theirs = send(mine, CORE)
+    weight, theirs, _ = lax.optimization_barrier((weight, theirs, blocks))
     quad = exchange(weight, QUADS, AXES).reshape(NX, NY * HD, 256)
-    theirs = send(mine, CORE)
 
     pair = jnp.where(first, jnp.concatenate([mine, theirs]), jnp.concatenate([theirs, mine]))
     pair_rank = pair[:, 512].astype(jnp.int32)
     count0 = jnp.sum((pair_rank[:rows] >= 0).astype(jnp.int32))
     pair_row = jnp.arange(2 * rows, dtype=jnp.int32)
     pair_rank = jnp.where(pair_rank >= 0, pair_rank + jnp.where(pair_row >= rows, count0, 0), -1)
-    wanted = core * OWN + jnp.arange(OWN, dtype=jnp.int32)
+    wanted = jnp.arange(OWN, dtype=jnp.int32)
+    wanted = jnp.concatenate([core * OWN + wanted, (1 - core) * OWN + wanted])
     chosen = wanted[:, None] == pair_rank[None, :]
     picked = jnp.dot(chosen.astype(BF), pair, preferred_element_type=F32)
-    token = zl * 2 * rows + jnp.sum(jnp.where(chosen, pair_row[None, :], 0), axis=1)
-    position = picked[:, 513] * 128.0 + picked[:, 514]
-    query = picked[:, :256].astype(BF).reshape(OWN, 2, HD).transpose(1, 0, 2).reshape(2 * OWN, HD)
-    own_residual = picked[:, 256:512].astype(BF)
-
-    kv_mine = jnp.concatenate(lax.optimization_barrier(blocks))
-    kv_theirs = send(kv_mine, CORE)
-    key_row = jnp.arange(ZL * rows, dtype=jnp.int32)
-    key_token = (zl - key_row // rows) * 2 * rows + key_row % rows
-    query_token = jnp.concatenate([token, token])
-
-    def scored(kv, offset):
-        scores = lax.dot_general(query, kv[:, :HD], (((1,), (1,)), ((), ())), preferred_element_type=F32)
-        at = key_token + offset
-        visible = (at[None, :] <= query_token[:, None]) & (at >= 0)[None, :]
-        return jnp.where(visible, scores * (1.0 / math.sqrt(HD)), -1e30)
-
-    score_a = scored(kv_mine, core * rows)
-    score_b = scored(kv_theirs, (1 - core) * rows)
-    top = jnp.maximum(jnp.max(score_a, axis=1), jnp.max(score_b, axis=1))[:, None]
-    prob_a, prob_b = jnp.exp(score_a - top), jnp.exp(score_b - top)
-    total = jnp.sum(prob_a, axis=1) + jnp.sum(prob_b, axis=1)
-    mixed = jnp.dot(prob_a.astype(BF), kv_mine[:, HD:], preferred_element_type=F32) + jnp.dot(
-        prob_b.astype(BF), kv_theirs[:, HD:], preferred_element_type=F32
-    )
-    attended = (mixed / total[:, None]).astype(BF)
-
-    attended = attended.reshape(2, OWN, HD)
+    token = jnp.sum(jnp.where(chosen, pair_row[None, :], 0), axis=1)
+    position = picked[:OWN, 513] * 128.0 + picked[:OWN, 514]
+    query = picked[:, :256].astype(BF).reshape(2, OWN, 2, HD).transpose(0, 2, 1, 3).reshape(4 * OWN, HD)
+    own_residual = picked[:OWN, 256:512].astype(BF)
+
+    token = jnp.broadcast_to(token.reshape(2, 1, OWN), (2, 2, OWN)).reshape(4 * OWN, 1)
+    parts = attend(jnp.stack([zl, core]).astype(jnp.int32), query, token, own_kv, quarters)
+    kept_part, taken_part = parts[0], send(parts[1], CORE)
+    top_a, top_b = kept_part[2:, :, :1], taken_part[2:, :, :1]
+    top = jnp.maximum(top_a, top_b)
+    fade_a, fade_b = jnp.exp(top_a - top), jnp.exp(top_b - top)
+    total = kept_part[2:, :, 1:2] * fade_a + taken_part[2:, :, 1:2] * fade_b
+    attended = ((kept_part[:2] * fade_a + taken_part[:2] * fade_b) / total).astype(BF)
+
     attended = jnp.where(first, attended, attended[::-1])
     paired_residual = own_residual.reshape(OWN, 2, HD).transpose(1, 0, 2)
     partner = send(jnp.concatenate([attended, paired_residual]), FOUR)

time: 176 us -> 188 us (1.068)
  the two profiles are of different devices: /device:TPU:65 before, /device:TPU:1 now
where the time goes in v4:
time: 188 us; the launch traced here: 187 us
  starting transfers between devices  107 us (57%)
  waiting for transfers between devices  48.9 us (26%)
  other arithmetic  11.1 us (6%)
  local copies, waits for them, and re-layouts  9.7 us (5%)
  matrix products  5.43 us (3%)
  between operations  3.22 us (2%)
    ppermute x23, starting transfers between devices, send(): return lax.ppermute(x, AXES, table)  85.8 us
    ppermute x23, waiting for transfers between devices, send(): return lax.ppermute(x, AXES, table)  32.7 us
    all_to_all x5, starting transfers between devices, exchange(): return lax.all_to_all(x, axes, 0, 0, tiled=True, axis_index_groups=groups)  21.5 us
    all_to_all x5, waiting for transfers between devices, exchange(): return lax.all_to_all(x, axes, 0, 0, tiled=True, axis_index_groups=groups)  16.2 us
  transfers between devices with their start and end apart: 28, of which 12 were waited for; matrix products, arithmetic and copies ran while one was open for 9% of the time, Pallas kernels for 1%

profile of v4, /device:TPU:1, one launch (start us, length us, event | category | flops | bytes accessed | tf_op | source)
XLA Modules:
  0.0 186.9 jit_solution(15059969561586961824)
XLA Ops:
  0.7 1.0 broadcast_select_fusion.6
  1.7 4.4 %collective-permute-start.2 = (bf16[64,256]{1,0:T(8,128)(2,1)S(1)}, bf16[64,256]{1,0:T(8,128)(2,1)S(1)}, u32[]{:S(2)}, u32[]{:S(2)}) collective-permute-start(bf16[64,256]{1,0:T(8,128)(2,1)S(1)} %get-tuple-element.36), channel_id=1, source_target_pairs={{0,64},{1,65},{2,66},{3,67},{4,68},{5,69},{6,70},{7,71},{8,72},{9,... | collective-permute-start | bytes 98312 | tf_op jit(solution)/shard_map/ppermute | solution.py:79
  6.1 4.9 %collective-permute-start.3 = (bf16[64,256]{1,0:T(8,128)(2,1)S(1)}, bf16[64,256]{1,0:T(8,128)(2,1)S(1)}, u32[]{:S(2)}, u32[]{:S(2)}) collective-permute-start(bf16[64,256]{1,0:T(8,128)(2,1)S(1)} %get-tuple-element.36), channel_id=1, source_target_pairs={{0,128},{1,129},{2,130},{3,131},{4,132},{5,133},{6,134},{7,135},{8... | collective-permute-start | bytes 98312 | tf_op jit(solution)/shard_map/ppermute | solution.py:79
  11.0 7.5 %collective-permute-start.4 = (bf16[64,256]{1,0:T(8,128)(2,1)S(1)}, bf16[64,256]{1,0:T(8,128)(2,1)S(1)}, u32[]{:S(2)}, u32[]{:S(2)}) collective-permute-start(bf16[64,256]{1,0:T(8,128)(2,1)S(1)} %get-tuple-element.36), channel_id=1, source_target_pairs={{0,192},{1,193},{2,194},{3,195},{4,196},{5,197},{6,198},{7,199},{8... | collective-permute-start | bytes 98312 | tf_op jit(solution)/shard_map/ppermute | solution.py:79
  18.5 2.0 %collective-permute-start.6 = (bf16[64,256]{1,0:T(8,128)(2,1)S(1)}, bf16[64,256]{1,0:T(8,128)(2,1)S(1)}, u32[]{:S(2)}, u32[]{:S(2)}) collective-permute-start(bf16[64,256]{1,0:T(8,128)(2,1)S(1)} %get-tuple-element.35), channel_id=1, source_target_pairs={{0,336},{1,337},{2,338},{3,339},{4,340},{5,341},{6,342},{7,343},{8... | collective-permute-start | bytes 98312 | tf_op jit(solution)/shard_map/ppermute | solution.py:79
  20.4 1.3 collective-permute-start.7
  21.7 0.9 constant_dynamic-slice_fusion.12.refs_0_
  22.7 0.7 fusion.70
  24.0 0.8 select_reduce_fusion
  25.1 0.9 constant_dynamic-slice_fusion.13
  26.1 1.0 pad_maximum_fusion.4
  27.2 1.3 collective-permute-start.8
  28.5 3.1 %collective-permute-start = (bf16[128,512]{1,0:T(8,128)(2,1)S(1)}, bf16[128,512]{1,0:T(8,128)(2,1)S(1)}, u32[]{:S(2)}, u32[]{:S(2)}) collective-permute-start(bf16[128,512]{1,0:T(8,128)(2,1)S(1)} %constant_dynamic-slice_fusion.13), channel_id=1, source_target_pairs={{0,32},{1,33},{2,34},{3,35},{4,36},{5,37},{6,38},{7,39},{8,40},{9,... | collective-permute-start | bytes 393224 | tf_op jit(solution)/shard_map/ppermute | solution.py:79
  31.7 1.9 %collective-permute-start.1 = (bf16[256,640]{1,0:T(8,128)(2,1)S(1)}, bf16[256,640]{1,0:T(8,128)(2,1)S(1)}, u32[]{:S(2)}, u32[]{:S(2)}) collective-permute-start(bf16[256,640]{1,0:T(8,128)(2,1)S(1)} %pad_maximum_fusion.4), channel_id=1, source_target_pairs={{0,32},{1,33},{2,34},{3,35},{4,36},{5,37},{6,38},{7,39},{8,40},{9,... | collective-permute-start | bytes 983048 | tf_op jit(solution)/shard_map/ppermute | solution.py:79
  33.6 1.7 collective-permute-start.5
  35.6 0.8 collective-permute-done.5
  36.5 1.1 broadcast_in_dim.97
  37.6 4.4 %all-to-all-start = ((bf16[16,128,256]{2,1,0:T(8,128)(2,1)}), bf16[16,128,256]{2,1,0:T(8,128)(2,1)S(1)}, u32[]{:S(2)}, u32[]{:S(2)}) async-start(bf16[16,128,256]{2,1,0:T(8,128)(2,1)} %bitcast.2), calls=%async_computation | async-start | bytes 2097152 | tf_op jit(solution)/shard_map/all_to_all | solution.py:83
  42.0 3.3 %collective-permute-start.9 = (bf16[7,64,256]{2,1,0:T(8,128)(2,1)S(1)}, bf16[7,64,256]{2,1,0:T(8,128)(2,1)S(1)}, u32[]{:S(2)}, u32[]{:S(2)}) collective-permute-start(bf16[7,64,256]{2,1,0:T(8,128)(2,1)S(1)} %bitcast_dynamic-update-slice_fusion.refs_1_), channel_id=1, source_target_pairs={{0,1},{1,2},{2,3},{3,0},{4,5},{5,6},{6,7},{7,4},{8,9},{9,10},{10,1... | collective-permute-start | bytes 688136 | tf_op jit(solution)/shard_map/ppermute | solution.py:79
  45.3 4.3 %collective-permute-start.10 = (bf16[7,64,256]{2,1,0:T(8,128)(2,1)S(1)}, bf16[7,64,256]{2,1,0:T(8,128)(2,1)S(1)}, u32[]{:S(2)}, u32[]{:S(2)}) collective-permute-start(bf16[7,64,256]{2,1,0:T(8,128)(2,1)S(1)} %bitcast_dynamic-update-slice_fusion.refs_1_), channel_id=1, source_target_pairs={{0,2},{1,3},{2,0},{3,1},{4,6},{5,7},{6,4},{7,5},{8,10},{9,11},{10,... | collective-permute-start | bytes 688136 | tf_op jit(solution)/shard_map/ppermute | solution.py:79
  49.6 3.1 %collective-permute-start.11 = (bf16[7,64,256]{2,1,0:T(8,128)(2,1)S(1)}, bf16[7,64,256]{2,1,0:T(8,128)(2,1)S(1)}, u32[]{:S(2)}, u32[]{:S(2)}) collective-permute-start(bf16[7,64,256]{2,1,0:T(8,128)(2,1)S(1)} %bitcast_dynamic-update-slice_fusion.refs_1_), channel_id=1, source_target_pairs={{0,3},{1,0},{2,1},{3,2},{4,7},{5,4},{6,5},{7,6},{8,11},{9,8},{10,9... | collective-permute-start | bytes 688136 | tf_op jit(solution)/shard_map/ppermute | solution.py:79
  53.0 0.7 convert_reduce_fusion.2
  53.9 0.7 add_select_fusion.1
  54.6 1.4 fusion.82
  56.7 2.9 %collective-permute-done.9.refs_2_ = bf16[7,64,256]{2,1,0:T(8,128)(2,1)S(1)} collective-permute-done((bf16[7,64,256]{2,1,0:T(8,128)(2,1)S(1)}, bf16[7,64,256]{2,1,0:T(8,128)(2,1)S(1)}, u32[]{:S(2)}, u32[]{:S(2)}) %collective-permute-start.9) | collective-permute-done | bytes 229408 | tf_op jit(solution)/shard_map/ppermute | solution.py:79
  59.6 4.8 %collective-permute-done.10.refs_3_ = bf16[7,64,256]{2,1,0:T(8,128)(2,1)S(1)} collective-permute-done((bf16[7,64,256]{2,1,0:T(8,128)(2,1)S(1)}, bf16[7,64,256]{2,1,0:T(8,128)(2,1)S(1)}, u32[]{:S(2)}, u32[]{:S(2)}) %collective-permute-start.10) | collective-permute-done | bytes 229408 | tf_op jit(solution)/shard_map/ppermute | solution.py:79
  64.3 1.6 collective-permute-done.11.refs_4_
  66.0 1.3 shard_map.104
  67.4 3.6 %collective-permute-start.12 = (f32[4,160,128]{2,1,0:T(8,128)S(1)}, f32[4,160,128]{2,1,0:T(8,128)S(1)}, u32[]{:S(2)}, u32[]{:S(2)}) collective-permute-start(f32[4,160,128]{2,1,0:T(8,128)S(1)} %get-tuple-element.46), channel_id=1, source_target_pairs={{0,32},{1,33},{2,34},{3,35},{4,36},{5,37},{6,38},{7,39},{8,40},{9,... | collective-permute-start | bytes 983048 | tf_op jit(solution)/shard_map/ppermute | solution.py:79
  71.0 1.2 collective-permute-done.12
  72.2 0.4 fusion.67
  72.9 11.5 %collective-permute-start.13 = (bf16[4,160,128]{2,1,0:T(8,128)(2,1)S(1)}, bf16[4,160,128]{2,1,0:T(8,128)(2,1)S(1)}, u32[]{:S(2)}, u32[]{:S(2)}) collective-permute-start(bf16[4,160,128]{2,1,0:T(8,128)(2,1)S(1)} %pad_maximum_fusion.7), channel_id=1, source_target_pairs={{0,256},{1,257},{2,258},{3,259},{4,260},{5,261},{6,262},{7,263},{8... | collective-permute-start | bytes 491528 | tf_op jit(solution)/shard_map/ppermute | solution.py:79
  84.6 14.6 %collective-permute-done.13 = bf16[4,160,128]{2,1,0:T(8,128)(2,1)S(1)} collective-permute-done((bf16[4,160,128]{2,1,0:T(8,128)(2,1)S(1)}, bf16[4,160,128]{2,1,0:T(8,128)(2,1)S(1)}, u32[]{:S(2)}, u32[]{:S(2)}) %collective-permute-start.13) | collective-permute-done | bytes 163872 | tf_op jit(solution)/shard_map/ppermute | solution.py:79
  99.2 0.9 broadcast_in_dim.104
  100.2 3.7 %all-to-all-start.1 = ((bf16[4,2,320,128]{3,2,1,0:T(8,128)(2,1)}), bf16[4,2,320,128]{3,2,1,0:T(8,128)(2,1)S(1)}, u32[]{:S(2)}, u32[]{:S(2)}) async-start(bf16[4,2,320,128]{3,2,1,0:T(8,128)(2,1)} %broadcast_in_dim.104), calls=%async_computation.1 | async-start | bytes 1310720 | tf_op jit(solution)/shard_map/all_to_all | solution.py:83
  103.8 3.0 %collective-permute-start.14 = (bf16[4,512,256]{2,1,0:T(8,128)(2,1)S(1)}, bf16[4,512,256]{2,1,0:T(8,128)(2,1)}, u32[]{:S(2)}, u32[]{:S(2)}) collective-permute-start(bf16[4,512,256]{2,1,0:T(8,128)(2,1)S(1)} %bitcast.136), channel_id=1, source_target_pairs={{0,32},{1,33},{2,34},{3,35},{4,36},{5,37},{6,38},{7,39},{8,40},{9,... | collective-permute-start | bytes 3145736 | tf_op jit(solution)/shard_map/ppermute | solution.py:79
  107.0 6.6 %all-to-all-done.1 = bf16[4,2,320,128]{3,2,1,0:T(8,128)(2,1)S(1)} async-done(((bf16[4,2,320,128]{3,2,1,0:T(8,128)(2,1)}), bf16[4,2,320,128]{3,2,1,0:T(8,128)(2,1)S(1)}, u32[]{:S(2)}, u32[]{:S(2)}) %all-to-all-start.1) | async-done | bytes 655392 | tf_op jit(solution)/shard_map/all_to_all | solution.py:83
  113.6 0.5 fusion.9
  114.2 2.6 %fusion.2 = bf16[4,320,256]{2,1,0:T(8,128)(2,1)} fusion(f32[4,256,320]{1,2,0:T(8,128)S(1)} %fusion.9, bf16[4,512,256]{2,1,0:T(8,128)(2,1)} %collective-permute-done.14, bf16[320,128]{1,0:T(8,128)(2,1)S(1)} %get-tuple-element.38, bf16[320,128]{1,0:T(8,128)(2,1)S(1)} %get-tuple-element.39, bf16[320,128]{1,0:T(8,128)(2,1)S(1)} %get-tuple-element.40, ...), kind=kOutput, calls=%fused_computation.6 | convolution fusion | flops 337510400 | bytes 3342336 | tf_op jit(solution)/shard_map/rk,ekn->ern/dot_general | solution.py:273
  116.8 4.2 %all-to-all-start.2 = ((bf16[4,320,256]{2,1,0:T(8,128)(2,1)}), bf16[4,320,256]{2,1,0:T(8,128)(2,1)S(1)}, u32[]{:S(2)}, u32[]{:S(2)}) async-start(bf16[4,320,256]{2,1,0:T(8,128)(2,1)} %fusion.2), calls=%async_computation.2 | async-start | bytes 1310720 | tf_op jit(solution)/shard_map/all_to_all | solution.py:83
  121.6 4.6 %collective-permute-start.17 = (bf16[4,64,256]{2,0,1:T(4,128)(2,1)S(1)}, bf16[4,64,256]{2,0,1:T(4,128)(2,1)S(1)}, u32[]{:S(2)}, u32[]{:S(2)}) collective-permute-start(bf16[4,64,256]{2,0,1:T(4,128)(2,1)S(1)} %get-tuple-element.61), channel_id=1, source_target_pairs={{0,12},{1,13},{2,14},{3,15},{4,0},{5,1},{6,2},{7,3},{8,4},{9,5},{1... | collective-permute-start | bytes 393224 | tf_op jit(solution)/shard_map/ppermute | solution.py:79
  126.2 2.5 %collective-permute-start.16 = (bf16[4,64,256]{2,0,1:T(4,128)(2,1)S(1)}, bf16[4,64,256]{2,0,1:T(4,128)(2,1)S(1)}, u32[]{:S(2)}, u32[]{:S(2)}) collective-permute-start(bf16[4,64,256]{2,0,1:T(4,128)(2,1)S(1)} %get-tuple-element.62), channel_id=1, source_target_pairs={{0,8},{1,9},{2,10},{3,11},{4,12},{5,13},{6,14},{7,15},{8,0},{9,1},... | collective-permute-start | bytes 393224 | tf_op jit(solution)/shard_map/ppermute | solution.py:79
  128.7 2.5 %collective-permute-start.15 = (bf16[4,64,256]{2,0,1:T(4,128)(2,1)S(1)}, bf16[4,64,256]{2,0,1:T(4,128)(2,1)S(1)}, u32[]{:S(2)}, u32[]{:S(2)}) collective-permute-start(bf16[4,64,256]{2,0,1:T(4,128)(2,1)S(1)} %get-tuple-element.60), channel_id=1, source_target_pairs={{0,4},{1,5},{2,6},{3,7},{4,8},{5,9},{6,10},{7,11},{8,12},{9,13},{1... | collective-permute-start | bytes 393224 | tf_op jit(solution)/shard_map/ppermute | solution.py:79
  131.3 0.8 pad_maximum_fusion.5
  132.1 5.4 %all-to-all-start.3 = ((bf16[4,160,256]{2,1,0:T(8,128)(2,1)}), bf16[4,160,256]{2,1,0:T(8,128)(2,1)S(1)}, u32[]{:S(2)}, u32[]{:S(2)}) async-start(bf16[4,160,256]{2,1,0:T(8,128)(2,1)} %pad_maximum_fusion.5), calls=%async_computation.3 | async-start | bytes 655360 | tf_op jit(solution)/shard_map/all_to_all | solution.py:83
  137.5 0.5 pad_maximum_fusion.1
  138.2 0.5 pad_maximum_fusion.2
  138.7 1.1 constant_dynamic-slice_fusion.7
  139.8 2.8 %collective-permute-start.20 = (bf16[4,64,256]{2,1,0:T(8,128)(2,1)S(1)}, bf16[4,64,256]{2,1,0:T(8,128)(2,1)S(1)}, u32[]{:S(2)}, u32[]{:S(2)}) collective-permute-start(bf16[4,64,256]{2,1,0:T(8,128)(2,1)S(1)} %bitcast.144), channel_id=1, source_target_pairs={{0,3},{1,0},{2,1},{3,2},{4,7},{5,4},{6,5},{7,6},{8,11},{9,8},{10,9... | collective-permute-start | bytes 393224 | tf_op jit(solution)/shard_map/ppermute | solution.py:79
  142.6 3.1 %collective-permute-start.19 = (bf16[4,64,256]{2,1,0:T(8,128)(2,1)S(1)}, bf16[4,64,256]{2,1,0:T(8,128)(2,1)S(1)}, u32[]{:S(2)}, u32[]{:S(2)}) collective-permute-start(bf16[4,64,256]{2,1,0:T(8,128)(2,1)S(1)} %bitcast.145), channel_id=1, source_target_pairs={{0,2},{1,3},{2,0},{3,1},{4,6},{5,7},{6,4},{7,5},{8,10},{9,11},{10,... | collective-permute-start | bytes 393224 | tf_op jit(solution)/shard_map/ppermute | solution.py:79
  145.8 1.9 %collective-permute-start.18 = (bf16[4,64,256]{2,1,0:T(8,128)(2,1)S(1)}, bf16[4,64,256]{2,1,0:T(8,128)(2,1)S(1)}, u32[]{:S(2)}, u32[]{:S(2)}) collective-permute-start(bf16[4,64,256]{2,1,0:T(8,128)(2,1)S(1)} %bitcast.146), channel_id=1, source_target_pairs={{0,1},{1,2},{2,3},{3,0},{4,5},{5,6},{6,7},{7,4},{8,9},{9,10},{10,1... | collective-permute-start | bytes 393224 | tf_op jit(solution)/shard_map/ppermute | solution.py:79
  147.8 2.4 %collective-permute-done.19 = bf16[4,64,256]{2,1,0:T(8,128)(2,1)S(1)} collective-permute-done((bf16[4,64,256]{2,1,0:T(8,128)(2,1)S(1)}, bf16[4,64,256]{2,1,0:T(8,128)(2,1)S(1)}, u32[]{:S(2)}, u32[]{:S(2)}) %collective-permute-start.19) | collective-permute-done | bytes 131104 | tf_op jit(solution)/shard_map/ppermute | solution.py:79
  150.1 2.5 %collective-permute-done.18 = bf16[4,64,256]{2,1,0:T(8,128)(2,1)S(1)} collective-permute-done((bf16[4,64,256]{2,1,0:T(8,128)(2,1)S(1)}, bf16[4,64,256]{2,1,0:T(8,128)(2,1)S(1)}, u32[]{:S(2)}, u32[]{:S(2)}) %collective-permute-start.18) | collective-permute-done | bytes 131104 | tf_op jit(solution)/shard_map/ppermute | solution.py:79
  152.9 7.4 %collective-permute-start.21 = (bf16[16,64,256]{2,1,0:T(8,128)(2,1)S(1)}, bf16[16,64,256]{2,1,0:T(8,128)(2,1)S(1)}, u32[]{:S(2)}, u32[]{:S(2)}) collective-permute-start(bf16[16,64,256]{2,1,0:T(8,128)(2,1)S(1)} %bitcast.138), channel_id=1, source_target_pairs={{0,32},{1,33},{2,34},{3,35},{4,36},{5,37},{6,38},{7,39},{8,40},{9,... | collective-permute-start | bytes 1572872 | tf_op jit(solution)/shard_map/ppermute | solution.py:79
  160.9 0.9 collective-permute-done.21
  162.4 1.2 copy.72
  163.6 3.8 %all-to-all-start.4 = ((bf16[16,160,128]{2,1,0:T(8,128)(2,1)}), bf16[16,160,128]{2,1,0:T(8,128)(2,1)S(1)}, u32[]{:S(2)}, u32[]{:S(2)}) async-start(bf16[16,160,128]{2,1,0:T(8,128)(2,1)} %copy.72), calls=%async_computation.4 | async-start | bytes 1310720 | tf_op jit(solution)/shard_map/all_to_all | solution.py:83
  168.1 1.2 fusion.50
  169.3 9.6 %all-to-all-done.4 = bf16[16,160,128]{2,1,0:T(8,128)(2,1)S(1)} async-done(((bf16[16,160,128]{2,1,0:T(8,128)(2,1)}), bf16[16,160,128]{2,1,0:T(8,128)(2,1)S(1)}, u32[]{:S(2)}, u32[]{:S(2)}) %all-to-all-start.4) | async-done | bytes 655392 | tf_op jit(solution)/shard_map/all_to_all | solution.py:83
  179.4 0.4 fusion.48
  179.9 4.3 %collective-permute-start.22 = (bf16[160,384]{1,0:T(8,128)(2,1)S(1)}, bf16[160,384]{1,0:T(8,128)(2,1)S(1)}, u32[]{:S(2)}, u32[]{:S(2)}) collective-permute-start(bf16[160,384]{1,0:T(8,128)(2,1)S(1)} %pad_maximum_fusion.10), channel_id=1, source_target_pairs={{0,32},{1,33},{2,34},{3,35},{4,36},{5,37},{6,38},{7,39},{8,40},{9,... | collective-permute-start | bytes 368648 | tf_op jit(solution)/shard_map/ppermute | solution.py:79
  184.2 0.9 collective-permute-done.22
  185.5 0.7 slice.200
  186.2 0.7 copy.73
  (106 shorter events, 5.6 us)
Async XLA Ops:
  0.6 34.6 %copy-start.3 = (bf16[256,512]{1,0:T(8,128)(2,1)S(1)}, bf16[256,512]{1,0:T(8,128)(2,1)}, u32[]{:S(2)}) copy-start(bf16[256,512]{1,0:T(8,128)(2,1)} %param.12) | copy-start | bytes 786436
  1.7 25.5 %collective-permute-start.2 = (bf16[64,256]{1,0:T(8,128)(2,1)S(1)}, bf16[64,256]{1,0:T(8,128)(2,1)S(1)}, u32[]{:S(2)}, u32[]{:S(2)}) collective-permute-start(bf16[64,256]{1,0:T(8,128)(2,1)S(1)} %get-tuple-element.36), channel_id=1, source_target_pairs={{0,64},{1,65},{2,66},{3,67},{4,68},{5,69},{6,70},{7,71},{8,72},{9,... | collective-permute-start | bytes 98312 | tf_op jit(solution)/shard_map/ppermute | solution.py:79
  6.1 22.4 %collective-permute-start.3 = (bf16[64,256]{1,0:T(8,128)(2,1)S(1)}, bf16[64,256]{1,0:T(8,128)(2,1)S(1)}, u32[]{:S(2)}, u32[]{:S(2)}) collective-permute-start(bf16[64,256]{1,0:T(8,128)(2,1)S(1)} %get-tuple-element.36), channel_id=1, source_target_pairs={{0,128},{1,129},{2,130},{3,131},{4,132},{5,133},{6,134},{7,135},{8... | collective-permute-start | bytes 98312 | tf_op jit(solution)/shard_map/ppermute | solution.py:79
  11.0 20.7 %collective-permute-start.4 = (bf16[64,256]{1,0:T(8,128)(2,1)S(1)}, bf16[64,256]{1,0:T(8,128)(2,1)S(1)}, u32[]{:S(2)}, u32[]{:S(2)}) collective-permute-start(bf16[64,256]{1,0:T(8,128)(2,1)S(1)} %get-tuple-element.36), channel_id=1, source_target_pairs={{0,192},{1,193},{2,194},{3,195},{4,196},{5,197},{6,198},{7,199},{8... | collective-permute-start | bytes 98312 | tf_op jit(solution)/shard_map/ppermute | solution.py:79
  18.5 18.0 %collective-permute-start.6 = (bf16[64,256]{1,0:T(8,128)(2,1)S(1)}, bf16[64,256]{1,0:T(8,128)(2,1)S(1)}, u32[]{:S(2)}, u32[]{:S(2)}) collective-permute-start(bf16[64,256]{1,0:T(8,128)(2,1)S(1)} %get-tuple-element.35), channel_id=1, source_target_pairs={{0,336},{1,337},{2,338},{3,339},{4,340},{5,341},{6,342},{7,343},{8... | collective-permute-start | bytes 98312 | tf_op jit(solution)/shard_map/ppermute | solution.py:79
  20.4 16.0 %collective-permute-start.7 = (bf16[64,256]{1,0:T(8,128)(2,1)S(1)}, bf16[64,256]{1,0:T(8,128)(2,1)S(1)}, u32[]{:S(2)}, u32[]{:S(2)}) collective-permute-start(bf16[64,256]{1,0:T(8,128)(2,1)S(1)} %get-tuple-element.35), channel_id=1, source_target_pairs={{0,400},{1,401},{2,402},{3,403},{4,404},{5,405},{6,406},{7,407},{8... | collective-permute-start | bytes 98312 | tf_op jit(solution)/shard_map/ppermute | solution.py:79
  27.2 9.3 %collective-permute-start.8 = (bf16[64,256]{1,0:T(8,128)(2,1)S(1)}, bf16[64,256]{1,0:T(8,128)(2,1)S(1)}, u32[]{:S(2)}, u32[]{:S(2)}) collective-permute-start(bf16[64,256]{1,0:T(8,128)(2,1)S(1)} %get-tuple-element.35), channel_id=1, source_target_pairs={{0,464},{1,465},{2,466},{3,467},{4,468},{5,469},{6,470},{7,471},{8... | collective-permute-start | bytes 98312 | tf_op jit(solution)/shard_map/ppermute | solution.py:79
  28.5 5.1 %collective-permute-start = (bf16[128,512]{1,0:T(8,128)(2,1)S(1)}, bf16[128,512]{1,0:T(8,128)(2,1)S(1)}, u32[]{:S(2)}, u32[]{:S(2)}) collective-permute-start(bf16[128,512]{1,0:T(8,128)(2,1)S(1)} %constant_dynamic-slice_fusion.13), channel_id=1, source_target_pairs={{0,32},{1,33},{2,34},{3,35},{4,36},{5,37},{6,38},{7,39},{8,40},{9,... | collective-permute-start | bytes 393224 | tf_op jit(solution)/shard_map/ppermute | solution.py:79
  31.7 4.8 %collective-permute-start.1 = (bf16[256,640]{1,0:T(8,128)(2,1)S(1)}, bf16[256,640]{1,0:T(8,128)(2,1)S(1)}, u32[]{:S(2)}, u32[]{:S(2)}) collective-permute-start(bf16[256,640]{1,0:T(8,128)(2,1)S(1)} %pad_maximum_fusion.4), channel_id=1, source_target_pairs={{0,32},{1,33},{2,34},{3,35},{4,36},{5,37},{6,38},{7,39},{8,40},{9,... | collective-permute-start | bytes 983048 | tf_op jit(solution)/shard_map/ppermute | solution.py:79
  33.6 2.8 %collective-permute-start.5 = (bf16[64,256]{1,0:T(8,128)(2,1)S(1)}, bf16[64,256]{1,0:T(8,128)(2,1)S(1)}, u32[]{:S(2)}, u32[]{:S(2)}) collective-permute-start(bf16[64,256]{1,0:T(8,128)(2,1)S(1)} %get-tuple-element.34), channel_id=1, source_target_pairs={{0,272},{1,273},{2,274},{3,275},{4,276},{5,277},{6,278},{7,279},{8... | collective-permute-start | bytes 98312 | tf_op jit(solution)/shard_map/ppermute | solution.py:79
  37.5 15.2 %copy-start = (bf16[256,256]{1,0:T(8,128)(2,1)S(1)}, bf16[256,256]{1,0:T(8,128)(2,1)}, u32[]{:S(2)}) copy-start(bf16[256,256]{1,0:T(8,128)(2,1)} %param.9) | copy-start | bytes 393220
  37.6 15.2 %copy-start.1 = (bf16[256,256]{1,0:T(8,128)(2,1)S(1)}, bf16[256,256]{1,0:T(8,128)(2,1)}, u32[]{:S(2)}) copy-start(bf16[256,256]{1,0:T(8,128)(2,1)} %param.10) | copy-start | bytes 393220
  37.6 61.7 %all-to-all-start = ((bf16[16,128,256]{2,1,0:T(8,128)(2,1)}), bf16[16,128,256]{2,1,0:T(8,128)(2,1)S(1)}, u32[]{:S(2)}, u32[]{:S(2)}) async-start(bf16[16,128,256]{2,1,0:T(8,128)(2,1)} %bitcast.2), calls=%async_computation | async-start | bytes 2097152 | tf_op jit(solution)/shard_map/all_to_all | solution.py:83
  42.0 17.5 %collective-permute-start.9 = (bf16[7,64,256]{2,1,0:T(8,128)(2,1)S(1)}, bf16[7,64,256]{2,1,0:T(8,128)(2,1)S(1)}, u32[]{:S(2)}, u32[]{:S(2)}) collective-permute-start(bf16[7,64,256]{2,1,0:T(8,128)(2,1)S(1)} %bitcast_dynamic-update-slice_fusion.refs_1_), channel_id=1, source_target_pairs={{0,1},{1,2},{2,3},{3,0},{4,5},{5,6},{6,7},{7,4},{8,9},{9,10},{10,1... | collective-permute-start | bytes 688136 | tf_op jit(solution)/shard_map/ppermute | solution.py:79
  45.3 19.0 %collective-permute-start.10 = (bf16[7,64,256]{2,1,0:T(8,128)(2,1)S(1)}, bf16[7,64,256]{2,1,0:T(8,128)(2,1)S(1)}, u32[]{:S(2)}, u32[]{:S(2)}) collective-permute-start(bf16[7,64,256]{2,1,0:T(8,128)(2,1)S(1)} %bitcast_dynamic-update-slice_fusion.refs_1_), channel_id=1, source_target_pairs={{0,2},{1,3},{2,0},{3,1},{4,6},{5,7},{6,4},{7,5},{8,10},{9,11},{10,... | collective-permute-start | bytes 688136 | tf_op jit(solution)/shard_map/ppermute | solution.py:79
  49.6 16.3 %collective-permute-start.11 = (bf16[7,64,256]{2,1,0:T(8,128)(2,1)S(1)}, bf16[7,64,256]{2,1,0:T(8,128)(2,1)S(1)}, u32[]{:S(2)}, u32[]{:S(2)}) collective-permute-start(bf16[7,64,256]{2,1,0:T(8,128)(2,1)S(1)} %bitcast_dynamic-update-slice_fusion.refs_1_), channel_id=1, source_target_pairs={{0,3},{1,0},{2,1},{3,2},{4,7},{5,4},{6,5},{7,6},{8,11},{9,8},{10,9... | collective-permute-start | bytes 688136 | tf_op jit(solution)/shard_map/ppermute | solution.py:79
  67.4 4.8 %collective-permute-start.12 = (f32[4,160,128]{2,1,0:T(8,128)S(1)}, f32[4,160,128]{2,1,0:T(8,128)S(1)}, u32[]{:S(2)}, u32[]{:S(2)}) collective-permute-start(f32[4,160,128]{2,1,0:T(8,128)S(1)} %get-tuple-element.46), channel_id=1, source_target_pairs={{0,32},{1,33},{2,34},{3,35},{4,36},{5,37},{6,38},{7,39},{8,40},{9,... | collective-permute-start | bytes 983048 | tf_op jit(solution)/shard_map/ppermute | solution.py:79
  72.9 26.3 %collective-permute-start.13 = (bf16[4,160,128]{2,1,0:T(8,128)(2,1)S(1)}, bf16[4,160,128]{2,1,0:T(8,128)(2,1)S(1)}, u32[]{:S(2)}, u32[]{:S(2)}) collective-permute-start(bf16[4,160,128]{2,1,0:T(8,128)(2,1)S(1)} %pad_maximum_fusion.7), channel_id=1, source_target_pairs={{0,256},{1,257},{2,258},{3,259},{4,260},{5,261},{6,262},{7,263},{8... | collective-permute-start | bytes 491528 | tf_op jit(solution)/shard_map/ppermute | solution.py:79
  100.2 13.4 %all-to-all-start.1 = ((bf16[4,2,320,128]{3,2,1,0:T(8,128)(2,1)}), bf16[4,2,320,128]{3,2,1,0:T(8,128)(2,1)S(1)}, u32[]{:S(2)}, u32[]{:S(2)}) async-start(bf16[4,2,320,128]{3,2,1,0:T(8,128)(2,1)} %broadcast_in_dim.104), calls=%async_computation.1 | async-start | bytes 1310720 | tf_op jit(solution)/shard_map/all_to_all | solution.py:83
  103.8 10.3 %collective-permute-start.14 = (bf16[4,512,256]{2,1,0:T(8,128)(2,1)S(1)}, bf16[4,512,256]{2,1,0:T(8,128)(2,1)}, u32[]{:S(2)}, u32[]{:S(2)}) collective-permute-start(bf16[4,512,256]{2,1,0:T(8,128)(2,1)S(1)} %bitcast.136), channel_id=1, source_target_pairs={{0,32},{1,33},{2,34},{3,35},{4,36},{5,37},{6,38},{7,39},{8,40},{9,... | collective-permute-start | bytes 3145736 | tf_op jit(solution)/shard_map/ppermute | solution.py:79
  116.8 4.2 %copy-start.2 = (bf16[8192,64]{0,1:T(8,128)(2,1)S(1)}, bf16[8192,64]{0,1:T(8,128)(2,1)}, u32[]{:S(2)}) copy-start(bf16[8192,64]{0,1:T(8,128)(2,1)} %param.14) | copy-start | bytes 3145732
  116.8 4.2 %dynamic-slice-start = ((f32[8192]{0:T(1024)}, s32[]{:T(128)}), f32[4096]{0:T(1024)S(1)}, s32[]{:S(2)}) async-start(f32[8192]{0:T(1024)} %param.13, s32[]{:T(128)} %select_n.401), calls=%async_computation.5 | async-start | bytes 33280 | tf_op jit(solution)/shard_map/dynamic_slice | solution.py:263
  116.8 14.4 %all-to-all-start.2 = ((bf16[4,320,256]{2,1,0:T(8,128)(2,1)}), bf16[4,320,256]{2,1,0:T(8,128)(2,1)S(1)}, u32[]{:S(2)}, u32[]{:S(2)}) async-start(bf16[4,320,256]{2,1,0:T(8,128)(2,1)} %fusion.2), calls=%async_computation.2 | async-start | bytes 1310720 | tf_op jit(solution)/shard_map/all_to_all | solution.py:83
  121.6 15.9 %collective-permute-start.17 = (bf16[4,64,256]{2,0,1:T(4,128)(2,1)S(1)}, bf16[4,64,256]{2,0,1:T(4,128)(2,1)S(1)}, u32[]{:S(2)}, u32[]{:S(2)}) collective-permute-start(bf16[4,64,256]{2,0,1:T(4,128)(2,1)S(1)} %get-tuple-element.61), channel_id=1, source_target_pairs={{0,12},{1,13},{2,14},{3,15},{4,0},{5,1},{6,2},{7,3},{8,4},{9,5},{1... | collective-permute-start | bytes 393224 | tf_op jit(solution)/shard_map/ppermute | solution.py:79
  126.2 11.3 %collective-permute-start.16 = (bf16[4,64,256]{2,0,1:T(4,128)(2,1)S(1)}, bf16[4,64,256]{2,0,1:T(4,128)(2,1)S(1)}, u32[]{:S(2)}, u32[]{:S(2)}) collective-permute-start(bf16[4,64,256]{2,0,1:T(4,128)(2,1)S(1)} %get-tuple-element.62), channel_id=1, source_target_pairs={{0,8},{1,9},{2,10},{3,11},{4,12},{5,13},{6,14},{7,15},{8,0},{9,1},... | collective-permute-start | bytes 393224 | tf_op jit(solution)/shard_map/ppermute | solution.py:79
  128.7 8.8 %collective-permute-start.15 = (bf16[4,64,256]{2,0,1:T(4,128)(2,1)S(1)}, bf16[4,64,256]{2,0,1:T(4,128)(2,1)S(1)}, u32[]{:S(2)}, u32[]{:S(2)}) collective-permute-start(bf16[4,64,256]{2,0,1:T(4,128)(2,1)S(1)} %get-tuple-element.60), channel_id=1, source_target_pairs={{0,4},{1,5},{2,6},{3,7},{4,8},{5,9},{6,10},{7,11},{8,12},{9,13},{1... | collective-permute-start | bytes 393224 | tf_op jit(solution)/shard_map/ppermute | solution.py:79
  132.1 28.2 %all-to-all-start.3 = ((bf16[4,160,256]{2,1,0:T(8,128)(2,1)}), bf16[4,160,256]{2,1,0:T(8,128)(2,1)S(1)}, u32[]{:S(2)}, u32[]{:S(2)}) async-start(bf16[4,160,256]{2,1,0:T(8,128)(2,1)} %pad_maximum_fusion.5), calls=%async_computation.3 | async-start | bytes 655360 | tf_op jit(solution)/shard_map/all_to_all | solution.py:83
  139.8 8.0 %collective-permute-start.20 = (bf16[4,64,256]{2,1,0:T(8,128)(2,1)S(1)}, bf16[4,64,256]{2,1,0:T(8,128)(2,1)S(1)}, u32[]{:S(2)}, u32[]{:S(2)}) collective-permute-start(bf16[4,64,256]{2,1,0:T(8,128)(2,1)S(1)} %bitcast.144), channel_id=1, source_target_pairs={{0,3},{1,0},{2,1},{3,2},{4,7},{5,4},{6,5},{7,6},{8,11},{9,8},{10,9... | collective-permute-start | bytes 393224 | tf_op jit(solution)/shard_map/ppermute | solution.py:79
  142.6 7.5 %collective-permute-start.19 = (bf16[4,64,256]{2,1,0:T(8,128)(2,1)S(1)}, bf16[4,64,256]{2,1,0:T(8,128)(2,1)S(1)}, u32[]{:S(2)}, u32[]{:S(2)}) collective-permute-start(bf16[4,64,256]{2,1,0:T(8,128)(2,1)S(1)} %bitcast.145), channel_id=1, source_target_pairs={{0,2},{1,3},{2,0},{3,1},{4,6},{5,7},{6,4},{7,5},{8,10},{9,11},{10,... | collective-permute-start | bytes 393224 | tf_op jit(solution)/shard_map/ppermute | solution.py:79
  145.8 6.9 %collective-permute-start.18 = (bf16[4,64,256]{2,1,0:T(8,128)(2,1)S(1)}, bf16[4,64,256]{2,1,0:T(8,128)(2,1)S(1)}, u32[]{:S(2)}, u32[]{:S(2)}) collective-permute-start(bf16[4,64,256]{2,1,0:T(8,128)(2,1)S(1)} %bitcast.146), channel_id=1, source_target_pairs={{0,1},{1,2},{2,3},{3,0},{4,5},{5,6},{6,7},{7,4},{8,9},{9,10},{10,1... | collective-permute-start | bytes 393224 | tf_op jit(solution)/shard_map/ppermute | solution.py:79
  152.9 8.9 %collective-permute-start.21 = (bf16[16,64,256]{2,1,0:T(8,128)(2,1)S(1)}, bf16[16,64,256]{2,1,0:T(8,128)(2,1)S(1)}, u32[]{:S(2)}, u32[]{:S(2)}) collective-permute-start(bf16[16,64,256]{2,1,0:T(8,128)(2,1)S(1)} %bitcast.138), channel_id=1, source_target_pairs={{0,32},{1,33},{2,34},{3,35},{4,36},{5,37},{6,38},{7,39},{8,40},{9,... | collective-permute-start | bytes 1572872 | tf_op jit(solution)/shard_map/ppermute | solution.py:79
  163.6 15.2 %all-to-all-start.4 = ((bf16[16,160,128]{2,1,0:T(8,128)(2,1)}), bf16[16,160,128]{2,1,0:T(8,128)(2,1)S(1)}, u32[]{:S(2)}, u32[]{:S(2)}) async-start(bf16[16,160,128]{2,1,0:T(8,128)(2,1)} %copy.72), calls=%async_computation.4 | async-start | bytes 1310720 | tf_op jit(solution)/shard_map/all_to_all | solution.py:83
  179.9 5.3 %collective-permute-start.22 = (bf16[160,384]{1,0:T(8,128)(2,1)S(1)}, bf16[160,384]{1,0:T(8,128)(2,1)S(1)}, u32[]{:S(2)}, u32[]{:S(2)}) collective-permute-start(bf16[160,384]{1,0:T(8,128)(2,1)S(1)} %pad_maximum_fusion.10), channel_id=1, source_target_pairs={{0,32},{1,33},{2,34},{3,35},{4,36},{5,37},{6,38},{7,39},{8,40},{9,... | collective-permute-start | bytes 368648 | tf_op jit(solution)/shard_map/ppermute | solution.py:79

commit v5 on v3

--- a/solution.py
+++ b/solution.py
@@ -229,14 +229,15 @@
     cache_rows = gathered[:, :columns] * lax.rsqrt(square_total / D + EPS)[:, None]
     cache_rot = turn(cache_rows, position, tp * columns).astype(BF)
 
-    own_hidden = jnp.where(zh == 0, hidden0, hidden1)
-    done = jnp.concatenate([own_hidden, jnp.pad(cache_rot, ((0, 0), (0, 128 - columns)))], axis=1)
-    done_other = send(done, CORE)
-    kept = jnp.where(first, jnp.concatenate([done, done_other]), jnp.concatenate([done_other, done]))
     own_rank = jnp.where(rank >= 0, rank + jnp.where(first, 0, count0), -1)
-    put = own_rank[:, None] == jnp.arange(PAIR_KEEP, dtype=jnp.int32)[None, :]
-    output = jnp.dot(put.astype(BF), kept, preferred_element_type=F32).astype(BF)
-    return output[:, :256], output[:, 256 : 256 + columns]
+    put = (own_rank[:, None] == jnp.arange(PAIR_KEEP, dtype=jnp.int32)[None, :]).astype(BF)
+
+    def back(mine):
+        theirs = send(mine, CORE)
+        kept = jnp.where(first, jnp.concatenate([mine, theirs]), jnp.concatenate([theirs, mine]))
+        return jnp.dot(put, kept, preferred_element_type=F32).astype(BF)
+
+    return back(jnp.where(zh == 0, hidden0, hidden1)), back(cache_rot)
 
 
 def solution(mesh):

time: 176 us -> 176 us (level)
  waiting for transfers between devices: 38.2 us -> 34.7 us
  starting transfers between devices: 108 us -> 111 us
    all_to_all x5, waiting for transfers between devices: 15.5 us -> 12.9 us  [exchange(): return lax.all_to_all(x, axes, 0, 0, tiled=True, axis_index_groups=groups)]
    ppermute x20 -> x21, starting transfers between devices: 78.8 us -> 81.3 us  [send(): return lax.ppermute(x, AXES, table)]
    ppermute x20 -> x21, waiting for transfers between devices: 22.6 us -> 21.8 us  [send(): return lax.ppermute(x, AXES, table)]
  transfers between devices with their start and end apart: 25 -> 26, of which waited for: 8 -> 7; matrix products, arithmetic and copies ran while one was open for 9% -> 11% of each run, Pallas kernels for 0% -> 0%
where the time goes in v5:
time: 176 us; the launch traced here: 174 us
  starting transfers between devices  111 us (63%)
  waiting for transfers between devices  34.7 us (20%)
  other arithmetic  11.1 us (6%)
  matrix products  7.51 us (4%)
  local copies, waits for them, and re-layouts  6.96 us (4%)
  between operations  3.19 us (2%)
    ppermute x21, starting transfers between devices, send(): return lax.ppermute(x, AXES, table)  81.3 us
    all_to_all x5, starting transfers between devices, exchange(): return lax.all_to_all(x, axes, 0, 0, tiled=True, axis_index_groups=groups)  29.7 us
    ppermute x21, waiting for transfers between devices, send(): return lax.ppermute(x, AXES, table)  21.8 us
    all_to_all x5, waiting for transfers between devices, exchange(): return lax.all_to_all(x, axes, 0, 0, tiled=True, axis_index_groups=groups)  12.9 us
  transfers between devices with their start and end apart: 26, of which 7 were waited for; matrix products, arithmetic and copies ran while one was open for 11% of the time, Pallas kernels for 0%

profile of v5, /device:TPU:65, one launch (start us, length us, event | category | flops | bytes accessed | tf_op | source)
XLA Modules:
  0.0 174.5 jit_solution(12681745468451532991)
XLA Ops:
  0.7 1.0 broadcast_select_fusion
  1.7 0.7 collective-permute-start.7
  2.4 10.8 %collective-permute-start.6 = (bf16[256,256]{1,0:T(8,128)(2,1)S(1)}, bf16[256,256]{1,0:T(8,128)(2,1)S(1)}, u32[]{:S(2)}, u32[]{:S(2)}) collective-permute-start(bf16[256,256]{1,0:T(8,128)(2,1)S(1)} %get-tuple-element.38), channel_id=1, source_target_pairs={{0,336},{1,337},{2,338},{3,339},{4,340},{5,341},{6,342},{7,343},{8... | collective-permute-start | bytes 393224 | tf_op jit(solution)/shard_map/ppermute | solution.py:76
  13.2 0.7 collective-permute-start.8
  13.9 0.9 constant_dynamic-slice_fusion.14
  14.9 2.9 %collective-permute-start = (bf16[128,512]{1,0:T(8,128)(2,1)S(1)}, bf16[128,512]{1,0:T(8,128)(2,1)S(1)}, u32[]{:S(2)}, u32[]{:S(2)}) collective-permute-start(bf16[128,512]{1,0:T(8,128)(2,1)S(1)} %constant_dynamic-slice_fusion.14), channel_id=1, source_target_pairs={{0,32},{1,33},{2,34},{3,35},{4,36},{5,37},{6,38},{7,39},{8,40},{9,... | collective-permute-start | bytes 393224 | tf_op jit(solution)/shard_map/ppermute | solution.py:76
  17.7 1.3 collective-permute-start.5
  19.8 0.8 select_reduce_fusion
  20.6 0.7 fusion.100
  21.5 1.0 fusion.35
  22.5 1.3 collective-permute-start.4
  23.8 14.7 %collective-permute-start.3 = (bf16[256,256]{1,0:T(8,128)(2,1)S(1)}, bf16[256,256]{1,0:T(8,128)(2,1)S(1)}, u32[]{:S(2)}, u32[]{:S(2)}) collective-permute-start(bf16[256,256]{1,0:T(8,128)(2,1)S(1)} %get-tuple-element.18), channel_id=1, source_target_pairs={{0,128},{1,129},{2,130},{3,131},{4,132},{5,133},{6,134},{7,135},{8... | collective-permute-start | bytes 393224 | tf_op jit(solution)/shard_map/ppermute | solution.py:76
  38.6 1.9 %collective-permute-start.2 = (bf16[256,256]{1,0:T(8,128)(2,1)S(1)}, bf16[256,256]{1,0:T(8,128)(2,1)S(1)}, u32[]{:S(2)}, u32[]{:S(2)}) collective-permute-start(bf16[256,256]{1,0:T(8,128)(2,1)S(1)} %get-tuple-element.18), channel_id=1, source_target_pairs={{0,64},{1,65},{2,66},{3,67},{4,68},{5,69},{6,70},{7,71},{8,72},{9,... | collective-permute-start | bytes 393224 | tf_op jit(solution)/shard_map/ppermute | solution.py:76
  40.5 1.0 broadcast_select_fusion.2
  41.8 2.5 %collective-permute-done.2 = bf16[256,256]{1,0:T(8,128)(2,1)S(1)} collective-permute-done((bf16[256,256]{1,0:T(8,128)(2,1)S(1)}, bf16[256,256]{1,0:T(8,128)(2,1)S(1)}, u32[]{:S(2)}, u32[]{:S(2)}) %collective-permute-start.2) | collective-permute-done | bytes 131104 | tf_op jit(solution)/shard_map/ppermute | solution.py:76
  44.3 1.1 broadcast_in_dim.68
  45.4 7.4 %all-to-all-start = ((bf16[16,128,256]{2,1,0:T(8,128)(2,1)}), bf16[16,128,256]{2,1,0:T(8,128)(2,1)S(1)}, u32[]{:S(2)}, u32[]{:S(2)}) async-start(bf16[16,128,256]{2,1,0:T(8,128)(2,1)} %bitcast.2), calls=%async_computation | async-start | bytes 2097152 | tf_op jit(solution)/shard_map/all_to_all | solution.py:80
  52.8 4.6 %collective-permute-start.1 = (bf16[256,640]{1,0:T(8,128)(2,1)S(1)}, bf16[256,640]{1,0:T(8,128)(2,1)S(1)}, u32[]{:S(2)}, u32[]{:S(2)}) collective-permute-start(bf16[256,640]{1,0:T(8,128)(2,1)S(1)} %fusion.35), channel_id=1, source_target_pairs={{0,32},{1,33},{2,34},{3,35},{4,36},{5,37},{6,38},{7,39},{8,40},{9,... | collective-permute-start | bytes 983048 | tf_op jit(solution)/shard_map/ppermute | solution.py:76
  57.5 1.9 %collective-permute-start.9 = (bf16[2048,256]{1,0:T(8,128)(2,1)S(1)}, bf16[2048,256]{1,0:T(8,128)(2,1)S(1)}, u32[]{:S(2)}, u32[]{:S(2)}) collective-permute-start(bf16[2048,256]{1,0:T(8,128)(2,1)S(1)} %constant_dynamic-update-slice_fusion), channel_id=1, source_target_pairs={{0,32},{1,33},{2,34},{3,35},{4,36},{5,37},{6,38},{7,39},{8,40},{9,... | collective-permute-start | bytes 3145736 | tf_op jit(solution)/shard_map/ppermute | solution.py:76
  59.5 0.3 maximum_select_fusion
  59.8 0.7 convert_reduce_fusion.2
  60.6 0.7 add_select_fusion.2
  61.2 0.3 fusion.113
  61.9 0.9 fusion.114
  62.8 0.9 fusion.115
  63.7 0.9 fusion.4
  64.6 0.6 fusion.9
  65.1 0.6 fusion.22
  65.8 3.8 %collective-permute-start.10 = (bf16[4,160,128]{2,1,0:T(8,128)(2,1)S(1)}, bf16[4,160,128]{2,1,0:T(8,128)(2,1)S(1)}, u32[]{:S(2)}, u32[]{:S(2)}) collective-permute-start(bf16[4,160,128]{2,1,0:T(8,128)(2,1)S(1)} %pad_maximum_fusion.6), channel_id=1, source_target_pairs={{0,256},{1,257},{2,258},{3,259},{4,260},{5,261},{6,262},{7,263},{8... | collective-permute-start | bytes 491528 | tf_op jit(solution)/shard_map/ppermute | solution.py:76
  69.8 15.0 %collective-permute-done.10 = bf16[4,160,128]{2,1,0:T(8,128)(2,1)S(1)} collective-permute-done((bf16[4,160,128]{2,1,0:T(8,128)(2,1)S(1)}, bf16[4,160,128]{2,1,0:T(8,128)(2,1)S(1)}, u32[]{:S(2)}, u32[]{:S(2)}) %collective-permute-start.10) | collective-permute-done | bytes 163872 | tf_op jit(solution)/shard_map/ppermute | solution.py:76
  84.9 0.9 broadcast_in_dim.109
  85.8 4.0 %all-to-all-start.1 = ((bf16[4,2,320,128]{3,2,1,0:T(8,128)(2,1)}), bf16[4,2,320,128]{3,2,1,0:T(8,128)(2,1)S(1)}, u32[]{:S(2)}, u32[]{:S(2)}) async-start(bf16[4,2,320,128]{3,2,1,0:T(8,128)(2,1)} %broadcast_in_dim.109), calls=%async_computation.1 | async-start | bytes 1310720 | tf_op jit(solution)/shard_map/all_to_all | solution.py:80
  89.8 3.7 %collective-permute-start.11 = (bf16[4,512,256]{2,1,0:T(8,128)(2,1)S(1)}, bf16[4,512,256]{2,1,0:T(8,128)(2,1)S(1)}, u32[]{:S(2)}, u32[]{:S(2)}) collective-permute-start(bf16[4,512,256]{2,1,0:T(8,128)(2,1)S(1)} %bitcast.116), channel_id=1, source_target_pairs={{0,32},{1,33},{2,34},{3,35},{4,36},{5,37},{6,38},{7,39},{8,40},{9,... | collective-permute-start | bytes 3145736 | tf_op jit(solution)/shard_map/ppermute | solution.py:76
  93.6 4.9 %all-to-all-done.1 = bf16[4,2,320,128]{3,2,1,0:T(8,128)(2,1)S(1)} async-done(((bf16[4,2,320,128]{3,2,1,0:T(8,128)(2,1)}), bf16[4,2,320,128]{3,2,1,0:T(8,128)(2,1)S(1)}, u32[]{:S(2)}, u32[]{:S(2)}) %all-to-all-start.1) | async-done | bytes 655392 | tf_op jit(solution)/shard_map/all_to_all | solution.py:80
  98.6 0.5 fusion.36
  99.2 1.4 fusion.14
  100.5 4.0 %all-to-all-start.2 = ((bf16[4,320,256]{2,1,0:T(8,128)(2,1)}), bf16[4,320,256]{2,1,0:T(8,128)(2,1)S(1)}, u32[]{:S(2)}, u32[]{:S(2)}) async-start(bf16[4,320,256]{2,1,0:T(8,128)(2,1)} %fusion.14), calls=%async_computation.2 | async-start | bytes 1310720 | tf_op jit(solution)/shard_map/all_to_all | solution.py:80
  104.6 0.4 reshape.219
  105.2 3.4 %collective-permute-start.13 = (bf16[4,64,256]{2,0,1:T(4,128)(2,1)S(1)}, bf16[4,64,256]{2,0,1:T(4,128)(2,1)S(1)}, u32[]{:S(2)}, u32[]{:S(2)}) collective-permute-start(bf16[4,64,256]{2,0,1:T(4,128)(2,1)S(1)} %get-tuple-element.61), channel_id=1, source_target_pairs={{0,4},{1,5},{2,6},{3,7},{4,8},{5,9},{6,10},{7,11},{8,12},{9,13},{1... | collective-permute-start | bytes 393224 | tf_op jit(solution)/shard_map/ppermute | solution.py:76
  108.6 3.1 %collective-permute-start.15 = (bf16[4,64,256]{2,0,1:T(4,128)(2,1)S(1)}, bf16[4,64,256]{2,0,1:T(4,128)(2,1)S(1)}, u32[]{:S(2)}, u32[]{:S(2)}) collective-permute-start(bf16[4,64,256]{2,0,1:T(4,128)(2,1)S(1)} %get-tuple-element.62), channel_id=1, source_target_pairs={{0,12},{1,13},{2,14},{3,15},{4,0},{5,1},{6,2},{7,3},{8,4},{9,5},{1... | collective-permute-start | bytes 393224 | tf_op jit(solution)/shard_map/ppermute | solution.py:76
  111.7 3.7 %collective-permute-start.14 = (bf16[4,64,256]{2,0,1:T(4,128)(2,1)S(1)}, bf16[4,64,256]{2,0,1:T(4,128)(2,1)S(1)}, u32[]{:S(2)}, u32[]{:S(2)}) collective-permute-start(bf16[4,64,256]{2,0,1:T(4,128)(2,1)S(1)} %get-tuple-element.63), channel_id=1, source_target_pairs={{0,8},{1,9},{2,10},{3,11},{4,12},{5,13},{6,14},{7,15},{8,0},{9,1},... | collective-permute-start | bytes 393224 | tf_op jit(solution)/shard_map/ppermute | solution.py:76
  115.6 0.7 pad_maximum_fusion.4
  116.3 10.6 %all-to-all-start.3 = ((bf16[4,160,256]{2,1,0:T(8,128)(2,1)}), bf16[4,160,256]{2,1,0:T(8,128)(2,1)S(1)}, u32[]{:S(2)}, u32[]{:S(2)}) async-start(bf16[4,160,256]{2,1,0:T(8,128)(2,1)} %pad_maximum_fusion.4), calls=%async_computation.3 | async-start | bytes 655360 | tf_op jit(solution)/shard_map/all_to_all | solution.py:80
  126.9 0.5 pad_maximum_fusion.1
  127.6 0.5 pad_maximum_fusion.2
  128.1 1.1 constant_dynamic-slice_fusion.7
  129.3 2.2 %collective-permute-start.16 = (bf16[4,64,256]{2,1,0:T(8,128)(2,1)S(1)}, bf16[4,64,256]{2,1,0:T(8,128)(2,1)S(1)}, u32[]{:S(2)}, u32[]{:S(2)}) collective-permute-start(bf16[4,64,256]{2,1,0:T(8,128)(2,1)S(1)} %bitcast.129), channel_id=1, source_target_pairs={{0,1},{1,2},{2,3},{3,0},{4,5},{5,6},{6,7},{7,4},{8,9},{9,10},{10,1... | collective-permute-start | bytes 393224 | tf_op jit(solution)/shard_map/ppermute | solution.py:76
  131.5 3.7 %collective-permute-start.17 = (bf16[4,64,256]{2,1,0:T(8,128)(2,1)S(1)}, bf16[4,64,256]{2,1,0:T(8,128)(2,1)S(1)}, u32[]{:S(2)}, u32[]{:S(2)}) collective-permute-start(bf16[4,64,256]{2,1,0:T(8,128)(2,1)S(1)} %bitcast.128), channel_id=1, source_target_pairs={{0,2},{1,3},{2,0},{3,1},{4,6},{5,7},{6,4},{7,5},{8,10},{9,11},{10,... | collective-permute-start | bytes 393224 | tf_op jit(solution)/shard_map/ppermute | solution.py:76
  135.2 2.7 %collective-permute-start.18 = (bf16[4,64,256]{2,1,0:T(8,128)(2,1)S(1)}, bf16[4,64,256]{2,1,0:T(8,128)(2,1)S(1)}, u32[]{:S(2)}, u32[]{:S(2)}) collective-permute-start(bf16[4,64,256]{2,1,0:T(8,128)(2,1)S(1)} %bitcast.127), channel_id=1, source_target_pairs={{0,3},{1,0},{2,1},{3,2},{4,7},{5,4},{6,5},{7,6},{8,11},{9,8},{10,9... | collective-permute-start | bytes 393224 | tf_op jit(solution)/shard_map/ppermute | solution.py:76
  138.0 1.0 collective-permute-done.17
  139.0 2.2 %collective-permute-done.18 = bf16[4,64,256]{2,1,0:T(8,128)(2,1)S(1)} collective-permute-done((bf16[4,64,256]{2,1,0:T(8,128)(2,1)S(1)}, bf16[4,64,256]{2,1,0:T(8,128)(2,1)S(1)}, u32[]{:S(2)}, u32[]{:S(2)}) %collective-permute-start.18) | collective-permute-done | bytes 131104 | tf_op jit(solution)/shard_map/ppermute | solution.py:76
  141.4 7.4 %collective-permute-start.19 = (bf16[16,64,256]{2,1,0:T(8,128)(2,1)S(1)}, bf16[16,64,256]{2,1,0:T(8,128)(2,1)S(1)}, u32[]{:S(2)}, u32[]{:S(2)}) collective-permute-start(bf16[16,64,256]{2,1,0:T(8,128)(2,1)S(1)} %bitcast.118), channel_id=1, source_target_pairs={{0,32},{1,33},{2,34},{3,35},{4,36},{5,37},{6,38},{7,39},{8,40},{9,... | collective-permute-start | bytes 1572872 | tf_op jit(solution)/shard_map/ppermute | solution.py:76
  149.0 0.3 fusion.78
  149.3 1.0 collective-permute-done.19
  150.3 0.3 fusion.15
  150.9 1.2 copy.57
  152.1 3.8 %all-to-all-start.4 = ((bf16[16,160,128]{2,1,0:T(8,128)(2,1)}), bf16[16,160,128]{2,1,0:T(8,128)(2,1)S(1)}, u32[]{:S(2)}, u32[]{:S(2)}) async-start(bf16[16,160,128]{2,1,0:T(8,128)(2,1)} %copy.57), calls=%async_computation.4 | async-start | bytes 1310720 | tf_op jit(solution)/shard_map/all_to_all | solution.py:80
  156.8 2.6 %collective-permute-start.12 = (bf16[160,256]{1,0:T(8,128)(2,1)S(1)}, bf16[160,256]{1,0:T(8,128)(2,1)S(1)}, u32[]{:S(2)}, u32[]{:S(2)}) collective-permute-start(bf16[160,256]{1,0:T(8,128)(2,1)S(1)} %select_bitcast_fusion), channel_id=1, source_target_pairs={{0,32},{1,33},{2,34},{3,35},{4,36},{5,37},{6,38},{7,39},{8,40},{9,... | collective-permute-start | bytes 245768 | tf_op jit(solution)/shard_map/ppermute | solution.py:76
  159.4 8.0 %all-to-all-done.4 = bf16[16,160,128]{2,1,0:T(8,128)(2,1)S(1)} async-done(((bf16[16,160,128]{2,1,0:T(8,128)(2,1)}), bf16[16,160,128]{2,1,0:T(8,128)(2,1)S(1)}, u32[]{:S(2)}, u32[]{:S(2)}) %all-to-all-start.4) | async-done | bytes 655392 | tf_op jit(solution)/shard_map/all_to_all | solution.py:80
  167.4 0.2 fusion.70
  167.9 0.4 fusion.64
  168.3 4.3 %collective-permute-start.20 = (bf16[160,64]{1,0:T(8,128)(2,1)S(1)}, bf16[160,64]{1,0:T(8,128)(2,1)S(1)}, u32[]{:S(2)}, u32[]{:S(2)}) collective-permute-start(bf16[160,64]{1,0:T(8,128)(2,1)S(1)} %fusion.64), channel_id=1, source_target_pairs={{0,32},{1,33},{2,34},{3,35},{4,36},{5,37},{6,38},{7,39},{8,40},{9,... | collective-permute-start | bytes 61448 | tf_op jit(solution)/shard_map/ppermute | solution.py:76
  172.7 0.9 convolution_convert_fusion
  173.6 0.9 convolution_convert_fusion.1
  (93 shorter events, 3.3 us)
Async XLA Ops:
  1.7 36.9 %collective-permute-start.7 = (bf16[256,256]{1,0:T(8,128)(2,1)S(1)}, bf16[256,256]{1,0:T(8,128)(2,1)S(1)}, u32[]{:S(2)}, u32[]{:S(2)}) collective-permute-start(bf16[256,256]{1,0:T(8,128)(2,1)S(1)} %get-tuple-element.38), channel_id=1, source_target_pairs={{0,400},{1,401},{2,402},{3,403},{4,404},{5,405},{6,406},{7,407},{8... | collective-permute-start | bytes 393224 | tf_op jit(solution)/shard_map/ppermute | solution.py:76
  2.4 39.3 %collective-permute-start.6 = (bf16[256,256]{1,0:T(8,128)(2,1)S(1)}, bf16[256,256]{1,0:T(8,128)(2,1)S(1)}, u32[]{:S(2)}, u32[]{:S(2)}) collective-permute-start(bf16[256,256]{1,0:T(8,128)(2,1)S(1)} %get-tuple-element.38), channel_id=1, source_target_pairs={{0,336},{1,337},{2,338},{3,339},{4,340},{5,341},{6,342},{7,343},{8... | collective-permute-start | bytes 393224 | tf_op jit(solution)/shard_map/ppermute | solution.py:76
  13.2 28.5 %collective-permute-start.8 = (bf16[256,256]{1,0:T(8,128)(2,1)S(1)}, bf16[256,256]{1,0:T(8,128)(2,1)S(1)}, u32[]{:S(2)}, u32[]{:S(2)}) collective-permute-start(bf16[256,256]{1,0:T(8,128)(2,1)S(1)} %get-tuple-element.38), channel_id=1, source_target_pairs={{0,464},{1,465},{2,466},{3,467},{4,468},{5,469},{6,470},{7,471},{8... | collective-permute-start | bytes 393224 | tf_op jit(solution)/shard_map/ppermute | solution.py:76
  14.9 7.7 %collective-permute-start = (bf16[128,512]{1,0:T(8,128)(2,1)S(1)}, bf16[128,512]{1,0:T(8,128)(2,1)S(1)}, u32[]{:S(2)}, u32[]{:S(2)}) collective-permute-start(bf16[128,512]{1,0:T(8,128)(2,1)S(1)} %constant_dynamic-slice_fusion.14), channel_id=1, source_target_pairs={{0,32},{1,33},{2,34},{3,35},{4,36},{5,37},{6,38},{7,39},{8,40},{9,... | collective-permute-start | bytes 393224 | tf_op jit(solution)/shard_map/ppermute | solution.py:76
  17.7 6.1 %collective-permute-start.5 = (bf16[256,256]{1,0:T(8,128)(2,1)S(1)}, bf16[256,256]{1,0:T(8,128)(2,1)S(1)}, u32[]{:S(2)}, u32[]{:S(2)}) collective-permute-start(bf16[256,256]{1,0:T(8,128)(2,1)S(1)} %get-tuple-element.37), channel_id=1, source_target_pairs={{0,272},{1,273},{2,274},{3,275},{4,276},{5,277},{6,278},{7,279},{8... | collective-permute-start | bytes 393224 | tf_op jit(solution)/shard_map/ppermute | solution.py:76
  22.5 19.2 %collective-permute-start.4 = (bf16[256,256]{1,0:T(8,128)(2,1)S(1)}, bf16[256,256]{1,0:T(8,128)(2,1)S(1)}, u32[]{:S(2)}, u32[]{:S(2)}) collective-permute-start(bf16[256,256]{1,0:T(8,128)(2,1)S(1)} %get-tuple-element.18), channel_id=1, source_target_pairs={{0,192},{1,193},{2,194},{3,195},{4,196},{5,197},{6,198},{7,199},{8... | collective-permute-start | bytes 393224 | tf_op jit(solution)/shard_map/ppermute | solution.py:76
  23.8 17.9 %collective-permute-start.3 = (bf16[256,256]{1,0:T(8,128)(2,1)S(1)}, bf16[256,256]{1,0:T(8,128)(2,1)S(1)}, u32[]{:S(2)}, u32[]{:S(2)}) collective-permute-start(bf16[256,256]{1,0:T(8,128)(2,1)S(1)} %get-tuple-element.18), channel_id=1, source_target_pairs={{0,128},{1,129},{2,130},{3,131},{4,132},{5,133},{6,134},{7,135},{8... | collective-permute-start | bytes 393224 | tf_op jit(solution)/shard_map/ppermute | solution.py:76
  38.6 5.7 %collective-permute-start.2 = (bf16[256,256]{1,0:T(8,128)(2,1)S(1)}, bf16[256,256]{1,0:T(8,128)(2,1)S(1)}, u32[]{:S(2)}, u32[]{:S(2)}) collective-permute-start(bf16[256,256]{1,0:T(8,128)(2,1)S(1)} %get-tuple-element.18), channel_id=1, source_target_pairs={{0,64},{1,65},{2,66},{3,67},{4,68},{5,69},{6,70},{7,71},{8,72},{9,... | collective-permute-start | bytes 393224 | tf_op jit(solution)/shard_map/ppermute | solution.py:76
  45.4 39.5 %all-to-all-start = ((bf16[16,128,256]{2,1,0:T(8,128)(2,1)}), bf16[16,128,256]{2,1,0:T(8,128)(2,1)S(1)}, u32[]{:S(2)}, u32[]{:S(2)}) async-start(bf16[16,128,256]{2,1,0:T(8,128)(2,1)} %bitcast.2), calls=%async_computation | async-start | bytes 2097152 | tf_op jit(solution)/shard_map/all_to_all | solution.py:80
  52.8 6.7 %collective-permute-start.1 = (bf16[256,640]{1,0:T(8,128)(2,1)S(1)}, bf16[256,640]{1,0:T(8,128)(2,1)S(1)}, u32[]{:S(2)}, u32[]{:S(2)}) collective-permute-start(bf16[256,640]{1,0:T(8,128)(2,1)S(1)} %fusion.35), channel_id=1, source_target_pairs={{0,32},{1,33},{2,34},{3,35},{4,36},{5,37},{6,38},{7,39},{8,40},{9,... | collective-permute-start | bytes 983048 | tf_op jit(solution)/shard_map/ppermute | solution.py:76
  57.5 5.3 %collective-permute-start.9 = (bf16[2048,256]{1,0:T(8,128)(2,1)S(1)}, bf16[2048,256]{1,0:T(8,128)(2,1)S(1)}, u32[]{:S(2)}, u32[]{:S(2)}) collective-permute-start(bf16[2048,256]{1,0:T(8,128)(2,1)S(1)} %constant_dynamic-update-slice_fusion), channel_id=1, source_target_pairs={{0,32},{1,33},{2,34},{3,35},{4,36},{5,37},{6,38},{7,39},{8,40},{9,... | collective-permute-start | bytes 3145736 | tf_op jit(solution)/shard_map/ppermute | solution.py:76
  65.8 19.1 %collective-permute-start.10 = (bf16[4,160,128]{2,1,0:T(8,128)(2,1)S(1)}, bf16[4,160,128]{2,1,0:T(8,128)(2,1)S(1)}, u32[]{:S(2)}, u32[]{:S(2)}) collective-permute-start(bf16[4,160,128]{2,1,0:T(8,128)(2,1)S(1)} %pad_maximum_fusion.6), channel_id=1, source_target_pairs={{0,256},{1,257},{2,258},{3,259},{4,260},{5,261},{6,262},{7,263},{8... | collective-permute-start | bytes 491528 | tf_op jit(solution)/shard_map/ppermute | solution.py:76
  85.8 12.7 %all-to-all-start.1 = ((bf16[4,2,320,128]{3,2,1,0:T(8,128)(2,1)}), bf16[4,2,320,128]{3,2,1,0:T(8,128)(2,1)S(1)}, u32[]{:S(2)}, u32[]{:S(2)}) async-start(bf16[4,2,320,128]{3,2,1,0:T(8,128)(2,1)} %broadcast_in_dim.109), calls=%async_computation.1 | async-start | bytes 1310720 | tf_op jit(solution)/shard_map/all_to_all | solution.py:80
  89.8 9.3 %collective-permute-start.11 = (bf16[4,512,256]{2,1,0:T(8,128)(2,1)S(1)}, bf16[4,512,256]{2,1,0:T(8,128)(2,1)S(1)}, u32[]{:S(2)}, u32[]{:S(2)}) collective-permute-start(bf16[4,512,256]{2,1,0:T(8,128)(2,1)S(1)} %bitcast.116), channel_id=1, source_target_pairs={{0,32},{1,33},{2,34},{3,35},{4,36},{5,37},{6,38},{7,39},{8,40},{9,... | collective-permute-start | bytes 3145736 | tf_op jit(solution)/shard_map/ppermute | solution.py:76
  99.1 5.4 %dynamic-slice-start = ((f32[8192]{0:T(1024)}, s32[]{:T(128)}), f32[4096]{0:T(1024)S(1)}, s32[]{:S(2)}) async-start(f32[8192]{0:T(1024)} %param.13, s32[]{:T(128)} %select_n.444), calls=%async_computation.5 | async-start | bytes 33280 | tf_op jit(solution)/shard_map/dynamic_slice | solution.py:193
  99.1 5.4 %copy-start = (bf16[8192,64]{0,1:T(8,128)(2,1)S(1)}, bf16[8192,64]{0,1:T(8,128)(2,1)}, u32[]{:S(2)}) copy-start(bf16[8192,64]{0,1:T(8,128)(2,1)} %param.14) | copy-start | bytes 3145732
  100.5 14.9 %all-to-all-start.2 = ((bf16[4,320,256]{2,1,0:T(8,128)(2,1)}), bf16[4,320,256]{2,1,0:T(8,128)(2,1)S(1)}, u32[]{:S(2)}, u32[]{:S(2)}) async-start(bf16[4,320,256]{2,1,0:T(8,128)(2,1)} %fusion.14), calls=%async_computation.2 | async-start | bytes 1310720 | tf_op jit(solution)/shard_map/all_to_all | solution.py:80
  105.2 21.7 %collective-permute-start.13 = (bf16[4,64,256]{2,0,1:T(4,128)(2,1)S(1)}, bf16[4,64,256]{2,0,1:T(4,128)(2,1)S(1)}, u32[]{:S(2)}, u32[]{:S(2)}) collective-permute-start(bf16[4,64,256]{2,0,1:T(4,128)(2,1)S(1)} %get-tuple-element.61), channel_id=1, source_target_pairs={{0,4},{1,5},{2,6},{3,7},{4,8},{5,9},{6,10},{7,11},{8,12},{9,13},{1... | collective-permute-start | bytes 393224 | tf_op jit(solution)/shard_map/ppermute | solution.py:76
  108.6 18.3 %collective-permute-start.15 = (bf16[4,64,256]{2,0,1:T(4,128)(2,1)S(1)}, bf16[4,64,256]{2,0,1:T(4,128)(2,1)S(1)}, u32[]{:S(2)}, u32[]{:S(2)}) collective-permute-start(bf16[4,64,256]{2,0,1:T(4,128)(2,1)S(1)} %get-tuple-element.62), channel_id=1, source_target_pairs={{0,12},{1,13},{2,14},{3,15},{4,0},{5,1},{6,2},{7,3},{8,4},{9,5},{1... | collective-permute-start | bytes 393224 | tf_op jit(solution)/shard_map/ppermute | solution.py:76
  111.7 15.2 %collective-permute-start.14 = (bf16[4,64,256]{2,0,1:T(4,128)(2,1)S(1)}, bf16[4,64,256]{2,0,1:T(4,128)(2,1)S(1)}, u32[]{:S(2)}, u32[]{:S(2)}) collective-permute-start(bf16[4,64,256]{2,0,1:T(4,128)(2,1)S(1)} %get-tuple-element.63), channel_id=1, source_target_pairs={{0,8},{1,9},{2,10},{3,11},{4,12},{5,13},{6,14},{7,15},{8,0},{9,1},... | collective-permute-start | bytes 393224 | tf_op jit(solution)/shard_map/ppermute | solution.py:76
  116.3 32.5 %all-to-all-start.3 = ((bf16[4,160,256]{2,1,0:T(8,128)(2,1)}), bf16[4,160,256]{2,1,0:T(8,128)(2,1)S(1)}, u32[]{:S(2)}, u32[]{:S(2)}) async-start(bf16[4,160,256]{2,1,0:T(8,128)(2,1)} %pad_maximum_fusion.4), calls=%async_computation.3 | async-start | bytes 655360 | tf_op jit(solution)/shard_map/all_to_all | solution.py:80
  129.3 8.7 %collective-permute-start.16 = (bf16[4,64,256]{2,1,0:T(8,128)(2,1)S(1)}, bf16[4,64,256]{2,1,0:T(8,128)(2,1)S(1)}, u32[]{:S(2)}, u32[]{:S(2)}) collective-permute-start(bf16[4,64,256]{2,1,0:T(8,128)(2,1)S(1)} %bitcast.129), channel_id=1, source_target_pairs={{0,1},{1,2},{2,3},{3,0},{4,5},{5,6},{6,7},{7,4},{8,9},{9,10},{10,1... | collective-permute-start | bytes 393224 | tf_op jit(solution)/shard_map/ppermute | solution.py:76
  131.5 7.5 %collective-permute-start.17 = (bf16[4,64,256]{2,1,0:T(8,128)(2,1)S(1)}, bf16[4,64,256]{2,1,0:T(8,128)(2,1)S(1)}, u32[]{:S(2)}, u32[]{:S(2)}) collective-permute-start(bf16[4,64,256]{2,1,0:T(8,128)(2,1)S(1)} %bitcast.128), channel_id=1, source_target_pairs={{0,2},{1,3},{2,0},{3,1},{4,6},{5,7},{6,4},{7,5},{8,10},{9,11},{10,... | collective-permute-start | bytes 393224 | tf_op jit(solution)/shard_map/ppermute | solution.py:76
  135.2 6.0 %collective-permute-start.18 = (bf16[4,64,256]{2,1,0:T(8,128)(2,1)S(1)}, bf16[4,64,256]{2,1,0:T(8,128)(2,1)S(1)}, u32[]{:S(2)}, u32[]{:S(2)}) collective-permute-start(bf16[4,64,256]{2,1,0:T(8,128)(2,1)S(1)} %bitcast.127), channel_id=1, source_target_pairs={{0,3},{1,0},{2,1},{3,2},{4,7},{5,4},{6,5},{7,6},{8,11},{9,8},{10,9... | collective-permute-start | bytes 393224 | tf_op jit(solution)/shard_map/ppermute | solution.py:76
  141.4 8.9 %collective-permute-start.19 = (bf16[16,64,256]{2,1,0:T(8,128)(2,1)S(1)}, bf16[16,64,256]{2,1,0:T(8,128)(2,1)S(1)}, u32[]{:S(2)}, u32[]{:S(2)}) collective-permute-start(bf16[16,64,256]{2,1,0:T(8,128)(2,1)S(1)} %bitcast.118), channel_id=1, source_target_pairs={{0,32},{1,33},{2,34},{3,35},{4,36},{5,37},{6,38},{7,39},{8,40},{9,... | collective-permute-start | bytes 1572872 | tf_op jit(solution)/shard_map/ppermute | solution.py:76
  152.1 15.2 %all-to-all-start.4 = ((bf16[16,160,128]{2,1,0:T(8,128)(2,1)}), bf16[16,160,128]{2,1,0:T(8,128)(2,1)S(1)}, u32[]{:S(2)}, u32[]{:S(2)}) async-start(bf16[16,160,128]{2,1,0:T(8,128)(2,1)} %copy.57), calls=%async_computation.4 | async-start | bytes 1310720 | tf_op jit(solution)/shard_map/all_to_all | solution.py:80
  156.8 15.8 %collective-permute-start.12 = (bf16[160,256]{1,0:T(8,128)(2,1)S(1)}, bf16[160,256]{1,0:T(8,128)(2,1)S(1)}, u32[]{:S(2)}, u32[]{:S(2)}) collective-permute-start(bf16[160,256]{1,0:T(8,128)(2,1)S(1)} %select_bitcast_fusion), channel_id=1, source_target_pairs={{0,32},{1,33},{2,34},{3,35},{4,36},{5,37},{6,38},{7,39},{8,40},{9,... | collective-permute-start | bytes 245768 | tf_op jit(solution)/shard_map/ppermute | solution.py:76
  168.3 5.3 %collective-permute-start.20 = (bf16[160,64]{1,0:T(8,128)(2,1)S(1)}, bf16[160,64]{1,0:T(8,128)(2,1)S(1)}, u32[]{:S(2)}, u32[]{:S(2)}) collective-permute-start(bf16[160,64]{1,0:T(8,128)(2,1)S(1)} %fusion.64), channel_id=1, source_target_pairs={{0,32},{1,33},{2,34},{3,35},{4,36},{5,37},{6,38},{7,39},{8,40},{9,... | collective-permute-start | bytes 61448 | tf_op jit(solution)/shard_map/ppermute | solution.py:76

commit v6 on v5

--- a/solution.py
+++ b/solution.py
@@ -125,8 +125,10 @@
     far_head = (1 - zh) * (KVH // ZH) + plane // NY
     own_kv = lax.dynamic_slice_in_dim(keys_values, head * 2 * HD, 2 * HD, 1)
     far_kv = lax.dynamic_slice_in_dim(keys_values, far_head * 2 * HD, 2 * HD, 1)
-    sent = {4: jnp.where(zl >= 2, own_kv, far_kv)}
-    blocks = [own_kv] + [send(sent.get(k, own_kv if k < 4 else far_kv), BACK[k]) for k in range(1, ZL)]
+    blocks = [own_kv] + [send(own_kv, BACK[k]) for k in (1, 2, 3)]
+    mixed_kv = jnp.where(zl >= 2, own_kv, far_kv)
+    far_kv, mixed_kv, _ = lax.optimization_barrier((far_kv, mixed_kv, blocks[1]))
+    blocks += [send(mixed_kv, BACK[4])] + [send(far_kv, BACK[k]) for k in range(5, ZL)]
 
     kept_rows = lax.dynamic_slice_in_dim(out_weight, core * HD, HD, 0)
     given_rows = lax.dynamic_slice_in_dim(out_weight, (1 - core) * HD, HD, 0)

time: 176 us -> 167 us (0.949)
  starting transfers between devices: 111 us -> 95.6 us
  waiting for transfers between devices: 34.7 us -> 41.4 us
    ppermute x21, starting transfers between devices: 81.3 us -> 72 us  [send(): return lax.ppermute(x, AXES, table)]
    all_to_all x5, starting transfers between devices: 29.7 us -> 23.5 us  [exchange(): return lax.all_to_all(x, axes, 0, 0, tiled=True, axis_index_groups=groups)]
    ppermute x21, waiting for transfers between devices: 21.8 us -> 26 us  [send(): return lax.ppermute(x, AXES, table)]
    all_to_all x5, waiting for transfers between devices: 12.9 us -> 15.4 us  [exchange(): return lax.all_to_all(x, axes, 0, 0, tiled=True, axis_index_groups=groups)]
  transfers between devices with their start and end apart: 26 -> 26, of which waited for: 7 -> 8; matrix products, arithmetic and copies ran while one was open for 11% -> 12% of each run, Pallas kernels for 0% -> 0%
where the time goes in v6:
time: 167 us; the launch traced here: 166 us
  starting transfers between devices  95.6 us (57%)
  waiting for transfers between devices  41.4 us (25%)
  other arithmetic  11.1 us (7%)
  matrix products  7.52 us (5%)
  local copies, waits for them, and re-layouts  6.96 us (4%)
  between operations  3.19 us (2%)
    ppermute x21, starting transfers between devices, send(): return lax.ppermute(x, AXES, table)  72 us
    ppermute x21, waiting for transfers between devices, send(): return lax.ppermute(x, AXES, table)  26 us
    all_to_all x5, starting transfers between devices, exchange(): return lax.all_to_all(x, axes, 0, 0, tiled=True, axis_index_groups=groups)  23.5 us
    all_to_all x5, waiting for transfers between devices, exchange(): return lax.all_to_all(x, axes, 0, 0, tiled=True, axis_index_groups=groups)  15.4 us
  transfers between devices with their start and end apart: 26, of which 8 were waited for; matrix products, arithmetic and copies ran while one was open for 12% of the time, Pallas kernels for 0%

profile of v6, /device:TPU:65, one launch (start us, length us, event | category | flops | bytes accessed | tf_op | source)
XLA Modules:
  0.0 165.8 jit_solution(12732673014567582844)
XLA Ops:
  0.7 1.0 broadcast_select_fusion
  1.7 7.5 %collective-permute-start.4 = (bf16[256,256]{1,0:T(8,128)(2,1)S(1)}, bf16[256,256]{1,0:T(8,128)(2,1)S(1)}, u32[]{:S(2)}, u32[]{:S(2)}) collective-permute-start(bf16[256,256]{1,0:T(8,128)(2,1)S(1)} %get-tuple-element.22), channel_id=1, source_target_pairs={{0,192},{1,193},{2,194},{3,195},{4,196},{5,197},{6,198},{7,199},{8... | collective-permute-start | bytes 393224 | tf_op jit(solution)/shard_map/ppermute | solution.py:76
  9.2 4.9 %collective-permute-start.3 = (bf16[256,256]{1,0:T(8,128)(2,1)S(1)}, bf16[256,256]{1,0:T(8,128)(2,1)S(1)}, u32[]{:S(2)}, u32[]{:S(2)}) collective-permute-start(bf16[256,256]{1,0:T(8,128)(2,1)S(1)} %get-tuple-element.22), channel_id=1, source_target_pairs={{0,128},{1,129},{2,130},{3,131},{4,132},{5,133},{6,134},{7,135},{8... | collective-permute-start | bytes 393224 | tf_op jit(solution)/shard_map/ppermute | solution.py:76
  14.1 1.9 %collective-permute-start.2 = (bf16[256,256]{1,0:T(8,128)(2,1)S(1)}, bf16[256,256]{1,0:T(8,128)(2,1)S(1)}, u32[]{:S(2)}, u32[]{:S(2)}) collective-permute-start(bf16[256,256]{1,0:T(8,128)(2,1)S(1)} %get-tuple-element.22), channel_id=1, source_target_pairs={{0,64},{1,65},{2,66},{3,67},{4,68},{5,69},{6,70},{7,71},{8,72},{9,... | collective-permute-start | bytes 393224 | tf_op jit(solution)/shard_map/ppermute | solution.py:76
  16.0 0.9 constant_dynamic-slice_fusion.14
  17.0 3.1 %collective-permute-start = (bf16[128,512]{1,0:T(8,128)(2,1)S(1)}, bf16[128,512]{1,0:T(8,128)(2,1)S(1)}, u32[]{:S(2)}, u32[]{:S(2)}) collective-permute-start(bf16[128,512]{1,0:T(8,128)(2,1)S(1)} %constant_dynamic-slice_fusion.14), channel_id=1, source_target_pairs={{0,32},{1,33},{2,34},{3,35},{4,36},{5,37},{6,38},{7,39},{8,40},{9,... | collective-permute-start | bytes 393224 | tf_op jit(solution)/shard_map/ppermute | solution.py:76
  20.8 0.8 select_reduce_fusion
  21.7 0.7 fusion.100
  22.6 1.0 fusion.35
  23.6 0.8 collective-permute-done.2
  24.4 0.7 collective-permute-start.8
  25.0 0.7 collective-permute-start.7
  25.7 1.3 collective-permute-start.6
  27.0 7.6 %collective-permute-start.5 = (bf16[256,256]{1,0:T(8,128)(2,1)S(1)}, bf16[256,256]{1,0:T(8,128)(2,1)S(1)}, u32[]{:S(2)}, u32[]{:S(2)}) collective-permute-start(bf16[256,256]{1,0:T(8,128)(2,1)S(1)} %get-tuple-element.20), channel_id=1, source_target_pairs={{0,272},{1,273},{2,274},{3,275},{4,276},{5,277},{6,278},{7,279},{8... | collective-permute-start | bytes 393224 | tf_op jit(solution)/shard_map/ppermute | solution.py:76
  34.6 1.0 broadcast_select_fusion.2
  35.8 1.1 broadcast_in_dim.68
  36.9 8.2 %all-to-all-start = ((bf16[16,128,256]{2,1,0:T(8,128)(2,1)}), bf16[16,128,256]{2,1,0:T(8,128)(2,1)S(1)}, u32[]{:S(2)}, u32[]{:S(2)}) async-start(bf16[16,128,256]{2,1,0:T(8,128)(2,1)} %bitcast.2), calls=%async_computation | async-start | bytes 2097152 | tf_op jit(solution)/shard_map/all_to_all | solution.py:80
  45.1 3.7 %collective-permute-start.1 = (bf16[256,640]{1,0:T(8,128)(2,1)S(1)}, bf16[256,640]{1,0:T(8,128)(2,1)S(1)}, u32[]{:S(2)}, u32[]{:S(2)}) collective-permute-start(bf16[256,640]{1,0:T(8,128)(2,1)S(1)} %fusion.35), channel_id=1, source_target_pairs={{0,32},{1,33},{2,34},{3,35},{4,36},{5,37},{6,38},{7,39},{8,40},{9,... | collective-permute-start | bytes 983048 | tf_op jit(solution)/shard_map/ppermute | solution.py:76
  49.0 1.9 %collective-permute-start.9 = (bf16[2048,256]{1,0:T(8,128)(2,1)S(1)}, bf16[2048,256]{1,0:T(8,128)(2,1)S(1)}, u32[]{:S(2)}, u32[]{:S(2)}) collective-permute-start(bf16[2048,256]{1,0:T(8,128)(2,1)S(1)} %constant_dynamic-update-slice_fusion), channel_id=1, source_target_pairs={{0,32},{1,33},{2,34},{3,35},{4,36},{5,37},{6,38},{7,39},{8,40},{9,... | collective-permute-start | bytes 3145736 | tf_op jit(solution)/shard_map/ppermute | solution.py:76
  51.0 0.3 maximum_select_fusion
  51.3 0.7 convert_reduce_fusion.2
  52.1 0.7 add_select_fusion.2
  52.7 0.3 fusion.113
  53.4 0.9 fusion.114
  54.3 0.9 fusion.115
  55.2 0.9 fusion.4
  56.1 0.6 fusion.9
  56.6 0.6 fusion.22
  57.3 3.0 %collective-permute-start.10 = (bf16[4,160,128]{2,1,0:T(8,128)(2,1)S(1)}, bf16[4,160,128]{2,1,0:T(8,128)(2,1)S(1)}, u32[]{:S(2)}, u32[]{:S(2)}) collective-permute-start(bf16[4,160,128]{2,1,0:T(8,128)(2,1)S(1)} %pad_maximum_fusion.6), channel_id=1, source_target_pairs={{0,256},{1,257},{2,258},{3,259},{4,260},{5,261},{6,262},{7,263},{8... | collective-permute-start | bytes 491528 | tf_op jit(solution)/shard_map/ppermute | solution.py:76
  60.5 20.7 %collective-permute-done.10 = bf16[4,160,128]{2,1,0:T(8,128)(2,1)S(1)} collective-permute-done((bf16[4,160,128]{2,1,0:T(8,128)(2,1)S(1)}, bf16[4,160,128]{2,1,0:T(8,128)(2,1)S(1)}, u32[]{:S(2)}, u32[]{:S(2)}) %collective-permute-start.10) | collective-permute-done | bytes 163872 | tf_op jit(solution)/shard_map/ppermute | solution.py:76
  81.3 0.9 broadcast_in_dim.109
  82.2 4.3 %all-to-all-start.1 = ((bf16[4,2,320,128]{3,2,1,0:T(8,128)(2,1)}), bf16[4,2,320,128]{3,2,1,0:T(8,128)(2,1)S(1)}, u32[]{:S(2)}, u32[]{:S(2)}) async-start(bf16[4,2,320,128]{3,2,1,0:T(8,128)(2,1)} %broadcast_in_dim.109), calls=%async_computation.1 | async-start | bytes 1310720 | tf_op jit(solution)/shard_map/all_to_all | solution.py:80
  86.5 2.7 %collective-permute-start.11 = (bf16[4,512,256]{2,1,0:T(8,128)(2,1)S(1)}, bf16[4,512,256]{2,1,0:T(8,128)(2,1)S(1)}, u32[]{:S(2)}, u32[]{:S(2)}) collective-permute-start(bf16[4,512,256]{2,1,0:T(8,128)(2,1)S(1)} %bitcast.116), channel_id=1, source_target_pairs={{0,32},{1,33},{2,34},{3,35},{4,36},{5,37},{6,38},{7,39},{8,40},{9,... | collective-permute-start | bytes 3145736 | tf_op jit(solution)/shard_map/ppermute | solution.py:76
  89.3 7.4 %all-to-all-done.1 = bf16[4,2,320,128]{3,2,1,0:T(8,128)(2,1)S(1)} async-done(((bf16[4,2,320,128]{3,2,1,0:T(8,128)(2,1)}), bf16[4,2,320,128]{3,2,1,0:T(8,128)(2,1)S(1)}, u32[]{:S(2)}, u32[]{:S(2)}) %all-to-all-start.1) | async-done | bytes 655392 | tf_op jit(solution)/shard_map/all_to_all | solution.py:80
  96.8 0.5 fusion.36
  97.3 1.4 fusion.14
  98.7 4.0 %all-to-all-start.2 = ((bf16[4,320,256]{2,1,0:T(8,128)(2,1)}), bf16[4,320,256]{2,1,0:T(8,128)(2,1)S(1)}, u32[]{:S(2)}, u32[]{:S(2)}) async-start(bf16[4,320,256]{2,1,0:T(8,128)(2,1)} %fusion.14), calls=%async_computation.2 | async-start | bytes 1310720 | tf_op jit(solution)/shard_map/all_to_all | solution.py:80
  102.8 0.4 reshape.219
  103.4 3.4 %collective-permute-start.13 = (bf16[4,64,256]{2,0,1:T(4,128)(2,1)S(1)}, bf16[4,64,256]{2,0,1:T(4,128)(2,1)S(1)}, u32[]{:S(2)}, u32[]{:S(2)}) collective-permute-start(bf16[4,64,256]{2,0,1:T(4,128)(2,1)S(1)} %get-tuple-element.65), channel_id=1, source_target_pairs={{0,4},{1,5},{2,6},{3,7},{4,8},{5,9},{6,10},{7,11},{8,12},{9,13},{1... | collective-permute-start | bytes 393224 | tf_op jit(solution)/shard_map/ppermute | solution.py:76
  106.7 3.1 %collective-permute-start.15 = (bf16[4,64,256]{2,0,1:T(4,128)(2,1)S(1)}, bf16[4,64,256]{2,0,1:T(4,128)(2,1)S(1)}, u32[]{:S(2)}, u32[]{:S(2)}) collective-permute-start(bf16[4,64,256]{2,0,1:T(4,128)(2,1)S(1)} %get-tuple-element.66), channel_id=1, source_target_pairs={{0,12},{1,13},{2,14},{3,15},{4,0},{5,1},{6,2},{7,3},{8,4},{9,5},{1... | collective-permute-start | bytes 393224 | tf_op jit(solution)/shard_map/ppermute | solution.py:76
  109.9 3.7 %collective-permute-start.14 = (bf16[4,64,256]{2,0,1:T(4,128)(2,1)S(1)}, bf16[4,64,256]{2,0,1:T(4,128)(2,1)S(1)}, u32[]{:S(2)}, u32[]{:S(2)}) collective-permute-start(bf16[4,64,256]{2,0,1:T(4,128)(2,1)S(1)} %get-tuple-element.67), channel_id=1, source_target_pairs={{0,8},{1,9},{2,10},{3,11},{4,12},{5,13},{6,14},{7,15},{8,0},{9,1},... | collective-permute-start | bytes 393224 | tf_op jit(solution)/shard_map/ppermute | solution.py:76
  113.7 0.7 pad_maximum_fusion.4
  114.4 3.5 %all-to-all-start.3 = ((bf16[4,160,256]{2,1,0:T(8,128)(2,1)}), bf16[4,160,256]{2,1,0:T(8,128)(2,1)S(1)}, u32[]{:S(2)}, u32[]{:S(2)}) async-start(bf16[4,160,256]{2,1,0:T(8,128)(2,1)} %pad_maximum_fusion.4), calls=%async_computation.3 | async-start | bytes 655360 | tf_op jit(solution)/shard_map/all_to_all | solution.py:80
  118.1 0.5 pad_maximum_fusion.1
  118.8 0.5 pad_maximum_fusion.2
  119.2 1.1 constant_dynamic-slice_fusion.7
  120.4 2.2 %collective-permute-start.16 = (bf16[4,64,256]{2,1,0:T(8,128)(2,1)S(1)}, bf16[4,64,256]{2,1,0:T(8,128)(2,1)S(1)}, u32[]{:S(2)}, u32[]{:S(2)}) collective-permute-start(bf16[4,64,256]{2,1,0:T(8,128)(2,1)S(1)} %bitcast.129), channel_id=1, source_target_pairs={{0,1},{1,2},{2,3},{3,0},{4,5},{5,6},{6,7},{7,4},{8,9},{9,10},{10,1... | collective-permute-start | bytes 393224 | tf_op jit(solution)/shard_map/ppermute | solution.py:76
  122.6 3.9 %collective-permute-start.17 = (bf16[4,64,256]{2,1,0:T(8,128)(2,1)S(1)}, bf16[4,64,256]{2,1,0:T(8,128)(2,1)S(1)}, u32[]{:S(2)}, u32[]{:S(2)}) collective-permute-start(bf16[4,64,256]{2,1,0:T(8,128)(2,1)S(1)} %bitcast.128), channel_id=1, source_target_pairs={{0,2},{1,3},{2,0},{3,1},{4,6},{5,7},{6,4},{7,5},{8,10},{9,11},{10,... | collective-permute-start | bytes 393224 | tf_op jit(solution)/shard_map/ppermute | solution.py:76
  126.5 2.5 %collective-permute-start.18 = (bf16[4,64,256]{2,1,0:T(8,128)(2,1)S(1)}, bf16[4,64,256]{2,1,0:T(8,128)(2,1)S(1)}, u32[]{:S(2)}, u32[]{:S(2)}) collective-permute-start(bf16[4,64,256]{2,1,0:T(8,128)(2,1)S(1)} %bitcast.127), channel_id=1, source_target_pairs={{0,3},{1,0},{2,1},{3,2},{4,7},{5,4},{6,5},{7,6},{8,11},{9,8},{10,9... | collective-permute-start | bytes 393224 | tf_op jit(solution)/shard_map/ppermute | solution.py:76
  129.2 1.2 collective-permute-done.17
  130.3 2.2 %collective-permute-done.18 = bf16[4,64,256]{2,1,0:T(8,128)(2,1)S(1)} collective-permute-done((bf16[4,64,256]{2,1,0:T(8,128)(2,1)S(1)}, bf16[4,64,256]{2,1,0:T(8,128)(2,1)S(1)}, u32[]{:S(2)}, u32[]{:S(2)}) %collective-permute-start.18) | collective-permute-done | bytes 131104 | tf_op jit(solution)/shard_map/ppermute | solution.py:76
  132.8 7.5 %collective-permute-start.19 = (bf16[16,64,256]{2,1,0:T(8,128)(2,1)S(1)}, bf16[16,64,256]{2,1,0:T(8,128)(2,1)S(1)}, u32[]{:S(2)}, u32[]{:S(2)}) collective-permute-start(bf16[16,64,256]{2,1,0:T(8,128)(2,1)S(1)} %bitcast.118), channel_id=1, source_target_pairs={{0,32},{1,33},{2,34},{3,35},{4,36},{5,37},{6,38},{7,39},{8,40},{9,... | collective-permute-start | bytes 1572872 | tf_op jit(solution)/shard_map/ppermute | solution.py:76
  140.5 0.3 fusion.78
  140.8 1.0 collective-permute-done.19
  141.8 0.3 fusion.15
  142.3 1.2 copy.57
  143.6 3.6 %all-to-all-start.4 = ((bf16[16,160,128]{2,1,0:T(8,128)(2,1)}), bf16[16,160,128]{2,1,0:T(8,128)(2,1)S(1)}, u32[]{:S(2)}, u32[]{:S(2)}) async-start(bf16[16,160,128]{2,1,0:T(8,128)(2,1)} %copy.57), calls=%async_computation.4 | async-start | bytes 1310720 | tf_op jit(solution)/shard_map/all_to_all | solution.py:80
  148.1 2.5 %collective-permute-start.12 = (bf16[160,256]{1,0:T(8,128)(2,1)S(1)}, bf16[160,256]{1,0:T(8,128)(2,1)S(1)}, u32[]{:S(2)}, u32[]{:S(2)}) collective-permute-start(bf16[160,256]{1,0:T(8,128)(2,1)S(1)} %select_bitcast_fusion), channel_id=1, source_target_pairs={{0,32},{1,33},{2,34},{3,35},{4,36},{5,37},{6,38},{7,39},{8,40},{9,... | collective-permute-start | bytes 245768 | tf_op jit(solution)/shard_map/ppermute | solution.py:76
  150.6 8.0 %all-to-all-done.4 = bf16[16,160,128]{2,1,0:T(8,128)(2,1)S(1)} async-done(((bf16[16,160,128]{2,1,0:T(8,128)(2,1)}), bf16[16,160,128]{2,1,0:T(8,128)(2,1)S(1)}, u32[]{:S(2)}, u32[]{:S(2)}) %all-to-all-start.4) | async-done | bytes 655392 | tf_op jit(solution)/shard_map/all_to_all | solution.py:80
  158.7 0.2 fusion.70
  159.2 0.4 fusion.64
  159.6 4.3 %collective-permute-start.20 = (bf16[160,64]{1,0:T(8,128)(2,1)S(1)}, bf16[160,64]{1,0:T(8,128)(2,1)S(1)}, u32[]{:S(2)}, u32[]{:S(2)}) collective-permute-start(bf16[160,64]{1,0:T(8,128)(2,1)S(1)} %fusion.64), channel_id=1, source_target_pairs={{0,32},{1,33},{2,34},{3,35},{4,36},{5,37},{6,38},{7,39},{8,40},{9,... | collective-permute-start | bytes 61448 | tf_op jit(solution)/shard_map/ppermute | solution.py:76
  163.9 0.9 convolution_convert_fusion
  164.9 0.9 convolution_convert_fusion.1
  (93 shorter events, 3.4 us)
Async XLA Ops:
  1.7 25.3 %collective-permute-start.4 = (bf16[256,256]{1,0:T(8,128)(2,1)S(1)}, bf16[256,256]{1,0:T(8,128)(2,1)S(1)}, u32[]{:S(2)}, u32[]{:S(2)}) collective-permute-start(bf16[256,256]{1,0:T(8,128)(2,1)S(1)} %get-tuple-element.22), channel_id=1, source_target_pairs={{0,192},{1,193},{2,194},{3,195},{4,196},{5,197},{6,198},{7,199},{8... | collective-permute-start | bytes 393224 | tf_op jit(solution)/shard_map/ppermute | solution.py:76
  9.2 35.9 %collective-permute-start.3 = (bf16[256,256]{1,0:T(8,128)(2,1)S(1)}, bf16[256,256]{1,0:T(8,128)(2,1)S(1)}, u32[]{:S(2)}, u32[]{:S(2)}) collective-permute-start(bf16[256,256]{1,0:T(8,128)(2,1)S(1)} %get-tuple-element.22), channel_id=1, source_target_pairs={{0,128},{1,129},{2,130},{3,131},{4,132},{5,133},{6,134},{7,135},{8... | collective-permute-start | bytes 393224 | tf_op jit(solution)/shard_map/ppermute | solution.py:76
  14.1 10.3 %collective-permute-start.2 = (bf16[256,256]{1,0:T(8,128)(2,1)S(1)}, bf16[256,256]{1,0:T(8,128)(2,1)S(1)}, u32[]{:S(2)}, u32[]{:S(2)}) collective-permute-start(bf16[256,256]{1,0:T(8,128)(2,1)S(1)} %get-tuple-element.22), channel_id=1, source_target_pairs={{0,64},{1,65},{2,66},{3,67},{4,68},{5,69},{6,70},{7,71},{8,72},{9,... | collective-permute-start | bytes 393224 | tf_op jit(solution)/shard_map/ppermute | solution.py:76
  17.0 8.8 %collective-permute-start = (bf16[128,512]{1,0:T(8,128)(2,1)S(1)}, bf16[128,512]{1,0:T(8,128)(2,1)S(1)}, u32[]{:S(2)}, u32[]{:S(2)}) collective-permute-start(bf16[128,512]{1,0:T(8,128)(2,1)S(1)} %constant_dynamic-slice_fusion.14), channel_id=1, source_target_pairs={{0,32},{1,33},{2,34},{3,35},{4,36},{5,37},{6,38},{7,39},{8,40},{9,... | collective-permute-start | bytes 393224 | tf_op jit(solution)/shard_map/ppermute | solution.py:76
  24.4 24.5 %collective-permute-start.8 = (bf16[256,256]{1,0:T(8,128)(2,1)S(1)}, bf16[256,256]{1,0:T(8,128)(2,1)S(1)}, u32[]{:S(2)}, u32[]{:S(2)}) collective-permute-start(bf16[256,256]{1,0:T(8,128)(2,1)S(1)} %get-tuple-element.21), channel_id=1, source_target_pairs={{0,464},{1,465},{2,466},{3,467},{4,468},{5,469},{6,470},{7,471},{8... | collective-permute-start | bytes 393224 | tf_op jit(solution)/shard_map/ppermute | solution.py:76
  25.0 23.8 %collective-permute-start.7 = (bf16[256,256]{1,0:T(8,128)(2,1)S(1)}, bf16[256,256]{1,0:T(8,128)(2,1)S(1)}, u32[]{:S(2)}, u32[]{:S(2)}) collective-permute-start(bf16[256,256]{1,0:T(8,128)(2,1)S(1)} %get-tuple-element.21), channel_id=1, source_target_pairs={{0,400},{1,401},{2,402},{3,403},{4,404},{5,405},{6,406},{7,407},{8... | collective-permute-start | bytes 393224 | tf_op jit(solution)/shard_map/ppermute | solution.py:76
  25.7 23.2 %collective-permute-start.6 = (bf16[256,256]{1,0:T(8,128)(2,1)S(1)}, bf16[256,256]{1,0:T(8,128)(2,1)S(1)}, u32[]{:S(2)}, u32[]{:S(2)}) collective-permute-start(bf16[256,256]{1,0:T(8,128)(2,1)S(1)} %get-tuple-element.21), channel_id=1, source_target_pairs={{0,336},{1,337},{2,338},{3,339},{4,340},{5,341},{6,342},{7,343},{8... | collective-permute-start | bytes 393224 | tf_op jit(solution)/shard_map/ppermute | solution.py:76
  27.0 21.8 %collective-permute-start.5 = (bf16[256,256]{1,0:T(8,128)(2,1)S(1)}, bf16[256,256]{1,0:T(8,128)(2,1)S(1)}, u32[]{:S(2)}, u32[]{:S(2)}) collective-permute-start(bf16[256,256]{1,0:T(8,128)(2,1)S(1)} %get-tuple-element.20), channel_id=1, source_target_pairs={{0,272},{1,273},{2,274},{3,275},{4,276},{5,277},{6,278},{7,279},{8... | collective-permute-start | bytes 393224 | tf_op jit(solution)/shard_map/ppermute | solution.py:76
  36.9 44.4 %all-to-all-start = ((bf16[16,128,256]{2,1,0:T(8,128)(2,1)}), bf16[16,128,256]{2,1,0:T(8,128)(2,1)S(1)}, u32[]{:S(2)}, u32[]{:S(2)}) async-start(bf16[16,128,256]{2,1,0:T(8,128)(2,1)} %bitcast.2), calls=%async_computation | async-start | bytes 2097152 | tf_op jit(solution)/shard_map/all_to_all | solution.py:80
  45.1 5.8 %collective-permute-start.1 = (bf16[256,640]{1,0:T(8,128)(2,1)S(1)}, bf16[256,640]{1,0:T(8,128)(2,1)S(1)}, u32[]{:S(2)}, u32[]{:S(2)}) collective-permute-start(bf16[256,640]{1,0:T(8,128)(2,1)S(1)} %fusion.35), channel_id=1, source_target_pairs={{0,32},{1,33},{2,34},{3,35},{4,36},{5,37},{6,38},{7,39},{8,40},{9,... | collective-permute-start | bytes 983048 | tf_op jit(solution)/shard_map/ppermute | solution.py:76
  49.0 5.3 %collective-permute-start.9 = (bf16[2048,256]{1,0:T(8,128)(2,1)S(1)}, bf16[2048,256]{1,0:T(8,128)(2,1)S(1)}, u32[]{:S(2)}, u32[]{:S(2)}) collective-permute-start(bf16[2048,256]{1,0:T(8,128)(2,1)S(1)} %constant_dynamic-update-slice_fusion), channel_id=1, source_target_pairs={{0,32},{1,33},{2,34},{3,35},{4,36},{5,37},{6,38},{7,39},{8,40},{9,... | collective-permute-start | bytes 3145736 | tf_op jit(solution)/shard_map/ppermute | solution.py:76
  57.3 24.0 %collective-permute-start.10 = (bf16[4,160,128]{2,1,0:T(8,128)(2,1)S(1)}, bf16[4,160,128]{2,1,0:T(8,128)(2,1)S(1)}, u32[]{:S(2)}, u32[]{:S(2)}) collective-permute-start(bf16[4,160,128]{2,1,0:T(8,128)(2,1)S(1)} %pad_maximum_fusion.6), channel_id=1, source_target_pairs={{0,256},{1,257},{2,258},{3,259},{4,260},{5,261},{6,262},{7,263},{8... | collective-permute-start | bytes 491528 | tf_op jit(solution)/shard_map/ppermute | solution.py:76
  82.2 14.5 %all-to-all-start.1 = ((bf16[4,2,320,128]{3,2,1,0:T(8,128)(2,1)}), bf16[4,2,320,128]{3,2,1,0:T(8,128)(2,1)S(1)}, u32[]{:S(2)}, u32[]{:S(2)}) async-start(bf16[4,2,320,128]{3,2,1,0:T(8,128)(2,1)} %broadcast_in_dim.109), calls=%async_computation.1 | async-start | bytes 1310720 | tf_op jit(solution)/shard_map/all_to_all | solution.py:80
  86.5 10.8 %collective-permute-start.11 = (bf16[4,512,256]{2,1,0:T(8,128)(2,1)S(1)}, bf16[4,512,256]{2,1,0:T(8,128)(2,1)S(1)}, u32[]{:S(2)}, u32[]{:S(2)}) collective-permute-start(bf16[4,512,256]{2,1,0:T(8,128)(2,1)S(1)} %bitcast.116), channel_id=1, source_target_pairs={{0,32},{1,33},{2,34},{3,35},{4,36},{5,37},{6,38},{7,39},{8,40},{9,... | collective-permute-start | bytes 3145736 | tf_op jit(solution)/shard_map/ppermute | solution.py:76
  97.3 5.4 %dynamic-slice-start = ((f32[8192]{0:T(1024)}, s32[]{:T(128)}), f32[4096]{0:T(1024)S(1)}, s32[]{:S(2)}) async-start(f32[8192]{0:T(1024)} %param.13, s32[]{:T(128)} %select_n.444), calls=%async_computation.5 | async-start | bytes 33280 | tf_op jit(solution)/shard_map/dynamic_slice | solution.py:195
  97.3 5.4 %copy-start = (bf16[8192,64]{0,1:T(8,128)(2,1)S(1)}, bf16[8192,64]{0,1:T(8,128)(2,1)}, u32[]{:S(2)}) copy-start(bf16[8192,64]{0,1:T(8,128)(2,1)} %param.14) | copy-start | bytes 3145732
  98.7 14.9 %all-to-all-start.2 = ((bf16[4,320,256]{2,1,0:T(8,128)(2,1)}), bf16[4,320,256]{2,1,0:T(8,128)(2,1)S(1)}, u32[]{:S(2)}, u32[]{:S(2)}) async-start(bf16[4,320,256]{2,1,0:T(8,128)(2,1)} %fusion.14), calls=%async_computation.2 | async-start | bytes 1310720 | tf_op jit(solution)/shard_map/all_to_all | solution.py:80
  103.4 14.5 %collective-permute-start.13 = (bf16[4,64,256]{2,0,1:T(4,128)(2,1)S(1)}, bf16[4,64,256]{2,0,1:T(4,128)(2,1)S(1)}, u32[]{:S(2)}, u32[]{:S(2)}) collective-permute-start(bf16[4,64,256]{2,0,1:T(4,128)(2,1)S(1)} %get-tuple-element.65), channel_id=1, source_target_pairs={{0,4},{1,5},{2,6},{3,7},{4,8},{5,9},{6,10},{7,11},{8,12},{9,13},{1... | collective-permute-start | bytes 393224 | tf_op jit(solution)/shard_map/ppermute | solution.py:76
  106.7 11.2 %collective-permute-start.15 = (bf16[4,64,256]{2,0,1:T(4,128)(2,1)S(1)}, bf16[4,64,256]{2,0,1:T(4,128)(2,1)S(1)}, u32[]{:S(2)}, u32[]{:S(2)}) collective-permute-start(bf16[4,64,256]{2,0,1:T(4,128)(2,1)S(1)} %get-tuple-element.66), channel_id=1, source_target_pairs={{0,12},{1,13},{2,14},{3,15},{4,0},{5,1},{6,2},{7,3},{8,4},{9,5},{1... | collective-permute-start | bytes 393224 | tf_op jit(solution)/shard_map/ppermute | solution.py:76
  109.9 8.2 %collective-permute-start.14 = (bf16[4,64,256]{2,0,1:T(4,128)(2,1)S(1)}, bf16[4,64,256]{2,0,1:T(4,128)(2,1)S(1)}, u32[]{:S(2)}, u32[]{:S(2)}) collective-permute-start(bf16[4,64,256]{2,0,1:T(4,128)(2,1)S(1)} %get-tuple-element.67), channel_id=1, source_target_pairs={{0,8},{1,9},{2,10},{3,11},{4,12},{5,13},{6,14},{7,15},{8,0},{9,1},... | collective-permute-start | bytes 393224 | tf_op jit(solution)/shard_map/ppermute | solution.py:76
  114.4 25.8 %all-to-all-start.3 = ((bf16[4,160,256]{2,1,0:T(8,128)(2,1)}), bf16[4,160,256]{2,1,0:T(8,128)(2,1)S(1)}, u32[]{:S(2)}, u32[]{:S(2)}) async-start(bf16[4,160,256]{2,1,0:T(8,128)(2,1)} %pad_maximum_fusion.4), calls=%async_computation.3 | async-start | bytes 655360 | tf_op jit(solution)/shard_map/all_to_all | solution.py:80
  120.4 8.7 %collective-permute-start.16 = (bf16[4,64,256]{2,1,0:T(8,128)(2,1)S(1)}, bf16[4,64,256]{2,1,0:T(8,128)(2,1)S(1)}, u32[]{:S(2)}, u32[]{:S(2)}) collective-permute-start(bf16[4,64,256]{2,1,0:T(8,128)(2,1)S(1)} %bitcast.129), channel_id=1, source_target_pairs={{0,1},{1,2},{2,3},{3,0},{4,5},{5,6},{6,7},{7,4},{8,9},{9,10},{10,1... | collective-permute-start | bytes 393224 | tf_op jit(solution)/shard_map/ppermute | solution.py:76
  122.6 7.7 %collective-permute-start.17 = (bf16[4,64,256]{2,1,0:T(8,128)(2,1)S(1)}, bf16[4,64,256]{2,1,0:T(8,128)(2,1)S(1)}, u32[]{:S(2)}, u32[]{:S(2)}) collective-permute-start(bf16[4,64,256]{2,1,0:T(8,128)(2,1)S(1)} %bitcast.128), channel_id=1, source_target_pairs={{0,2},{1,3},{2,0},{3,1},{4,6},{5,7},{6,4},{7,5},{8,10},{9,11},{10,... | collective-permute-start | bytes 393224 | tf_op jit(solution)/shard_map/ppermute | solution.py:76
  126.5 6.0 %collective-permute-start.18 = (bf16[4,64,256]{2,1,0:T(8,128)(2,1)S(1)}, bf16[4,64,256]{2,1,0:T(8,128)(2,1)S(1)}, u32[]{:S(2)}, u32[]{:S(2)}) collective-permute-start(bf16[4,64,256]{2,1,0:T(8,128)(2,1)S(1)} %bitcast.127), channel_id=1, source_target_pairs={{0,3},{1,0},{2,1},{3,2},{4,7},{5,4},{6,5},{7,6},{8,11},{9,8},{10,9... | collective-permute-start | bytes 393224 | tf_op jit(solution)/shard_map/ppermute | solution.py:76
  132.8 9.0 %collective-permute-start.19 = (bf16[16,64,256]{2,1,0:T(8,128)(2,1)S(1)}, bf16[16,64,256]{2,1,0:T(8,128)(2,1)S(1)}, u32[]{:S(2)}, u32[]{:S(2)}) collective-permute-start(bf16[16,64,256]{2,1,0:T(8,128)(2,1)S(1)} %bitcast.118), channel_id=1, source_target_pairs={{0,32},{1,33},{2,34},{3,35},{4,36},{5,37},{6,38},{7,39},{8,40},{9,... | collective-permute-start | bytes 1572872 | tf_op jit(solution)/shard_map/ppermute | solution.py:76
  143.6 15.0 %all-to-all-start.4 = ((bf16[16,160,128]{2,1,0:T(8,128)(2,1)}), bf16[16,160,128]{2,1,0:T(8,128)(2,1)S(1)}, u32[]{:S(2)}, u32[]{:S(2)}) async-start(bf16[16,160,128]{2,1,0:T(8,128)(2,1)} %copy.57), calls=%async_computation.4 | async-start | bytes 1310720 | tf_op jit(solution)/shard_map/all_to_all | solution.py:80
  148.1 15.8 %collective-permute-start.12 = (bf16[160,256]{1,0:T(8,128)(2,1)S(1)}, bf16[160,256]{1,0:T(8,128)(2,1)S(1)}, u32[]{:S(2)}, u32[]{:S(2)}) collective-permute-start(bf16[160,256]{1,0:T(8,128)(2,1)S(1)} %select_bitcast_fusion), channel_id=1, source_target_pairs={{0,32},{1,33},{2,34},{3,35},{4,36},{5,37},{6,38},{7,39},{8,40},{9,... | collective-permute-start | bytes 245768 | tf_op jit(solution)/shard_map/ppermute | solution.py:76
  159.6 5.3 %collective-permute-start.20 = (bf16[160,64]{1,0:T(8,128)(2,1)S(1)}, bf16[160,64]{1,0:T(8,128)(2,1)S(1)}, u32[]{:S(2)}, u32[]{:S(2)}) collective-permute-start(bf16[160,64]{1,0:T(8,128)(2,1)S(1)} %fusion.64), channel_id=1, source_target_pairs={{0,32},{1,33},{2,34},{3,35},{4,36},{5,37},{6,38},{7,39},{8,40},{9,... | collective-permute-start | bytes 61448 | tf_op jit(solution)/shard_map/ppermute | solution.py:76
